TPU v7x, 32 devices: a whole 2x2x4 slice. The times are simulated.
32 devices in a mesh: dp: 4 (over x, core), pix: 8 (over z, y).
Axes of the slice: x: 2, y: 2, z: 4, core: 2. Of those that a mesh axis runs over, the one named last changes fastest.
Arguments:
- image_sides: int32 [4, 2, 8], P('dp'), may hold values from 32 to 64, as said below
- pixels: bfloat16 [4, 2, 32768, 261], P('dp', None, 'pix'), may hold values from -6 to 6
- latent_array: bfloat16 [512, 1024], P('pix'), may hold values from -6 to 6
- pixel_gain: bfloat16 [261], replicated, may hold values from 0.099609375 to 1.8984375
- latent_gain: bfloat16 [1024], P('pix'), may hold values from 0.099609375 to 1.8984375
- query_weight: bfloat16 [1024, 1024], P('pix'), may hold values from -0.1875 to 0.1875
- key_weight: bfloat16 [261, 1024], P(None, 'pix'), may hold values from -0.375 to 0.375
- value_weight: bfloat16 [261, 1024], P(None, 'pix'), may hold values from -0.375 to 0.375
- cross_out_weight: bfloat16 [1024, 1024], P('pix'), may hold values from -6 to 6
- cross_mlp_gain: bfloat16 [1024], P('pix'), may hold values from 0.099609375 to 1.8984375
- cross_mlp_in: bfloat16 [1024, 1024], P('pix'), may hold values from -0.1875 to 0.1875
- cross_mlp_out: bfloat16 [1024, 1024], P('pix'), may hold values from -0.1875 to 0.1875
- self_gain: bfloat16 [1024], P('pix'), may hold values from 0.099609375 to 1.8984375
- self_qkv_weight: bfloat16 [1024, 3072], P('pix'), may hold values from -0.1875 to 0.1875
- self_out_weight: bfloat16 [1024, 1024], P('pix'), may hold values from -3 to 3
- self_mlp_gain: bfloat16 [1024], P('pix'), may hold values from 0.099609375 to 1.8984375
- self_mlp_in: bfloat16 [1024, 1024], P('pix'), may hold values from -0.1875 to 0.1875
- self_mlp_out: bfloat16 [1024, 1024], P('pix'), may hold values from -0.1875 to 0.1875
- cotangent: bfloat16 [4, 2, 8, 512, 1024], P('dp', None, None, 'pix'), may hold values from -6 to 6
Outputs:
- latent_out: bfloat16 [4, 2, 8, 512, 1024], P('dp', None, None, 'pix')
- pixel_grad: float32 [4, 2, 32768, 261], P('dp', None, 'pix')
- latent_grad: float32 [512, 1024], P('pix')
- pixel_gain_grad: float32 [261], replicated
- latent_gain_grad: float32 [1024], P('pix')
- query_grad: float32 [1024, 1024], P('pix')
- key_grad: float32 [261, 1024], P(None, 'pix')
- value_grad: float32 [261, 1024], P(None, 'pix')
- cross_out_grad: float32 [1024, 1024], P('pix')
- cross_mlp_gain_grad: float32 [1024], P('pix')
- cross_mlp_in_grad: float32 [1024, 1024], P('pix')
- cross_mlp_out_grad: float32 [1024, 1024], P('pix')
- self_gain_grad: float32 [1024], P('pix')
- self_qkv_grad: float32 [1024, 3072], P('pix')
- self_out_grad: float32 [1024, 1024], P('pix')
- self_mlp_gain_grad: float32 [1024], P('pix')
- self_mlp_in_grad: float32 [1024, 1024], P('pix')
- self_mlp_out_grad: float32 [1024, 1024], P('pix')
Inputs may be any that keep to these rules, and one draw needn't show every extreme that they name: `image_sides`: every side is 64 // 4 times 2, 3 or 4; each group (one index of dp, one micro-batch) holds at least one image of side 64 and one of side 64 // 2.
All inputs are finite; a program needn't handle non-finite values.
Results may differ from a plain program's by a relative error of at most 0.034.
Values may be sent and summed in bfloat16 or wider, within the bound.
A program may use at most 208 MiB of HBM per device.

v0:
```python
import jax
import jax.numpy as jnp
from jax import lax
from jax.sharding import PartitionSpec as P

HEADS = 8
SIDE = 64


highest = lax.Precision.HIGHEST
big_value = 1e30


def layer_norm(values, gain):
    average = jnp.mean(values, -1, keepdims=True)
    centered = values - average
    return centered * lax.rsqrt(jnp.mean(centered * centered, -1, keepdims=True) + 1e-05) * gain


def matmul(left, right):
    return jnp.dot(left, right, preferred_element_type=jnp.float32)


def left_matmul(left, right):
    return lax.dot_general(
        left, right, (((0,), (0,)), ((), ())), preferred_element_type=jnp.float32
    )


def right_matmul(left, right):
    return lax.dot_general(
        left, right, (((1,), (1,)), ((), ())), preferred_element_type=jnp.float32
    )


def norm_back(values, gain, grad):
    unused, pullback = jax.vjp(layer_norm, values, gain)
    return pullback(grad)


def mlp_forward(inputs, gain, w_in, w_out):
    normed = layer_norm(inputs, gain).astype(jnp.bfloat16)
    hidden = matmul(normed, w_in)
    active = jax.nn.gelu(hidden).astype(jnp.bfloat16)
    return (inputs + matmul(active, w_out), (normed, hidden, active))


def mlp_backward(grad, inputs, gain, w_in, w_out, kept):
    normed, hidden, active = kept
    grad_low = grad.astype(jnp.bfloat16)
    grad_out = left_matmul(active, grad_low)
    grad_active = right_matmul(grad_low, w_out)
    unused, pullback = jax.vjp(jax.nn.gelu, hidden)
    grad_hidden = pullback(grad_active)[0].astype(jnp.bfloat16)
    grad_in = left_matmul(normed, grad_hidden)
    grad_normed = right_matmul(grad_hidden, w_in)
    grad_inputs, grad_gain = norm_back(inputs, gain, grad_normed)
    return (grad + grad_inputs, grad_gain, grad_in, grad_out)


def body(
    image_sides,
    pixels,
    latent_array,
    pixel_gain,
    latent_gain,
    query_weight,
    key_weight,
    value_weight,
    cross_out_weight,
    cross_mlp_gain,
    cross_mlp_in,
    cross_mlp_out,
    self_gain,
    self_qkv_weight,
    self_out_weight,
    self_mlp_gain,
    self_mlp_in,
    self_mlp_out,
    cotangent,
):
    pieces = lax.axis_size("pix")
    position = lax.axis_index("pix")
    micros = image_sides.shape[1]
    images = image_sides.shape[2]
    capacity = pixels.shape[2]
    row_count = latent_array.shape[0]
    model_width = latent_array.shape[1]
    head_size = model_width // HEADS
    unit_count = images * HEADS // pieces
    window = min(images, (capacity - 2) // (SIDE * SIDE // 4) + 2)
    cross_scale = model_width ** (-0.5)
    self_scale = head_size ** (-0.5)
    shards = (
        latent_array,
        latent_gain,
        query_weight,
        key_weight,
        value_weight,
        cross_out_weight,
        cross_mlp_gain,
        cross_mlp_in,
        cross_mlp_out,
        self_gain,
        self_qkv_weight,
        self_out_weight,
        self_mlp_gain,
        self_mlp_in,
        self_mlp_out,
    )
    lat_rows = latent_array.astype(jnp.float32)
    gain_pix = pixel_gain.astype(jnp.float32)
    grad_rows = jnp.zeros((row_count, model_width), jnp.float32)
    grad_pix_gain = jnp.zeros(gain_pix.shape, jnp.float32)
    outputs = []
    pixel_grads = []
    totals = None
    for step_index in range(micros):
        gathered = (
            lax.all_gather(shards[0], "pix", axis=0, tiled=True),
            lax.all_gather(shards[1], "pix", axis=0, tiled=True),
            lax.all_gather(shards[2], "pix", axis=0, tiled=True),
            lax.all_gather(shards[3], "pix", axis=1, tiled=True),
            lax.all_gather(shards[4], "pix", axis=1, tiled=True),
            lax.all_gather(shards[5], "pix", axis=0, tiled=True),
            lax.all_gather(shards[6], "pix", axis=0, tiled=True),
            lax.all_gather(shards[7], "pix", axis=0, tiled=True),
            lax.all_gather(shards[8], "pix", axis=0, tiled=True),
            lax.all_gather(shards[9], "pix", axis=0, tiled=True),
            lax.all_gather(shards[10], "pix", axis=0, tiled=True),
            lax.all_gather(shards[11], "pix", axis=0, tiled=True),
            lax.all_gather(shards[12], "pix", axis=0, tiled=True),
            lax.all_gather(shards[13], "pix", axis=0, tiled=True),
            lax.all_gather(shards[14], "pix", axis=0, tiled=True),
        )
        lat_full, g_lat, wq, wk, wv, wo, g_cross, w1c, w2c, g_self, wqkv, wos, g_mlp, w1s, w2s = (
            gathered
        )
        g_lat_f = g_lat.astype(jnp.float32)
        gc_f = g_cross.astype(jnp.float32)
        gs_f = g_self.astype(jnp.float32)
        gm_f = g_mlp.astype(jnp.float32)
        if step_index == 0:
            normed_lat = layer_norm(lat_full.astype(jnp.float32), g_lat_f).astype(jnp.bfloat16)
            queries = matmul(normed_lat, wq).astype(jnp.bfloat16)
        side_list = image_sides[0, step_index]
        lengths = side_list * side_list
        ends = jnp.cumsum(lengths)
        slot_ids = position * capacity + jnp.arange(capacity, dtype=jnp.int32)
        segment = jnp.sum((slot_ids[:, None] >= ends[None, :]).astype(jnp.int32), 1)
        window_ids = segment[0] + jnp.arange(window, dtype=jnp.int32)
        select = (window_ids[:, None] == jnp.arange(images, dtype=jnp.int32)[None, :]).astype(
            jnp.float32
        )
        in_window = segment[None, :] == window_ids[:, None]
        raw_pixels = pixels[0, step_index].astype(jnp.float32)
        normed_pix = layer_norm(raw_pixels, gain_pix).astype(jnp.bfloat16)
        pixel_keys = matmul(normed_pix, wk).astype(jnp.bfloat16)
        pixel_values = matmul(normed_pix, wv).astype(jnp.bfloat16)
        scores = right_matmul(queries, pixel_keys) * cross_scale
        local_top = jnp.max(jnp.where(in_window[:, None, :], scores[None], -big_value), 2)
        image_top = jnp.max(jnp.where(select[:, :, None] > 0, local_top[:, None, :], -big_value), 0)
        image_top = lax.pmax(image_top, "pix")
        window_top = jnp.einsum("wb,br->wr", select, image_top, precision=highest)
        weights = jnp.where(
            in_window[:, None, :], jnp.exp(scores[None] - window_top[:, :, None]), 0.0
        )
        partial_den = jnp.sum(weights, 2)
        partial_num = jnp.einsum(
            "wrc,cd->wrd",
            weights.astype(jnp.bfloat16),
            pixel_values,
            preferred_element_type=jnp.float32,
        )
        full_num = jnp.einsum("wb,wrd->brd", select, partial_num, precision=highest)
        full_den = jnp.einsum("wb,wr->br", select, partial_den, precision=highest)
        num_rows, den_rows = (
            lax.psum_scatter(
                full_num.astype(jnp.bfloat16), "pix", scatter_dimension=1, tiled=True
            ).astype(jnp.float32),
            lax.psum_scatter(
                full_den.astype(jnp.bfloat16), "pix", scatter_dimension=1, tiled=True
            ).astype(jnp.float32),
        )
        attended = num_rows / den_rows[:, :, None]
        attended_low = attended.astype(jnp.bfloat16).reshape(images * row_count, model_width)
        start_rows = jnp.broadcast_to(lat_rows[None], (images, row_count, model_width)).reshape(
            images * row_count, model_width
        )
        after_cross = start_rows + matmul(attended_low, wo)
        after_mlp, cross_kept = mlp_forward(after_cross, gc_f, w1c, w2c)
        normed_self = layer_norm(after_mlp, gs_f).astype(jnp.bfloat16)
        packed = matmul(normed_self, wqkv).astype(jnp.bfloat16)
        packed = packed.reshape(images, row_count, HEADS, 3 * head_size).transpose(0, 2, 1, 3)
        packed = packed.reshape(pieces, unit_count, row_count, 3 * head_size)
        packed = lax.all_to_all(packed, "pix", split_axis=0, concat_axis=2, tiled=True)[0]
        head_query = packed[:, :, :head_size]
        head_key = packed[:, :, head_size : 2 * head_size]
        head_value = packed[:, :, 2 * head_size :]
        self_scores = (
            jnp.einsum("uqd,ukd->uqk", head_query, head_key, preferred_element_type=jnp.float32)
            * self_scale
        )
        self_top = jnp.max(self_scores, 2, keepdims=True)
        self_weights = jnp.exp(self_scores - self_top)
        self_den = jnp.sum(self_weights, 2, keepdims=True)
        self_num = jnp.einsum(
            "uqk,ukd->uqd",
            self_weights.astype(jnp.bfloat16),
            head_value,
            preferred_element_type=jnp.float32,
        )
        self_out = self_num / self_den
        returned = lax.all_to_all(
            self_out.astype(jnp.bfloat16), "pix", split_axis=1, concat_axis=0, tiled=True
        )
        returned = (
            returned.reshape(images, HEADS, row_count, head_size)
            .transpose(0, 2, 1, 3)
            .reshape(images * row_count, model_width)
        )
        after_self = after_mlp + matmul(returned, wos)
        final, final_kept = mlp_forward(after_self, gm_f, w1s, w2s)
        outputs.append(final.astype(jnp.bfloat16).reshape(images, row_count, model_width))
        grad = cotangent[0, step_index].astype(jnp.float32).reshape(images * row_count, model_width)
        grad, d_gm, d_w1s, d_w2s = mlp_backward(grad, after_self, gm_f, w1s, w2s, final_kept)
        grad_low = grad.astype(jnp.bfloat16)
        d_wos = left_matmul(returned, grad_low)
        grad_self = right_matmul(grad_low, wos)
        grad_self = grad_self.reshape(images, row_count, HEADS, head_size).transpose(0, 2, 1, 3)
        grad_self = grad_self.reshape(pieces, unit_count, row_count, head_size)
        grad_self = lax.all_to_all(
            grad_self.astype(jnp.bfloat16), "pix", split_axis=0, concat_axis=2, tiled=True
        ).astype(grad_self.dtype)[0]
        grad_num = (grad_self / self_den).astype(jnp.bfloat16)
        grad_den = -jnp.sum(grad_self * self_out, 2, keepdims=True) / self_den
        again_scores = (
            jnp.einsum("uqd,ukd->uqk", head_query, head_key, preferred_element_type=jnp.float32)
            * self_scale
        )
        again_weights = jnp.exp(again_scores - self_top)
        grad_weights = (
            jnp.einsum("uqd,ukd->uqk", grad_num, head_value, preferred_element_type=jnp.float32)
            + grad_den
        )
        grad_scores = (again_weights * grad_weights).astype(jnp.bfloat16)
        grad_query = (
            jnp.einsum("uqk,ukd->uqd", grad_scores, head_key, preferred_element_type=jnp.float32)
            * self_scale
        )
        grad_key = (
            jnp.einsum("uqk,uqd->ukd", grad_scores, head_query, preferred_element_type=jnp.float32)
            * self_scale
        )
        grad_value = jnp.einsum(
            "uqk,uqd->ukd",
            again_weights.astype(jnp.bfloat16),
            grad_num,
            preferred_element_type=jnp.float32,
        )
        grad_packed = jnp.concatenate([grad_query, grad_key, grad_value], 2).astype(jnp.bfloat16)
        grad_packed = lax.all_to_all(grad_packed, "pix", split_axis=1, concat_axis=0, tiled=True)
        grad_packed = (
            grad_packed.reshape(images, HEADS, row_count, 3 * head_size)
            .transpose(0, 2, 1, 3)
            .reshape(images * row_count, 3 * model_width)
        )
        d_wqkv = left_matmul(normed_self, grad_packed)
        grad_normed = right_matmul(grad_packed, wqkv)
        grad_inputs, d_gs = norm_back(after_mlp, gs_f, grad_normed)
        grad = grad + grad_inputs
        grad, d_gc, d_w1c, d_w2c = mlp_backward(grad, after_cross, gc_f, w1c, w2c, cross_kept)
        grad_rows = grad_rows + jnp.sum(grad.reshape(images, row_count, model_width), 0)
        grad_low = grad.astype(jnp.bfloat16)
        d_wo = left_matmul(attended_low, grad_low)
        grad_cross = right_matmul(grad_low, wo).reshape(images, row_count, model_width)
        cross_gnum = (grad_cross / den_rows[:, :, None]).astype(jnp.bfloat16)
        cross_gden = (-jnp.sum(grad_cross * attended, 2) / den_rows).astype(jnp.bfloat16)
        all_num, all_den = (
            lax.all_gather(cross_gnum, "pix", axis=1, tiled=True),
            lax.all_gather(cross_gden, "pix", axis=1, tiled=True),
        )
        select_low = select.astype(jnp.bfloat16)
        window_num = jnp.einsum(
            "wb,brd->wrd", select_low, all_num, preferred_element_type=jnp.float32
        ).astype(jnp.bfloat16)
        window_den = jnp.einsum(
            "wb,br->wr", select_low, all_den, preferred_element_type=jnp.float32
        )
        scores = right_matmul(queries, pixel_keys) * cross_scale
        weights = jnp.where(
            in_window[:, None, :], jnp.exp(scores[None] - window_top[:, :, None]), 0.0
        )
        cross_gweights = (
            jnp.einsum("wrd,cd->wrc", window_num, pixel_values, preferred_element_type=jnp.float32)
            + window_den[:, :, None]
        )
        cross_gscores = jnp.sum(weights * cross_gweights, 0).astype(jnp.bfloat16)
        query_terms = matmul(cross_gscores, pixel_keys) * cross_scale
        grad_keys = (left_matmul(cross_gscores, queries) * cross_scale).astype(jnp.bfloat16)
        grad_values = jnp.einsum(
            "wrc,wrd->cd",
            weights.astype(jnp.bfloat16),
            window_num,
            preferred_element_type=jnp.float32,
        ).astype(jnp.bfloat16)
        d_wk = left_matmul(normed_pix, grad_keys)
        d_wv = left_matmul(normed_pix, grad_values)
        grad_normed_pix = right_matmul(grad_keys, wk) + right_matmul(grad_values, wv)
        grad_pixels, d_gpix = norm_back(raw_pixels, gain_pix, grad_normed_pix)
        pixel_grads.append(grad_pixels)
        grad_pix_gain = grad_pix_gain + d_gpix
        terms = (
            d_wk,
            d_wv,
            d_wo,
            d_gc,
            d_w1c,
            d_w2c,
            d_gs,
            d_wqkv,
            d_wos,
            d_gm,
            d_w1s,
            d_w2s,
            query_terms,
        )
        reduced = (
            lax.psum_scatter(
                terms[0].astype(jnp.bfloat16), "pix", scatter_dimension=1, tiled=True
            ).astype(jnp.float32),
            lax.psum_scatter(
                terms[1].astype(jnp.bfloat16), "pix", scatter_dimension=1, tiled=True
            ).astype(jnp.float32),
            lax.psum_scatter(
                terms[2].astype(jnp.bfloat16), "pix", scatter_dimension=0, tiled=True
            ).astype(jnp.float32),
            lax.psum_scatter(
                terms[3].astype(jnp.bfloat16), "pix", scatter_dimension=0, tiled=True
            ).astype(jnp.float32),
            lax.psum_scatter(
                terms[4].astype(jnp.bfloat16), "pix", scatter_dimension=0, tiled=True
            ).astype(jnp.float32),
            lax.psum_scatter(
                terms[5].astype(jnp.bfloat16), "pix", scatter_dimension=0, tiled=True
            ).astype(jnp.float32),
            lax.psum_scatter(
                terms[6].astype(jnp.bfloat16), "pix", scatter_dimension=0, tiled=True
            ).astype(jnp.float32),
            lax.psum_scatter(
                terms[7].astype(jnp.bfloat16), "pix", scatter_dimension=0, tiled=True
            ).astype(jnp.float32),
            lax.psum_scatter(
                terms[8].astype(jnp.bfloat16), "pix", scatter_dimension=0, tiled=True
            ).astype(jnp.float32),
            lax.psum_scatter(
                terms[9].astype(jnp.bfloat16), "pix", scatter_dimension=0, tiled=True
            ).astype(jnp.float32),
            lax.psum_scatter(
                terms[10].astype(jnp.bfloat16), "pix", scatter_dimension=0, tiled=True
            ).astype(jnp.float32),
            lax.psum_scatter(
                terms[11].astype(jnp.bfloat16), "pix", scatter_dimension=0, tiled=True
            ).astype(jnp.float32),
            lax.psum_scatter(
                terms[12].astype(jnp.bfloat16), "pix", scatter_dimension=0, tiled=True
            ).astype(jnp.float32),
        )
        totals = reduced if totals is None else jax.tree.map(jnp.add, totals, reduced)
    s_wk, s_wv, s_wo, s_gc, s_w1c, s_w2c, s_gs, s_wqkv, s_wos, s_gm, s_w1s, s_w2s, s_query = totals
    summed = (
        lax.psum(s_wk.astype(jnp.bfloat16), "dp").astype(jnp.float32),
        lax.psum(s_wv.astype(jnp.bfloat16), "dp").astype(jnp.float32),
        lax.psum(s_wo.astype(jnp.bfloat16), "dp").astype(jnp.float32),
        lax.psum(s_gc.astype(jnp.bfloat16), "dp").astype(jnp.float32),
        lax.psum(s_w1c.astype(jnp.bfloat16), "dp").astype(jnp.float32),
        lax.psum(s_w2c.astype(jnp.bfloat16), "dp").astype(jnp.float32),
        lax.psum(s_gs.astype(jnp.bfloat16), "dp").astype(jnp.float32),
        lax.psum(s_wqkv.astype(jnp.bfloat16), "dp").astype(jnp.float32),
        lax.psum(s_wos.astype(jnp.bfloat16), "dp").astype(jnp.float32),
        lax.psum(s_gm.astype(jnp.bfloat16), "dp").astype(jnp.float32),
        lax.psum(s_w1s.astype(jnp.bfloat16), "dp").astype(jnp.float32),
        lax.psum(s_w2s.astype(jnp.bfloat16), "dp").astype(jnp.float32),
        lax.psum(s_query.astype(jnp.bfloat16), "dp").astype(jnp.float32),
        lax.psum(grad_rows.astype(jnp.bfloat16), "dp").astype(jnp.float32),
    )
    (
        f_wk,
        f_wv,
        f_wo,
        f_gc,
        f_w1c,
        f_w2c,
        f_gs,
        f_wqkv,
        f_wos,
        f_gm,
        f_w1s,
        f_w2s,
        query_rows,
        rows_total,
    ) = summed
    query_low = query_rows.astype(jnp.bfloat16)
    normed_rows = lax.dynamic_slice_in_dim(normed_lat, position * row_count, row_count, 0)
    d_wq_part = left_matmul(normed_rows, query_low)
    grad_normed_rows = right_matmul(query_low, wq)
    grad_lat_norm, d_glat_part = norm_back(lat_rows, g_lat_f, grad_normed_rows)
    d_wq, d_glat = (
        lax.psum_scatter(
            d_wq_part.astype(jnp.bfloat16), "pix", scatter_dimension=0, tiled=True
        ).astype(jnp.float32),
        lax.psum_scatter(
            d_glat_part.astype(jnp.bfloat16), "pix", scatter_dimension=0, tiled=True
        ).astype(jnp.float32),
    )
    d_gpix = lax.psum(grad_pix_gain, ("dp", "pix"))
    latent_out = jnp.stack(outputs)[None]
    pixel_out = jnp.stack(pixel_grads)[None]
    return (
        latent_out,
        pixel_out,
        rows_total + grad_lat_norm,
        d_gpix,
        d_glat,
        d_wq,
        f_wk,
        f_wv,
        f_wo,
        f_gc,
        f_w1c,
        f_w2c,
        f_gs,
        f_wqkv,
        f_wos,
        f_gm,
        f_w1s,
        f_w2s,
    )


def solution(mesh):
    return jax.shard_map(
        body,
        mesh=mesh,
        in_specs=(
            P("dp", None, None),
            P("dp", None, "pix", None),
            P("pix", None),
            P(),
            P("pix"),
            P("pix", None),
            P(None, "pix"),
            P(None, "pix"),
            P("pix", None),
            P("pix"),
            P("pix", None),
            P("pix", None),
            P("pix"),
            P("pix", None),
            P("pix", None),
            P("pix"),
            P("pix", None),
            P("pix", None),
            P("dp", None, None, "pix", None),
        ),
        out_specs=(
            P("dp", None, None, "pix", None),
            P("dp", None, "pix", None),
            P("pix", None),
            P(),
            P("pix"),
            P("pix", None),
            P(None, "pix"),
            P(None, "pix"),
            P("pix", None),
            P("pix"),
            P("pix", None),
            P("pix", None),
            P("pix"),
            P("pix", None),
            P("pix", None),
            P("pix"),
            P("pix", None),
            P("pix", None),
        ),
        check_vma=False,
    )
```

profile of v0, /device:TPU:0, one launch (start us, length us, event | category | flops | bytes accessed | tf_op | source)
XLA Modules:
  0.0 3260.1 jit_solution(12284732090400327805)
XLA Ops:
  10.5 22.3 all-gather
  35.5 29.7 all_gather.75
  92.1 29.8 all_gather.74
  174.7 44.7 %all-reduce.7 = (f32[8,512]{1,0:T(8,128)S(1)}, f32[8,512]{1,0:T(8,128)S(1)}) all-reduce(f32[8,512]{1,0:T(8,128)S(1)} %select_reduce_fusion.3, f32[8,512]{1,0:T(8,128)S(1)} %select_reduce_fusion.2), channel_id=1, replica_groups=mesh['dp'=4,'pix'=8] {'pix'}, use_global_device_ids=true, to_apply=%region_8.9 | all-reduce | flops 8192 | bytes 65536 | tf_op jit(solution)/shard_map/pmax | solution.py:163
  239.9 29.3 fusion.10
  270.5 21.0 fusion.43
  298.7 29.7 fusion.6
  328.4 21.1 fusion.40
  352.4 16.2 all-gather.1
  368.5 18.5 all-gather.2
  389.3 123.9 %reduce-scatter.40.cloned.1.call-done = bf16[8,64,1024]{2,0,1:T(8,128)(2,1)} async-done(((bf16[8,512,1024]{2,0,1:T(8,128)(2,1)}), bf16[8,64,1024]{2,0,1:T(8,128)(2,1)}) %reduce-scatter.40.cloned.1.call-update) | async-done | bytes 1048592 | tf_op jit(solution)/shard_map/reduce_scatter | solution.py:178
  516.3 148.9 %reduce-scatter.38.cloned.1.call-done = bf16[8,64,1024]{2,0,1:T(8,128)(2,1)} async-done(((bf16[8,512,1024]{2,0,1:T(8,128)(2,1)}), bf16[8,64,1024]{2,0,1:T(8,128)(2,1)}) %reduce-scatter.38.cloned.1.call-update) | async-done | bytes 1048592 | tf_op jit(solution)/shard_map/reduce_scatter | solution.py:178
  667.4 48.3 %all-gather.22.cloned.1.call-done = bf16[1024,1024]{1,0:T(8,128)(2,1)} async-done(((bf16[128,1024]{1,0:T(8,128)(2,1)}), bf16[1024,1024]{1,0:T(8,128)(2,1)}) %all-gather.22.cloned.1.call-update) | async-done | bytes 2097168 | tf_op jit(solution)/shard_map/all_gather | solution.py:125
  724.0 41.5 %all-gather.24.cloned.1.call-done = bf16[1024,1024]{1,0:T(8,128)(2,1)} async-done(((bf16[128,1024]{1,0:T(8,128)(2,1)}), bf16[1024,1024]{1,0:T(8,128)(2,1)}) %all-gather.24.cloned.1.call-update) | async-done | bytes 2097168 | tf_op jit(solution)/shard_map/all_gather | solution.py:127
  769.7 45.8 %all-gather.26.cloned.1.call-done = bf16[1024,1024]{1,0:T(8,128)(2,1)} async-done(((bf16[128,1024]{1,0:T(8,128)(2,1)}), bf16[1024,1024]{1,0:T(8,128)(2,1)}) %all-gather.26.cloned.1.call-update) | async-done | bytes 2097168 | tf_op jit(solution)/shard_map/all_gather | solution.py:128
  821.0 94.1 %all-gather.28.cloned.1.call-done = bf16[1024,3072]{1,0:T(8,128)(2,1)} async-done(((bf16[128,3072]{1,0:T(8,128)(2,1)}), bf16[1024,3072]{1,0:T(8,128)(2,1)}) %all-gather.28.cloned.1.call-update) | async-done | bytes 6291472 | tf_op jit(solution)/shard_map/all_gather | solution.py:130
  942.5 83.1 %all-to-all-done.2 = bf16[8,8,64,384]{3,1,2,0:T(8,128)(2,1)} async-done(((bf16[8,8,64,384]{3,1,2,0:T(8,128)(2,1)}), bf16[8,8,64,384]{3,1,2,0:T(8,128)(2,1)}, u32[]{:S(2)}, u32[]{:S(2)}) %all-to-all-start.2) | async-done | bytes 3145760 | tf_op jit(solution)/shard_map/all_to_all | solution.py:196
  1043.5 81.9 %all-to-all-done = bf16[8,8,64,384]{3,1,2,0:T(8,128)(2,1)S(1)} async-done(((bf16[8,8,64,384]{3,1,2,0:T(8,128)(2,1)}), bf16[8,8,64,384]{3,1,2,0:T(8,128)(2,1)S(1)}, u32[]{:S(2)}, u32[]{:S(2)}) %all-to-all-start) | async-done | bytes 3145760 | tf_op jit(solution)/shard_map/all_to_all | solution.py:196
  1129.8 38.1 %all-gather.3 = bf16[8,1,128]{2,1,0:T(2,128)(2,1)S(1)} all-gather(bf16[1,1,128]{2,1,0:T(2,128)(2,1)S(1)} %bitcast.460), channel_id=1, replica_groups=mesh['dp'=4,'pix'=8] {'pix'}, dimensions={0}, use_global_device_ids=true | all-gather | bytes 2304 | tf_op jit(solution)/shard_map/all_gather | solution.py:132
  1207.1 13.0 all-to-all-start.1
  1224.5 32.1 all-to-all-done.1
  1298.7 27.6 all-to-all-done.6
  1396.9 59.9 %all-to-all-done.7 = bf16[8,512,384]{2,0,1:T(8,128)(2,1)} async-done(((bf16[8,512,384]{2,0,1:T(8,128)(2,1)}), bf16[8,512,384]{2,0,1:T(8,128)(2,1)}, u32[]{:S(2)}, u32[]{:S(2)}) %all-to-all-start.7) | async-done | bytes 3145760 | tf_op jit(solution)/shard_map/all_to_all | solution.py:262
  1475.1 64.2 %all-to-all-done.5 = bf16[8,512,384]{2,0,1:T(8,128)(2,1)} async-done(((bf16[8,512,384]{2,0,1:T(8,128)(2,1)}), bf16[8,512,384]{2,0,1:T(8,128)(2,1)}, u32[]{:S(2)}, u32[]{:S(2)}) %all-to-all-start.5) | async-done | bytes 3145760 | tf_op jit(solution)/shard_map/all_to_all | solution.py:262
  1646.4 23.0 reduce-scatter.74.cloned.1.call-done
  1669.4 70.3 %reduce-scatter.72.cloned.1.call-done = bf16[128,1024]{1,0:T(8,128)(2,1)} async-done(((bf16[1024,1024]{1,0:T(8,128)(2,1)}), bf16[128,1024]{1,0:T(8,128)(2,1)}) %reduce-scatter.72.cloned.1.call-update) | async-done | bytes 262160 | tf_op jit(solution)/shard_map/reduce_scatter | solution.py:362
  1748.8 26.1 all-gather.4
  1775.0 26.0 all-gather.5
  1810.0 70.5 %reduce-scatter.56.cloned.1.call-done = bf16[128,1024]{1,0:T(8,128)(2,1)} async-done(((bf16[1024,1024]{1,0:T(8,128)(2,1)}), bf16[128,1024]{1,0:T(8,128)(2,1)}) %reduce-scatter.56.cloned.1.call-update) | async-done | bytes 262160 | tf_op jit(solution)/shard_map/reduce_scatter | solution.py:344
  1882.3 68.7 %reduce-scatter.52.cloned.1.call-done = bf16[128,1024]{1,0:T(8,128)(2,1)} async-done(((bf16[1024,1024]{1,0:T(8,128)(2,1)}), bf16[128,1024]{1,0:T(8,128)(2,1)}) %reduce-scatter.52.cloned.1.call-update) | async-done | bytes 262160 | tf_op jit(solution)/shard_map/reduce_scatter | solution.py:341
  1951.0 70.5 %reduce-scatter.54.cloned.1.call-done = bf16[128,1024]{1,0:T(8,128)(2,1)} async-done(((bf16[1024,1024]{1,0:T(8,128)(2,1)}), bf16[128,1024]{1,0:T(8,128)(2,1)}) %reduce-scatter.54.cloned.1.call-update) | async-done | bytes 262160 | tf_op jit(solution)/shard_map/reduce_scatter | solution.py:341
  2023.2 68.3 %reduce-scatter.48.cloned.1.call-done = bf16[128,1024]{1,0:T(8,128)(2,1)} async-done(((bf16[1024,1024]{1,0:T(8,128)(2,1)}), bf16[128,1024]{1,0:T(8,128)(2,1)}) %reduce-scatter.48.cloned.1.call-update) | async-done | bytes 262160 | tf_op jit(solution)/shard_map/reduce_scatter | solution.py:335
  2091.5 70.4 %reduce-scatter.50.cloned.1.call-done = bf16[128,1024]{1,0:T(8,128)(2,1)} async-done(((bf16[1024,1024]{1,0:T(8,128)(2,1)}), bf16[128,1024]{1,0:T(8,128)(2,1)}) %reduce-scatter.50.cloned.1.call-update) | async-done | bytes 262160 | tf_op jit(solution)/shard_map/reduce_scatter | solution.py:335
  2163.7 118.6 %reduce-scatter.62.cloned.1.call-done = bf16[128,3072]{1,0:T(8,128)(2,1)} async-done(((bf16[1024,3072]{1,0:T(8,128)(2,1)}), bf16[128,3072]{1,0:T(8,128)(2,1)}) %reduce-scatter.62.cloned.1.call-update) | async-done | bytes 786448 | tf_op jit(solution)/shard_map/reduce_scatter | solution.py:350
  2282.3 120.6 %reduce-scatter.60.cloned.1.call-done = bf16[128,3072]{1,0:T(8,128)(2,1)} async-done(((bf16[1024,3072]{1,0:T(8,128)(2,1)}), bf16[128,3072]{1,0:T(8,128)(2,1)}) %reduce-scatter.60.cloned.1.call-update) | async-done | bytes 786448 | tf_op jit(solution)/shard_map/reduce_scatter | solution.py:350
  2405.3 123.8 %all-gather.38.cloned.1.call-done = bf16[8,512,1024]{2,0,1:T(8,128)(2,1)} async-done(((bf16[8,64,1024]{2,0,1:T(8,128)(2,1)}), bf16[8,512,1024]{2,0,1:T(8,128)(2,1)}) %all-gather.38.cloned.1.call-update) | async-done | bytes 8388624 | tf_op jit(solution)/shard_map/all_gather | solution.py:280
  2538.4 36.2 %bitcast_convert_fusion = bf16[4096,1024]{1,0:T(8,128)(2,1)} fusion(f32[5,512]{1,0:T(8,128)S(1)} %copy-done.176, f32[512,4096]{1,0:T(8,128)} %copy-done.46, pred[5,4096]{1,0:T(8,128)(4,1)S(1)} %copy-done.113, bf16[5,512,1024]{2,0,1:T(8,128)(2,1)} %fusion.184), kind=kOutput, calls=%fused_computation.30 | convolution fusion | flops 21510488064 | bytes 22050816 | tf_op jit(solution)/shard_map/wrc,wrd->cd/dot_general | solution.py:301
  2581.8 38.3 %multiply_reduce_fusion = bf16[512,4096]{1,0:T(8,128)(2,1)} fusion(f32[5,512]{1,0:T(8,128)S(1)} %fusion.182, f32[5,512]{1,0:T(8,128)S(1)} %copy-done.176, f32[512,4096]{1,0:T(8,128)} %copy-done.46, pred[5,4096]{1,0:T(8,128)(4,1)S(1)} %copy-done.113, bf16[4096,1024]{1,0:T(8,128)(2,1)} %convolution_convert_fusion, bf16[5,512,1024]{2,0,1:T(8,128)(2,1)} %fusion.184), kind=kOutput, calls=%fused_computation | convolution fusion | flops 21525168128 | bytes 26255360 | tf_op jit(solution)/shard_map/wrd,cd->wrc/dot_general | solution.py:295
  2620.2 34.2 %all-gather.36.cloned.1.call-done = bf16[8,512,1024]{2,0,1:T(8,128)(2,1)} async-done(((bf16[8,64,1024]{2,0,1:T(8,128)(2,1)}), bf16[8,512,1024]{2,0,1:T(8,128)(2,1)}) %all-gather.36.cloned.1.call-update) | async-done | bytes 8388624 | tf_op jit(solution)/shard_map/all_gather | solution.py:280
  2663.4 38.3 %multiply_reduce_fusion.1 = bf16[512,4096]{1,0:T(8,128)(2,1)} fusion(f32[5,512]{1,0:T(8,128)S(1)} %fusion.180, f32[5,512]{1,0:T(8,128)S(1)} %copy-done.174, f32[512,4096]{1,0:T(8,128)} %copy-done.44, pred[5,4096]{1,0:T(8,128)(4,1)S(1)} %copy-done.111, bf16[4096,1024]{1,0:T(8,128)(2,1)} %convolution_convert_fusion.2, bf16[5,512,1024]{2,0,1:T(8,128)(2,1)} %fusion.186), kind=kOutput, calls=%fused_computation.1 | convolution fusion | flops 21525168128 | bytes 26255360 | tf_op jit(solution)/shard_map/wrd,cd->wrc/dot_general | solution.py:295
  2701.7 34.1 %bitcast_convert_fusion.1 = bf16[4096,1024]{1,0:T(8,128)(2,1)S(1)} fusion(f32[5,512]{1,0:T(8,128)S(1)} %copy-done.174, f32[512,4096]{1,0:T(8,128)} %copy-done.44, pred[5,4096]{1,0:T(8,128)(4,1)S(1)} %copy-done.111, bf16[5,512,1024]{2,0,1:T(8,128)(2,1)} %fusion.186), kind=kOutput, calls=%fused_computation.31 | convolution fusion | flops 21510488064 | bytes 22050816 | tf_op jit(solution)/shard_map/wrc,wrd->cd/dot_general | solution.py:301
  2818.6 50.0 %reduce-scatter.82.cloned.1.call-done = bf16[128,261]{1,0:T(8,128)(2,1)} async-done(((bf16[1024,261]{1,0:T(8,128)(2,1)}), bf16[128,261]{1,0:T(8,128)(2,1)}) %reduce-scatter.82.cloned.1.call-update) | async-done | bytes 66832
  2869.6 64.0 %reduce-scatter.80.cloned.1.call-done = bf16[128,261]{1,0:T(8,128)(2,1)} async-done(((bf16[1024,261]{1,0:T(8,128)(2,1)}), bf16[128,261]{1,0:T(8,128)(2,1)}) %reduce-scatter.80.cloned.1.call-update) | async-done | bytes 66832
  2935.9 63.6 %reduce-scatter.42.cloned.1.call-done = bf16[64,1024]{1,0:T(8,128)(2,1)} async-done(((bf16[512,1024]{1,0:T(8,128)(2,1)}), bf16[64,1024]{1,0:T(8,128)(2,1)}) %reduce-scatter.42.cloned.1.call-update) | async-done | bytes 131088 | tf_op jit(solution)/shard_map/reduce_scatter | solution.py:365
  2999.4 66.2 %reduce-scatter.44.cloned.1.call-done = bf16[64,1024]{1,0:T(8,128)(2,1)} async-done(((bf16[512,1024]{1,0:T(8,128)(2,1)}), bf16[64,1024]{1,0:T(8,128)(2,1)}) %reduce-scatter.44.cloned.1.call-update) | async-done | bytes 131088 | tf_op jit(solution)/shard_map/reduce_scatter | solution.py:365
  3080.6 53.2 %all-reduce.13.cloned.1.call-done = (bf16[64,1024]{1,0:T(8,128)(2,1)}, bf16[64,1024]{1,0:T(8,128)(2,1)}, bf16[261,128]{1,0:T(8,128)(2,1)}, bf16[261,128]{1,0:T(8...) async-done(((bf16[64,1024]{1,0:T(8,128)(2,1)}, ...) | async-done | bytes 2755088 | tf_op jit(solution)/shard_map/psum | solution.py:385
  3155.2 39.5 %psum.107 = f32[261]{0:T(512)} all-reduce(f32[261]{0:T(512)S(1)} %add.454), channel_id=1, replica_groups=mesh['dp'=4,'pix'=8] {'dp','pix'}, use_global_device_ids=true, to_apply=%region_72.73 | all-reduce | flops 261 | bytes 2088 | tf_op jit(solution)/shard_map/psum | solution.py:416
  3197.3 37.1 %all-reduce.8 = (bf16[1024]{0:T(1024)(128)(2,1)S(1)}, bf16[1024]{0:T(1024)(128)(2,1)S(1)}, bf16[1024]{0:T(1024)(128)(2,1)S(1)}, bf16[1024]{0:T(1024)(128)(2,1)S(...) all-reduce(bf16[1024]{0:T(1024)(128)(2,1)S(1)} %get-tuple-element.1, ...), channel_id=8, replica_groups=mesh['dp'=4,'pix'=8] {'pix'}, use_global_device_ids=true, to_apply=%region_74.75.clone | all-reduce | flops 7168 | bytes 28672
  (756 shorter events, 666.0 us)
Async XLA Ops:
  7.2 128.9 %all-gather.18.cloned.1.call-start = ((), (), s32[]{:S(2)}) async-start(), calls=%async_computation.33 | async-start | bytes 1179648 | tf_op jit(solution)/shard_map/all_gather | solution.py:120
  7.9 132.7 %all-gather.20.cloned.1.call-start = ((), (), s32[]{:S(2)}) async-start(), calls=%async_computation.34 | async-start | bytes 2359296 | tf_op jit(solution)/shard_map/all_gather | solution.py:122
  8.7 378.4 %reduce-scatter.76.cloned.1.call-start = ((), (), s32[]{:S(2)}) async-start(), calls=%async_computation.63 | async-start | bytes 147456
  239.8 148.1 %reduce-scatter.78.cloned.1.call-start = ((), (), s32[]{:S(2)}) async-start(), calls=%async_computation.64 | async-start | bytes 147456
  270.3 242.9 %reduce-scatter.40.cloned.1.call-start = ((), (), s32[]{:S(2)}) async-start(), calls=%async_computation.43 | async-start | bytes 9437184 | tf_op jit(solution)/shard_map/reduce_scatter | solution.py:178
  291.6 373.6 %reduce-scatter.38.cloned.1.call-start = ((), (), s32[]{:S(2)}) async-start(), calls=%async_computation.35 | async-start | bytes 9437184 | tf_op jit(solution)/shard_map/reduce_scatter | solution.py:178
  349.5 366.2 %all-gather.22.cloned.1.call-start = ((), (), s32[]{:S(2)}) async-start(), calls=%async_computation.36 | async-start | bytes 2359296 | tf_op jit(solution)/shard_map/all_gather | solution.py:125
  350.2 415.3 %all-gather.24.cloned.1.call-start = ((), (), s32[]{:S(2)}) async-start(), calls=%async_computation.37 | async-start | bytes 2359296 | tf_op jit(solution)/shard_map/all_gather | solution.py:127
  351.0 464.5 %all-gather.26.cloned.1.call-start = ((), (), s32[]{:S(2)}) async-start(), calls=%async_computation.38 | async-start | bytes 2359296 | tf_op jit(solution)/shard_map/all_gather | solution.py:128
  351.7 563.4 %all-gather.28.cloned.1.call-start = ((), (), s32[]{:S(2)}) async-start(), calls=%async_computation.39 | async-start | bytes 7077888 | tf_op jit(solution)/shard_map/all_gather | solution.py:130
  352.3 579.6 %copy-start.23 = (f32[64,1024]{1,0:T(8,128)}, f32[64,1024]{1,0:T(8,128)S(1)}, u32[]{:S(2)}) copy-start(f32[64,1024]{1,0:T(8,128)S(1)} %convert_element_type.570) | copy-start | bytes 786436
  368.5 353.2 %copy-start.120 = (f32[8,1,128]{2,1,0:T(1,128)}, f32[8,1,128]{2,1,0:T(1,128)S(1)}, u32[]{:S(2)}) copy-start(f32[8,1,128]{2,1,0:T(1,128)S(1)} %convert_element_type.757) | copy-start | bytes 12292
  387.0 548.7 %copy-start.151 = (f32[8,1,128]{2,1,0:T(1,128)}, f32[8,1,128]{2,1,0:T(1,128)S(1)}, u32[]{:S(2)}) copy-start(f32[8,1,128]{2,1,0:T(1,128)S(1)} %convert_element_type.758) | copy-start | bytes 12292
  925.2 100.5 %all-to-all-start.2 = ((bf16[8,8,64,384]{3,1,2,0:T(8,128)(2,1)}), bf16[8,8,64,384]{3,1,2,0:T(8,128)(2,1)}, u32[]{:S(2)}, u32[]{:S(2)}) async-start(bf16[8,8,64,384]{3,1,2,0:T(8,128)(2,1)} %bitcast_bitcast_fusion), calls=%async_computation.4 | async-start | bytes 6291456 | tf_op jit(solution)/shard_map/all_to_all | solution.py:196
  929.9 241.1 %all-gather.34.cloned.1.call-start = ((), (), s32[]{:S(2)}) async-start(), calls=%async_computation.42 | async-start | bytes 2359296 | tf_op jit(solution)/shard_map/all_gather | solution.py:134
  1025.7 99.8 %all-to-all-start = ((bf16[8,8,64,384]{3,1,2,0:T(8,128)(2,1)}), bf16[8,8,64,384]{3,1,2,0:T(8,128)(2,1)S(1)}, u32[]{:S(2)}, u32[]{:S(2)}) async-start(bf16[8,8,64,384]{3,1,2,0:T(8,128)(2,1)} %bitcast_bitcast_fusion.1), calls=%async_computation.1 | async-start | bytes 6291456 | tf_op jit(solution)/shard_map/all_to_all | solution.py:196
  1029.3 153.4 %all-gather.30.cloned.1.call-start = ((), (), s32[]{:S(2)}) async-start(), calls=%async_computation.40 | async-start | bytes 2359296 | tf_op jit(solution)/shard_map/all_gather | solution.py:131
  1029.9 157.9 %all-gather.32.cloned.1.call-start = ((), (), s32[]{:S(2)}) async-start(), calls=%async_computation.41 | async-start | bytes 2359296 | tf_op jit(solution)/shard_map/all_gather | solution.py:133
  1125.4 57.2 %all-to-all-start.3 = ((bf16[8,512,128]{2,0,1:T(8,128)(2,1)}), bf16[8,512,128]{2,0,1:T(8,128)(2,1)}, u32[]{:S(2)}, u32[]{:S(2)}) async-start(bf16[8,512,128]{2,0,1:T(8,128)(2,1)} %copy.276), calls=%async_computation.5 | async-start | bytes 2097152 | tf_op jit(solution)/shard_map/all_to_all | solution.py:214
  1129.7 512.9 %reduce-scatter.70.cloned.1.call-start = ((), (), s32[]{:S(2)}) async-start(), calls=%async_computation.60 | async-start | bytes 2359296 | tf_op jit(solution)/shard_map/reduce_scatter | solution.py:359
  1207.1 49.5 %all-to-all-start.1 = ((bf16[8,512,128]{2,0,1:T(8,128)(2,1)}), bf16[8,512,128]{2,0,1:T(8,128)(2,1)}, u32[]{:S(2)}, u32[]{:S(2)}) async-start(bf16[8,512,128]{2,0,1:T(8,128)(2,1)} %copy.265), calls=%async_computation.2 | async-start | bytes 2097152 | tf_op jit(solution)/shard_map/all_to_all | solution.py:214
  1220.1 422.5 %reduce-scatter.68.cloned.1.call-start = ((), (), s32[]{:S(2)}) async-start(), calls=%async_computation.59 | async-start | bytes 2359296 | tf_op jit(solution)/shard_map/reduce_scatter | solution.py:359
  1285.0 41.2 %all-to-all-start.6 = ((bf16[8,8,64,128]{3,2,1,0:T(8,128)(2,1)}), bf16[8,8,64,128]{3,2,1,0:T(8,128)(2,1)}, u32[]{:S(2)}, u32[]{:S(2)}) async-start(bf16[8,8,64,128]{3,2,1,0:T(8,128)(2,1)} %bitcast.409), calls=%async_computation.8 | async-start | bytes 2097152 | tf_op jit(solution)/shard_map/all_to_all | solution.py:232
  1289.3 355.2 %reduce-scatter.66.cloned.1.call-start = ((), (), s32[]{:S(2)}) async-start(), calls=%async_computation.58 | async-start | bytes 2359296 | tf_op jit(solution)/shard_map/reduce_scatter | solution.py:353
  1326.2 33.3 %all-to-all-start.4 = ((bf16[8,8,64,128]{3,2,1,0:T(8,128)(2,1)}), bf16[8,8,64,128]{3,2,1,0:T(8,128)(2,1)}, u32[]{:S(2)}, u32[]{:S(2)}) async-start(bf16[8,8,64,128]{3,2,1,0:T(8,128)(2,1)} %bitcast.408), calls=%async_computation.6 | async-start | bytes 2097152 | tf_op jit(solution)/shard_map/all_to_all | solution.py:232
  1359.6 97.3 %all-to-all-start.7 = ((bf16[8,512,384]{2,0,1:T(8,128)(2,1)}), bf16[8,512,384]{2,0,1:T(8,128)(2,1)}, u32[]{:S(2)}, u32[]{:S(2)}) async-start(bf16[8,512,384]{2,0,1:T(8,128)(2,1)} %copy.310), calls=%async_computation.9 | async-start | bytes 6291456 | tf_op jit(solution)/shard_map/all_to_all | solution.py:262
  1365.5 278.9 %reduce-scatter.64.cloned.1.call-start = ((), (), s32[]{:S(2)}) async-start(), calls=%async_computation.57 | async-start | bytes 2359296 | tf_op jit(solution)/shard_map/reduce_scatter | solution.py:353
  1456.9 82.4 %all-to-all-start.5 = ((bf16[8,512,384]{2,0,1:T(8,128)(2,1)}), bf16[8,512,384]{2,0,1:T(8,128)(2,1)}, u32[]{:S(2)}, u32[]{:S(2)}) async-start(bf16[8,512,384]{2,0,1:T(8,128)(2,1)} %copy.290), calls=%async_computation.7 | async-start | bytes 6291456 | tf_op jit(solution)/shard_map/all_to_all | solution.py:262
  1461.3 208.1 %reduce-scatter.74.cloned.1.call-start = ((), (), s32[]{:S(2)}) async-start(), calls=%async_computation.62 | async-start | bytes 2359296 | tf_op jit(solution)/shard_map/reduce_scatter | solution.py:362
  1466.1 273.6 %reduce-scatter.72.cloned.1.call-start = ((), (), s32[]{:S(2)}) async-start(), calls=%async_computation.61 | async-start | bytes 2359296 | tf_op jit(solution)/shard_map/reduce_scatter | solution.py:362
  1470.6 339.5 %reduce-scatter.58.cloned.1.call-start = ((), (), s32[]{:S(2)}) async-start(), calls=%async_computation.54 | async-start | bytes 2359296 | tf_op jit(solution)/shard_map/reduce_scatter | solution.py:344
  1561.2 319.3 %reduce-scatter.56.cloned.1.call-start = ((), (), s32[]{:S(2)}) async-start(), calls=%async_computation.53 | async-start | bytes 2359296 | tf_op jit(solution)/shard_map/reduce_scatter | solution.py:344
  1569.2 381.8 %reduce-scatter.52.cloned.1.call-start = ((), (), s32[]{:S(2)}) async-start(), calls=%async_computation.51 | async-start | bytes 2359296 | tf_op jit(solution)/shard_map/reduce_scatter | solution.py:341
  1579.1 442.3 %reduce-scatter.54.cloned.1.call-start = ((), (), s32[]{:S(2)}) async-start(), calls=%async_computation.52 | async-start | bytes 2359296 | tf_op jit(solution)/shard_map/reduce_scatter | solution.py:341
  1587.5 504.1 %reduce-scatter.48.cloned.1.call-start = ((), (), s32[]{:S(2)}) async-start(), calls=%async_computation.49 | async-start | bytes 2359296 | tf_op jit(solution)/shard_map/reduce_scatter | solution.py:335
  1601.2 560.7 %reduce-scatter.50.cloned.1.call-start = ((), (), s32[]{:S(2)}) async-start(), calls=%async_computation.50 | async-start | bytes 2359296 | tf_op jit(solution)/shard_map/reduce_scatter | solution.py:335
  1608.7 673.6 %reduce-scatter.62.cloned.1.call-start = ((), (), s32[]{:S(2)}) async-start(), calls=%async_computation.56 | async-start | bytes 7077888 | tf_op jit(solution)/shard_map/reduce_scatter | solution.py:350
  1617.7 785.1 %reduce-scatter.60.cloned.1.call-start = ((), (), s32[]{:S(2)}) async-start(), calls=%async_computation.55 | async-start | bytes 7077888 | tf_op jit(solution)/shard_map/reduce_scatter | solution.py:350
  1626.8 902.3 %all-gather.38.cloned.1.call-start = ((), (), s32[]{:S(2)}) async-start(), calls=%async_computation.45 | async-start | bytes 9437184 | tf_op jit(solution)/shard_map/all_gather | solution.py:280
  1633.6 1020.8 %all-gather.36.cloned.1.call-start = ((), (), s32[]{:S(2)}) async-start(), calls=%async_computation.44 | async-start | bytes 9437184 | tf_op jit(solution)/shard_map/all_gather | solution.py:280
  1802.2 1014.3 %reduce-scatter.86.cloned.1.call-start = ((), (), s32[]{:S(2)}) async-start(), calls=%async_computation.68 | async-start | bytes 884736
  2620.1 197.4 %reduce-scatter.84.cloned.1.call-start = ((), (), s32[]{:S(2)}) async-start(), calls=%async_computation.67 | async-start | bytes 884736
  2743.0 125.5 %reduce-scatter.82.cloned.1.call-start = ((), (), s32[]{:S(2)}) async-start(), calls=%async_computation.66 | async-start | bytes 884736
  2757.9 175.7 %reduce-scatter.80.cloned.1.call-start = ((), (), s32[]{:S(2)}) async-start(), calls=%async_computation.65 | async-start | bytes 884736
  2772.2 227.2 %reduce-scatter.42.cloned.1.call-start = ((), (), s32[]{:S(2)}) async-start(), calls=%async_computation.46 | async-start | bytes 1179648 | tf_op jit(solution)/shard_map/reduce_scatter | solution.py:365
  2782.5 283.2 %reduce-scatter.44.cloned.1.call-start = ((), (), s32[]{:S(2)}) async-start(), calls=%async_computation.47 | async-start | bytes 1179648 | tf_op jit(solution)/shard_map/reduce_scatter | solution.py:365
  2799.0 334.7 %all-reduce.13.cloned.1.call-start = ((), (), s32[]{:S(2)}) async-start(), calls=%async_computation.69 | async-start | bytes 5513216 | tf_op jit(solution)/shard_map/psum | solution.py:385
  3067.4 183.7 %reduce-scatter.46.cloned.1.call-start = ((), (), s32[]{:S(2)}) async-start(), calls=%async_computation.48 | async-start | bytes 2359296 | tf_op jit(solution)/shard_map/reduce_scatter | solution.py:409
  (192 other events, 5487.7 us)
Sparse Core Ops, SparseCore 0:
  10.1 44.1 all-gather.17
  56.5 53.7 all-gather.19
  239.9 58.0 reduce-scatter.75
  301.7 59.8 reduce-scatter.77
  365.2 147.9 reduce-scatter.39
  517.1 148.0 reduce-scatter.37
  667.3 48.2 all-gather.21
  717.8 47.7 all-gather.23
  767.7 47.7 all-gather.25
  817.5 97.5 all-gather.27
  932.9 85.9 all-gather.33
  1032.0 86.6 all-gather.29
  1120.8 58.6 all-gather.31
  1197.7 89.4 reduce-scatter.69
  1290.5 91.3 reduce-scatter.67
  1385.3 143.2 reduce-scatter.65
  1532.0 67.2 reduce-scatter.63
  1602.7 66.6 reduce-scatter.73
  1672.9 66.7 reduce-scatter.71
  1743.1 66.9 reduce-scatter.57
  1813.6 66.8 reduce-scatter.55
  1884.0 66.8 reduce-scatter.51
  1954.5 66.8 reduce-scatter.53
  2024.8 66.6 reduce-scatter.47
  2095.0 66.7 reduce-scatter.49
  2165.3 116.9 reduce-scatter.61
  2285.7 117.0 reduce-scatter.59
  2405.0 124.0 all-gather.37
  2531.2 123.1 all-gather.35
  2657.5 60.5 reduce-scatter.85
  2743.1 60.6 reduce-scatter.83
  2807.1 61.3 reduce-scatter.81
  2872.1 61.4 reduce-scatter.79
  2937.0 62.4 reduce-scatter.41
  3003.2 62.4 reduce-scatter.43
  3070.5 63.2 all-reduce.12
  3137.6 67.8 reduce-scatter.45
where the time goes:
time: 3270 us; the launch traced here: 3260 us
  waiting for transfers between devices  2000 us (61%)
  matrix products  593 us (18%)
  blocking collectives  334 us (10%)
  other arithmetic  136 us (4%)
  local copies, waits for them, and re-layouts  126 us (4%)
  starting transfers between devices  51.2 us (2%)
    reduce_scatter x2, waiting for transfers between devices, body(): lax.psum_scatter(full_num.astype(jnp.bfloat16), 'pix', scatter_dimension=...  273 us
    reduce_scatter x2, waiting for transfers between devices, body(): lax.psum_scatter(terms[7].astype(jnp.bfloat16), 'pix', scatter_dimension=...  239 us
    all_to_all x2, waiting for transfers between devices, body(): lax.all_to_all(packed, 'pix', split_axis=0, concat_axis=2, tiled=True)[0]  165 us
    all_gather x2, waiting for transfers between devices, body(): lax.all_gather(cross_gnum, 'pix', axis=1, tiled=True)  158 us
    reduce_scatter x2, waiting for transfers between devices, body(): lax.psum_scatter(terms[4].astype(jnp.bfloat16), 'pix', scatter_dimension=...  139 us
    reduce_scatter x2, waiting for transfers between devices, body(): lax.psum_scatter(terms[2].astype(jnp.bfloat16), 'pix', scatter_dimension=...  139 us
    reduce_scatter x2, waiting for transfers between devices, body(): lax.psum_scatter(terms[12].astype(jnp.bfloat16), 'pix', scatter_dimension...  130 us
    all_to_all x2, waiting for transfers between devices, body(): lax.all_to_all(grad_packed, 'pix', split_axis=1, concat_axis=0, tiled=True)  124 us
  transfers between devices with their start and end apart: 45, of which 29 were waited for; matrix products, arithmetic and copies ran while one was open for 22% of the time, Pallas kernels for 0%

commit v1 on v0

--- a/solution.py
+++ b/solution.py
@@ -1,6 +1,10 @@
+import functools
+
 import jax
 import jax.numpy as jnp
 from jax import lax
+from jax.experimental import pallas as pl
+from jax.experimental.pallas import tpu as pltpu
 from jax.sharding import PartitionSpec as P
 
 HEADS = 8
@@ -58,7 +62,7 @@
     return (grad + grad_inputs, grad_gain, grad_in, grad_out)
 
 
-def body(
+def starting_body(
     image_sides,
     pixels,
     latent_array,
@@ -438,9 +442,942 @@
     )
 
 
+MESH = pl.DeviceIdType.MESH
+HBM = pl.BlockSpec(memory_space=pl.ANY)
+VMEM = pl.BlockSpec(memory_space=pltpu.VMEM)
+MIB = 1024 * 1024
+PIECE = 256
+BLOCK = 1024
+FROWS = 272
+DEN_ROW = 261
+TOP_ROW = 263
+
+
+def place():
+    dp, pix = lax.axis_index("dp"), lax.axis_index("pix")
+    return dp // 2, dp % 2, pix // 2, pix % 2
+
+
+def device(x, c, z, y):
+    return {"dp": x * 2 + c, "pix": z * 2 + y}
+
+
+def greet(partners):
+    barrier = pltpu.get_barrier_semaphore()
+    for partner in partners:
+        pl.semaphore_signal(barrier, inc=1, device_id=partner, device_id_type=MESH)
+    pl.semaphore_wait(barrier, len(partners))
+
+
+def remote(source, target, sems, index, partner):
+    return pltpu.make_async_remote_copy(
+        src_ref=source,
+        dst_ref=target,
+        send_sem=sems[0].at[index],
+        recv_sem=sems[1].at[index],
+        device_id=partner,
+        device_id_type=MESH,
+    )
+
+
+def remote_params(collective_id, vmem=48 * MIB):
+    return pltpu.CompilerParams(
+        collective_id=collective_id, has_side_effects=True, vmem_limit_bytes=vmem
+    )
+
+
+def gather_kernel(splits, *refs):
+    count = len(splits)
+    shards, cot = refs[:count], refs[count]
+    wholes, cot_rows = refs[count + 1 : 2 * count + 1], refs[2 * count + 1]
+    send, recv, local, cot_send, cot_recv = refs[2 * count + 2 :]
+    x, c, z, y = place()
+    pix = lax.axis_index("pix")
+    sems = (send, recv)
+    others = [(pix + i) % 8 for i in range(1, 8)]
+    core, across, beside = device(x, 1 - c, z, y), device(1 - x, c, z, y), device(x, c, z, 1 - y)
+    greet([{"dp": x * 2 + c, "pix": other} for other in others] + [core, across])
+
+    def part(ref, split):
+        return ref.at[x, c] if split else ref.at[:, c]
+
+    locals_ = []
+    for k in range(count):
+        copy = pltpu.make_async_copy(shards[k], wholes[k].at[z, y], local.at[k])
+        copy.start()
+        locals_.append(copy)
+    copy = pltpu.make_async_copy(cot.at[:, pix], cot_rows.at[:, pix], local.at[count])
+    copy.start()
+    locals_.append(copy)
+    along, side, over, between = {}, {}, {}, {}
+    for k in range(count):
+        mine, home = part(shards[k], splits[k]), part(wholes[k].at[z, y], splits[k])
+        for i in (1, 2, 3):
+            along[k, i] = remote(mine, home, sems, (k, i - 1), device(x, c, (z + i) % 4, y))
+            along[k, i].start()
+        side[k, 0] = remote(mine, home, sems, (k, 3), beside)
+        side[k, 0].start()
+    cots = []
+    for i, other in enumerate(others):
+        copy = remote(
+            cot.at[:, other],
+            cot_rows.at[:, pix],
+            (cot_send, cot_recv),
+            i,
+            {"dp": x * 2 + c, "pix": other},
+        )
+        copy.start()
+        cots.append(copy)
+
+    def to_side(k):
+        for i in (1, 2, 3):
+            along[k, i].wait_recv()
+            block = part(wholes[k].at[(z + 4 - i) % 4, y], splits[k])
+            side[k, i] = remote(block, block, sems, (k, 3 + i), beside)
+            side[k, i].start()
+
+    def over_part(k, i):
+        if i == 0:
+            return wholes[k].at[z, 1 - y, x, c]
+        return wholes[k].at[(z + 4 - i) % 4, :, x, c]
+
+    def core_part(k, i):
+        if i == 0:
+            return wholes[k].at[z, 1 - y, :, c]
+        return wholes[k].at[(z + 4 - i) % 4, :, :, c]
+
+    def to_over(k):
+        for i in range(4):
+            side[k, i].wait_recv()
+            if splits[k]:
+                over[k, i] = remote(
+                    over_part(k, i), over_part(k, i), sems, (k, 7 + i), across
+                )
+                over[k, i].start()
+
+    def to_core(k):
+        for i in range(4):
+            if splits[k]:
+                over[k, i].wait_recv()
+            between[k, i] = remote(core_part(k, i), core_part(k, i), sems, (k, 11 + i), core)
+            between[k, i].start()
+
+    for step in range(count + 2):
+        if step < count:
+            to_side(step)
+        if 1 <= step <= count:
+            to_over(step - 1)
+        if step >= 2:
+            to_core(step - 2)
+    for copy in locals_:
+        copy.wait()
+    for copy in cots:
+        copy.wait()
+    for copy in between.values():
+        copy.wait()
+    for group in (along, side, over):
+        for copy in group.values():
+            copy.wait_send()
+
+
+def gather_weights(shards, splits, cot):
+    count = len(shards)
+    views = [
+        shard.reshape(2, 2, shard.shape[0] // 4, shard.shape[1]) for shard in shards
+    ]
+    outs = [jax.ShapeDtypeStruct((4, 2, *view.shape), view.dtype) for view in views]
+    results = pl.pallas_call(
+        functools.partial(gather_kernel, splits),
+        out_shape=[*outs, jax.ShapeDtypeStruct(cot.shape, cot.dtype)],
+        in_specs=[HBM] * (count + 1),
+        out_specs=[HBM] * (count + 1),
+        scratch_shapes=[
+            pltpu.SemaphoreType.DMA((count, 15)),
+            pltpu.SemaphoreType.DMA((count, 15)),
+            pltpu.SemaphoreType.DMA((count + 1,)),
+            pltpu.SemaphoreType.DMA((7,)),
+            pltpu.SemaphoreType.DMA((7,)),
+        ],
+        compiler_params=remote_params(0),
+        name="gather_weights",
+    )(*views, cot)
+    wholes = [
+        whole.reshape(8 * shard.shape[0], shard.shape[1])
+        for whole, shard in zip(results[:-1], shards, strict=True)
+    ]
+    return wholes, results[-1]
+
+
+def normed_block(raw, gain, wide_ref):
+    features = raw.shape[1]
+    values = raw.astype(jnp.float32)
+    average = jnp.sum(values, 1, keepdims=True) * (1.0 / features)
+    centered = values - average
+    scale = lax.rsqrt(jnp.sum(centered * centered, 1, keepdims=True) * (1.0 / features) + 1e-05)
+    unit = centered * scale
+    lanes = lax.broadcasted_iota(jnp.int32, wide_ref.shape, 1)
+    wide_ref[...] = jnp.where(lanes == DEN_ROW, 1.0, 0.0).astype(jnp.bfloat16)
+    wide_ref[:, :features] = (unit * gain).astype(jnp.bfloat16)
+    return unit, scale
+
+
+def three_parts(row):
+    first = row.astype(jnp.bfloat16).astype(jnp.float32)
+    rest = row - first
+    second = rest.astype(jnp.bfloat16).astype(jnp.float32)
+    return first, second, rest - second
+
+
+def with_rows(tail, den, top):
+    rows = lax.broadcasted_iota(jnp.int32, tail.shape, 0) + (FROWS - 16)
+    high = den.astype(jnp.bfloat16).astype(jnp.float32)
+    first, second, third = three_parts(top)
+    tail = jnp.where(rows == DEN_ROW, high, tail)
+    tail = jnp.where(rows == DEN_ROW + 1, den - high, tail)
+    tail = jnp.where(rows == TOP_ROW, first, tail)
+    tail = jnp.where(rows == TOP_ROW + 1, second, tail)
+    return jnp.where(rows == TOP_ROW + 2, third, tail)
+
+
+def read_rows(tail):
+    at = DEN_ROW - (FROWS - 16)
+    den = tail[at : at + 1] + tail[at + 1 : at + 2]
+    at = TOP_ROW - (FROWS - 16)
+    top = tail[at : at + 1] + tail[at + 1 : at + 2] + tail[at + 2 : at + 3]
+    return den, top
+
+
+def pixel_forward_kernel(
+    segs, pixels, gain, queries, weights, tops, sums, wide_ref, total, largest
+):
+    micro, block = pl.program_id(0), pl.program_id(1)
+    pieces = BLOCK // PIECE
+    per_micro = pieces * pl.num_programs(1)
+    images = total.shape[0]
+
+    @pl.when(block == 0)
+    def _():
+        total[...] = jnp.zeros_like(total)
+        largest[...] = jnp.full(largest.shape, -big_value, jnp.float32)
+
+    normed_block(pixels[0], gain[...], wide_ref)
+    for k in range(pieces):
+        rows = pl.ds(k * PIECE, PIECE)
+        wide = wide_ref[rows, :]
+        scores = jnp.dot(wide, queries[...], preferred_element_type=jnp.float32)
+        top = jnp.max(scores, 0, keepdims=True)
+        low = jnp.exp(scores - top).astype(jnp.bfloat16)
+        weights[0, rows, :] = low
+        tops[0, k] = top
+        added = lax.dot_general(
+            wide[:, :FROWS], low, (((0,), (0,)), ((), ())), preferred_element_type=jnp.float32
+        )
+        seg = segs[micro * per_micro + block * pieces + k]
+
+        @pl.when(seg < images)
+        def _():
+            before = largest[seg, 0:1]
+            now = jnp.maximum(before, top)
+            total[seg] = total[seg] * jnp.exp(before - now) + added * jnp.exp(top - now)
+            largest[seg, 0:1] = now
+
+    @pl.when(block == pl.num_programs(1) - 1)
+    def _():
+        def finish(image, carry):
+            sums[0, image, : FROWS - 16] = total[image, : FROWS - 16].astype(jnp.bfloat16)
+            tail = total[image, FROWS - 16 :]
+            den = total[image, DEN_ROW : DEN_ROW + 1]
+            sums[0, image, FROWS - 16 :] = with_rows(tail, den, largest[image, 0:1]).astype(
+                jnp.bfloat16
+            )
+            return carry
+
+        lax.fori_loop(0, images, finish, 0)
+
+
+def pixel_forward(segs, pixels, gain, queries, images):
+    micros, slots, features = pixels.shape
+    latents = queries.shape[1]
+    blocks = slots // BLOCK
+    return pl.pallas_call(
+        pixel_forward_kernel,
+        grid_spec=pltpu.PrefetchScalarGridSpec(
+            num_scalar_prefetch=1,
+            grid=(micros, blocks),
+            in_specs=[
+                pl.BlockSpec((1, BLOCK, features), lambda m, b, s: (m, b, 0)),
+                pl.BlockSpec((1, features), lambda m, b, s: (0, 0)),
+                pl.BlockSpec(queries.shape, lambda m, b, s: (0, 0)),
+            ],
+            out_specs=[
+                pl.BlockSpec((1, BLOCK, latents), lambda m, b, s: (m, b, 0)),
+                pl.BlockSpec((1, BLOCK // PIECE, 1, latents), lambda m, b, s: (m, b, 0, 0)),
+                pl.BlockSpec((1, images, FROWS, latents), lambda m, b, s: (m, 0, 0, 0)),
+            ],
+            scratch_shapes=[
+                pltpu.VMEM((BLOCK, queries.shape[0]), jnp.bfloat16),
+                pltpu.VMEM((images, FROWS, latents), jnp.float32),
+                pltpu.VMEM((images, 8, latents), jnp.float32),
+            ],
+        ),
+        out_shape=[
+            jax.ShapeDtypeStruct((micros, slots, latents), jnp.bfloat16),
+            jax.ShapeDtypeStruct((micros, slots // PIECE, 1, latents), jnp.float32),
+            jax.ShapeDtypeStruct((micros, images, FROWS, latents), jnp.bfloat16),
+        ],
+        compiler_params=pltpu.CompilerParams(vmem_limit_bytes=48 * MIB),
+        name="pixel_forward",
+    )(segs, pixels, gain, queries)
+
+
+def pixel_backward_kernel(
+    segs,
+    pixels,
+    gain,
+    queries,
+    weights,
+    tops,
+    grads,
+    out,
+    query_sums,
+    gain_sums,
+    wide_ref,
+    scores_ref,
+    back_ref,
+):
+    micro, block = pl.program_id(0), pl.program_id(1)
+    pieces = BLOCK // PIECE
+    per_micro = pieces * pl.num_programs(1)
+    images = grads.shape[1]
+    features = pixels.shape[2]
+
+    @pl.when((block == 0) & (micro == 0))
+    def _():
+        query_sums[...] = jnp.zeros_like(query_sums)
+        gain_sums[...] = jnp.zeros_like(gain_sums)
+
+    unit, scale = normed_block(pixels[0], gain[...], wide_ref)
+    for k in range(pieces):
+        rows = pl.ds(k * PIECE, PIECE)
+        seg = segs[micro * per_micro + block * pieces + k]
+        image = jnp.minimum(seg, images - 1)
+        grad = grads[0, image]
+        unused, top = read_rows(grads[0, image, FROWS - 16 :].astype(jnp.float32))
+        factor = jnp.where(seg < images, jnp.exp(tops[0, k] - top), 0.0)
+        full = weights[0, rows, :].astype(jnp.float32) * factor
+        slopes = jnp.dot(
+            wide_ref[rows, :FROWS], grad, preferred_element_type=jnp.float32
+        )
+        scores_ref[rows, :] = (full * slopes).astype(jnp.bfloat16)
+        back_ref[rows, :] = lax.dot_general(
+            full.astype(jnp.bfloat16),
+            grad,
+            (((1,), (1,)), ((), ())),
+            preferred_element_type=jnp.float32,
+        )
+    scores = scores_ref[...]
+    query_sums[...] += lax.dot_general(
+        wide_ref[:, :FROWS], scores, (((0,), (0,)), ((), ())), preferred_element_type=jnp.float32
+    )
+    back = back_ref[...] + lax.dot_general(
+        scores, queries[:FROWS], (((1,), (1,)), ((), ())), preferred_element_type=jnp.float32
+    )
+    back = back[:, :features]
+    gain_sums[...] += jnp.sum(back * unit, 0, keepdims=True)
+    back = back * gain[...]
+    mean = jnp.sum(back, 1, keepdims=True) * (1.0 / features)
+    slope = jnp.sum(back * unit, 1, keepdims=True) * (1.0 / features)
+    out[0] = (back - mean - unit * slope) * scale
+
+
+def pixel_backward(segs, pixels, gain, queries, weights, tops, grads):
+    micros, slots, features = pixels.shape
+    latents = queries.shape[1]
+    blocks = slots // BLOCK
+    images = grads.shape[1]
+    return pl.pallas_call(
+        pixel_backward_kernel,
+        grid_spec=pltpu.PrefetchScalarGridSpec(
+            num_scalar_prefetch=1,
+            grid=(micros, blocks),
+            in_specs=[
+                pl.BlockSpec((1, BLOCK, features), lambda m, b, s: (m, b, 0)),
+                pl.BlockSpec((1, features), lambda m, b, s: (0, 0)),
+                pl.BlockSpec(queries.shape, lambda m, b, s: (0, 0)),
+                pl.BlockSpec((1, BLOCK, latents), lambda m, b, s: (m, b, 0)),
+                pl.BlockSpec((1, BLOCK // PIECE, 1, latents), lambda m, b, s: (m, b, 0, 0)),
+                pl.BlockSpec((1, images, FROWS, latents), lambda m, b, s: (m, 0, 0, 0)),
+            ],
+            out_specs=[
+                pl.BlockSpec((1, BLOCK, features), lambda m, b, s: (m, b, 0)),
+                pl.BlockSpec((FROWS, latents), lambda m, b, s: (0, 0)),
+                pl.BlockSpec((1, features), lambda m, b, s: (0, 0)),
+            ],
+            scratch_shapes=[
+                pltpu.VMEM((BLOCK, queries.shape[0]), jnp.bfloat16),
+                pltpu.VMEM((BLOCK, latents), jnp.bfloat16),
+                pltpu.VMEM((BLOCK, FROWS), jnp.float32),
+            ],
+        ),
+        out_shape=[
+            jax.ShapeDtypeStruct((micros, slots, features), jnp.float32),
+            jax.ShapeDtypeStruct((FROWS, latents), jnp.float32),
+            jax.ShapeDtypeStruct((1, features), jnp.float32),
+        ],
+        compiler_params=pltpu.CompilerParams(vmem_limit_bytes=48 * MIB),
+        name="pixel_backward",
+    )(segs, pixels, gain, queries, weights, tops, grads)
+
+
+def merge(pieces):
+    bodies = [piece[: FROWS - 16].astype(jnp.float32) for piece in pieces]
+    tails = [piece[FROWS - 16 :].astype(jnp.float32) for piece in pieces]
+    read = [read_rows(tail) for tail in tails]
+    top = functools.reduce(jnp.maximum, [row for unused, row in read])
+    factors = [jnp.exp(row - top) for unused, row in read]
+    body = sum(values * factor for values, factor in zip(bodies, factors, strict=True))
+    tail = sum(values * factor for values, factor in zip(tails, factors, strict=True))
+    den = sum(row * factor for (row, unused), factor in zip(read, factors, strict=True))
+    return body, tail, den, top
+
+
+def owner_kernel(sums, out, rows_out, own, side_in, along_in, send, recv, local):
+    x, c, z, y = place()
+    sems = (send, recv)
+    micros = out.shape[0]
+    beside = device(x, c, z, 1 - y)
+    greet([device(x, c, (z + i) % 4, y) for i in (1, 2, 3)] + [beside])
+    sides, loads = {}, {}
+    for i in (1, 2, 3, 0):
+        sides[i] = remote(sums.at[:, (z + i) % 4, 1 - y], side_in.at[i], sems, i, beside)
+        sides[i].start()
+        loads[i] = pltpu.make_async_copy(sums.at[:, (z + i) % 4, y], own.at[i], local.at[i])
+        loads[i].start()
+    alongs = []
+    for i in (1, 2, 3, 0):
+        loads[i].wait()
+        sides[i].wait_recv()
+        for m in range(micros):
+            body, tail, den, top = merge([own[i, m], side_in[i, m]])
+            own[i, m, : FROWS - 16] = body.astype(jnp.bfloat16)
+            own[i, m, FROWS - 16 :] = with_rows(tail, den, top).astype(jnp.bfloat16)
+        if i:
+            copy = remote(own.at[i], along_in.at[i - 1], sems, 3 + i, device(x, c, (z + i) % 4, y))
+            copy.start()
+            alongs.append(copy)
+    for copy in alongs:
+        copy.wait_recv()
+    for m in range(micros):
+        body, tail, den, top = merge([own[0, m]] + [along_in[i, m] for i in range(3)])
+        rows = lax.broadcasted_iota(jnp.int32, tail.shape, 0) + (FROWS - 16)
+        out[m, : FROWS - 16] = (body / den).astype(jnp.bfloat16)
+        out[m, FROWS - 16 :] = jnp.where(rows < DEN_ROW, tail / den, 0.0).astype(jnp.bfloat16)
+        rows_out[m, 0:1] = den
+        rows_out[m, 1:2] = top
+    for copy in alongs:
+        copy.wait_send()
+    for copy in sides.values():
+        copy.wait_send()
+
+
+def to_owners(sums):
+    micros, images, rows, latents = sums.shape
+    views = sums.reshape(micros, 4, 2, rows, latents)
+    return pl.pallas_call(
+        owner_kernel,
+        out_shape=[
+            jax.ShapeDtypeStruct((micros, rows, latents), jnp.bfloat16),
+            jax.ShapeDtypeStruct((micros, 2, latents), jnp.float32),
+        ],
+        in_specs=[HBM],
+        out_specs=[VMEM, VMEM],
+        scratch_shapes=[
+            pltpu.VMEM((4, micros, rows, latents), jnp.bfloat16),
+            pltpu.VMEM((4, micros, rows, latents), jnp.bfloat16),
+            pltpu.VMEM((3, micros, rows, latents), jnp.bfloat16),
+            pltpu.SemaphoreType.DMA((7,)),
+            pltpu.SemaphoreType.DMA((7,)),
+            pltpu.SemaphoreType.DMA((4,)),
+        ],
+        compiler_params=remote_params(1),
+        name="to_owners",
+    )(views)
+
+
+def holder_kernel(grads, rows_in, out, packed, send, recv, local):
+    x, c, z, y = place()
+    sems = (send, recv)
+    micros = grads.shape[0]
+    beside = device(x, c, z, 1 - y)
+    greet([device(x, c, (z + i) % 4, y) for i in (1, 2, 3)] + [beside])
+    for m in range(micros):
+        packed[m, : FROWS - 16] = grads[m, : FROWS - 16].astype(jnp.bfloat16)
+        tail = grads[m, FROWS - 16 :]
+        rows = lax.broadcasted_iota(jnp.int32, tail.shape, 0) + (FROWS - 16)
+        tail = with_rows(tail, rows_in[m, 0:1], rows_in[m, 1:2])
+        tail = jnp.where(rows == DEN_ROW + 1, 0.0, tail)
+        packed[m, FROWS - 16 :] = tail.astype(jnp.bfloat16)
+    home = out.at[:, z, y]
+    alongs, sides = {}, {}
+    for i in (1, 2, 3):
+        alongs[i] = remote(packed, home, sems, i, device(x, c, (z + i) % 4, y))
+        alongs[i].start()
+    sides[0] = remote(packed, home, sems, 0, beside)
+    sides[0].start()
+    keep = pltpu.make_async_copy(packed, home, local)
+    keep.start()
+    for i in (1, 2, 3):
+        alongs[i].wait_recv()
+        block = out.at[:, (z + 4 - i) % 4, y]
+        sides[i] = remote(block, block, sems, 3 + i, beside)
+        sides[i].start()
+    for copy in sides.values():
+        copy.wait()
+    for copy in alongs.values():
+        copy.wait_send()
+    keep.wait()
+
+
+def to_holders(grads, rows):
+    micros, frows, latents = grads.shape
+    out = pl.pallas_call(
+        holder_kernel,
+        out_shape=jax.ShapeDtypeStruct((micros, 4, 2, frows, latents), jnp.bfloat16),
+        in_specs=[VMEM, VMEM],
+        out_specs=HBM,
+        scratch_shapes=[
+            pltpu.VMEM((micros, frows, latents), jnp.bfloat16),
+            pltpu.SemaphoreType.DMA((7,)),
+            pltpu.SemaphoreType.DMA((7,)),
+            pltpu.SemaphoreType.DMA,
+        ],
+        compiler_params=remote_params(2),
+        name="to_holders",
+    )(grads, rows)
+    return out.reshape(micros, 8, frows, latents)
+
+
+def softmax_parts(packed, scale):
+    width = packed.shape[1] // 3
+    query, key, value = packed[:, :width], packed[:, width : 2 * width], packed[:, 2 * width :]
+    scores = right_matmul(query, key) * scale
+    weights = jnp.exp(scores - jnp.max(scores, 1, keepdims=True))
+    return query, key, value, weights, jnp.sum(weights, 1, keepdims=True)
+
+
+def attention_kernel(scale, packed, out):
+    query, key, value, weights, den = softmax_parts(packed[0], scale)
+    out[0] = (matmul(weights.astype(jnp.bfloat16), value) / den).astype(jnp.bfloat16)
+
+
+def attention_back_kernel(scale, packed, grad, out):
+    width = grad.shape[2]
+    query, key, value, weights, den = softmax_parts(packed[0], scale)
+    grad_num = (grad[0] / den).astype(jnp.bfloat16)
+    slopes = right_matmul(grad_num, value)
+    grad_den = -jnp.sum(weights * slopes, 1, keepdims=True) / den
+    scores = (weights * (slopes + grad_den)).astype(jnp.bfloat16)
+    out[0, :, :width] = (matmul(scores, key) * scale).astype(jnp.bfloat16)
+    out[0, :, width : 2 * width] = (left_matmul(scores, query) * scale).astype(jnp.bfloat16)
+    out[0, :, 2 * width :] = left_matmul(weights.astype(jnp.bfloat16), grad_num).astype(
+        jnp.bfloat16
+    )
+
+
+def head_spec(rows, width):
+    return pl.BlockSpec((1, rows, width), lambda m, h: (m, 0, h))
+
+
+def attention(packed, scale):
+    micros, rows, columns = packed.shape
+    width = columns // HEADS
+    return pl.pallas_call(
+        functools.partial(attention_kernel, scale),
+        grid=(micros, HEADS),
+        in_specs=[head_spec(rows, width)],
+        out_specs=head_spec(rows, width // 3),
+        out_shape=jax.ShapeDtypeStruct((micros, rows, columns // 3), jnp.bfloat16),
+        compiler_params=pltpu.CompilerParams(vmem_limit_bytes=48 * MIB),
+        name="attention",
+    )(packed)
+
+
+def attention_back(packed, grad, scale):
+    micros, rows, columns = packed.shape
+    width = columns // HEADS
+    return pl.pallas_call(
+        functools.partial(attention_back_kernel, scale),
+        grid=(micros, HEADS),
+        in_specs=[head_spec(rows, width), head_spec(rows, width // 3)],
+        out_specs=head_spec(rows, width),
+        out_shape=jax.ShapeDtypeStruct(packed.shape, jnp.bfloat16),
+        compiler_params=pltpu.CompilerParams(vmem_limit_bytes=48 * MIB),
+        name="attention_back",
+    )(packed, grad)
+
+
+def reduce_kernel(splits, *refs):
+    count = len(splits)
+    grads, rows_in = refs[:count], refs[count]
+    finals, rows_out = refs[count + 1 : 2 * count + 1], refs[2 * count + 1]
+    rest = refs[2 * count + 2 :]
+    own, core_in, over_in, side_in, along_in = (
+        rest[i * count : (i + 1) * count] for i in range(5)
+    )
+    send, recv, local, row_send, row_recv = rest[5 * count :]
+    x, c, z, y = place()
+    pix = lax.axis_index("pix")
+    sems = (send, recv)
+    others = [(pix + i) % 8 for i in range(1, 8)]
+    core, across, beside = device(x, 1 - c, z, y), device(1 - x, c, z, y), device(x, c, z, 1 - y)
+    greet([{"dp": x * 2 + c, "pix": other} for other in others] + [core, across])
+    loads, between, over, side, along, back, last = [], [], {}, {}, {}, {}, {}
+    for k in range(count):
+        between.append(remote(grads[k].at[:, :, :, 1 - c], core_in[k], sems, (k, 0), core))
+        between[k].start()
+        loads.append(pltpu.make_async_copy(grads[k].at[:, :, :, c], own[k], local.at[k]))
+        loads[k].start()
+    keep = pltpu.make_async_copy(rows_in.at[:, pix], rows_out.at[:, pix], local.at[count])
+    keep.start()
+    rows = []
+    for i, other in enumerate(others):
+        copy = remote(
+            rows_in.at[:, other],
+            rows_out.at[:, pix],
+            (row_send, row_recv),
+            i,
+            {"dp": x * 2 + c, "pix": other},
+        )
+        copy.start()
+        rows.append(copy)
+
+    def after_core(k):
+        loads[k].wait()
+        between[k].wait()
+
+        def add(i, carry):
+            own[k][i // 2, i % 2] = own[k][i // 2, i % 2] + core_in[k][i // 2, i % 2]
+            return carry
+
+        lax.fori_loop(0, 8, add, 0)
+        if splits[k]:
+            over[k] = remote(own[k].at[:, :, 1 - x], over_in[k], sems, (k, 1), across)
+            over[k].start()
+
+    def after_over(k):
+        if splits[k]:
+            over[k].wait()
+
+            def add(i, carry):
+                own[k][i // 2, i % 2, x] = own[k][i // 2, i % 2, x] + over_in[k][i // 2, i % 2]
+                return carry
+
+            lax.fori_loop(0, 8, add, 0)
+            source = own[k].at[:, 1 - y, x]
+        else:
+            source = own[k].at[:, 1 - y]
+        side[k] = remote(source, side_in[k], sems, (k, 2), beside)
+        side[k].start()
+
+    def after_side(k):
+        side[k].wait()
+
+        def add(i, carry):
+            if splits[k]:
+                own[k][i, y, x] = own[k][i, y, x] + side_in[k][i]
+            else:
+                own[k][i, y] = own[k][i, y] + side_in[k][i]
+            return carry
+
+        lax.fori_loop(0, 4, add, 0)
+        for i in (1, 2, 3):
+            block = own[k].at[(z + i) % 4, y]
+            along[k, i] = remote(
+                block.at[x] if splits[k] else block,
+                along_in[k].at[i - 1],
+                sems,
+                (k, 2 + i),
+                device(x, c, (z + i) % 4, y),
+            )
+            along[k, i].start()
+
+    def after_along(k):
+        for i in (1, 2, 3):
+            along[k, i].wait()
+        block = own[k][z, y, x] if splits[k] else own[k][z, y]
+        total = block.astype(jnp.float32)
+        for i in range(3):
+            total = total + along_in[k][i].astype(jnp.float32)
+        total = total.astype(jnp.bfloat16)
+        if splits[k]:
+            finals[k][x, c] = total
+            back[k] = remote(finals[k].at[x, c], finals[k].at[x, c], sems, (k, 6), across)
+        else:
+            own[k][z, y] = total
+            back[k] = remote(own[k].at[z, y], over_in[k], sems, (k, 6), across)
+        back[k].start()
+
+    def after_back(k):
+        back[k].wait()
+        if not splits[k]:
+            finals[k][:, c] = own[k][z, y] + over_in[k][...]
+        last[k] = remote(finals[k].at[:, c], finals[k].at[:, c], sems, (k, 7), core)
+        last[k].start()
+
+    stages = (after_core, after_over, after_side, after_along, after_back)
+    for step in range(count + len(stages) - 1):
+        for number, stage in enumerate(stages):
+            if 0 <= step - number < count:
+                stage(step - number)
+    for k in range(count):
+        last[k].wait()
+    for copy in rows:
+        copy.wait()
+    keep.wait()
+
+
+def reduce_grads(grads, splits, rows):
+    count = len(grads)
+    views = [
+        grad.reshape(4, 2, 2, 2, grad.shape[0] // 32, grad.shape[1]).astype(jnp.bfloat16)
+        for grad in grads
+    ]
+    buffers = ([], [], [], [], [])
+    for view, split in zip(views, splits, strict=True):
+        block = view.shape[4:]
+        lead = () if split else (2,)
+        for group, shape in zip(
+            buffers,
+            (
+                (4, 2, 2, *block),
+                (4, 2, 2, *block),
+                (4, 2, *block) if split else (2, *block),
+                (4, *lead, *block),
+                (3, *lead, *block),
+            ),
+            strict=True,
+        ):
+            group.append(pltpu.VMEM(shape, jnp.bfloat16))
+    results = pl.pallas_call(
+        functools.partial(reduce_kernel, splits),
+        out_shape=[jax.ShapeDtypeStruct((2, 2, *view.shape[4:]), jnp.bfloat16) for view in views]
+        + [jax.ShapeDtypeStruct(rows.shape, rows.dtype)],
+        in_specs=[HBM] * (count + 1),
+        out_specs=[VMEM] * count + [HBM],
+        scratch_shapes=[
+            *(shape for group in buffers for shape in group),
+            pltpu.SemaphoreType.DMA((count, 8)),
+            pltpu.SemaphoreType.DMA((count, 8)),
+            pltpu.SemaphoreType.DMA((count + 1,)),
+            pltpu.SemaphoreType.DMA((7,)),
+            pltpu.SemaphoreType.DMA((7,)),
+        ],
+        compiler_params=remote_params(3, 56 * MIB),
+        name="reduce_grads",
+    )(*views, rows)
+    shards = [
+        result.reshape(grad.shape[0] // 8, grad.shape[1])
+        for result, grad in zip(results[:-1], grads, strict=True)
+    ]
+    return shards, results[-1]
+
+
+def spread_kernel(block, out, send, recv):
+    pix, dp = lax.axis_index("pix"), lax.axis_index("dp")
+    others = [(pix + i) % 8 for i in range(1, 8)]
+    greet([{"dp": dp, "pix": other} for other in others])
+    copies = []
+    for i, other in enumerate(others):
+        copy = remote(block, out.at[pix], (send, recv), i, {"dp": dp, "pix": other})
+        copy.start()
+        copies.append(copy)
+    out[pix] = block[...]
+    for copy in copies:
+        copy.wait()
+
+
+def spread(block):
+    return pl.pallas_call(
+        spread_kernel,
+        out_shape=jax.ShapeDtypeStruct((8, *block.shape), block.dtype),
+        in_specs=[VMEM],
+        out_specs=VMEM,
+        scratch_shapes=[pltpu.SemaphoreType.DMA((7,)), pltpu.SemaphoreType.DMA((7,))],
+        compiler_params=remote_params(4),
+        name="spread",
+    )(block)
+
+
+def image_body(
+    image_sides,
+    pixels,
+    latent_array,
+    pixel_gain,
+    latent_gain,
+    query_weight,
+    key_weight,
+    value_weight,
+    cross_out_weight,
+    cross_mlp_gain,
+    cross_mlp_in,
+    cross_mlp_out,
+    self_gain,
+    self_qkv_weight,
+    self_out_weight,
+    self_mlp_gain,
+    self_mlp_in,
+    self_mlp_out,
+    cotangent,
+):
+    position = lax.axis_index("pix")
+    micros, images = image_sides.shape[1:]
+    capacity, features = pixels.shape[2:]
+    row_count, width = latent_array.shape
+    latents = row_count * 8
+    head_size = width // HEADS
+    cross_scale = width ** (-0.5)
+    self_scale = head_size ** (-0.5)
+    f32, bf16 = jnp.float32, jnp.bfloat16
+
+    def widen(values, columns):
+        return jnp.pad(values, ((0, 0), (0, columns - values.shape[1])))
+
+    gains = jnp.stack([latent_gain, cross_mlp_gain, self_gain, self_mlp_gain], 1)
+    misc = jnp.concatenate(
+        [widen(key_weight.T, 384), widen(value_weight.T, 384), widen(gains, 256)], 1
+    )
+    shards = (
+        latent_array,
+        query_weight,
+        misc,
+        cross_out_weight,
+        cross_mlp_in,
+        cross_mlp_out,
+        self_qkv_weight,
+        self_out_weight,
+        self_mlp_in,
+        self_mlp_out,
+    )
+    splits = (True, True, True, True, True, True, True, True, True, True)
+    wholes, cot_rows = gather_weights(shards, splits, cotangent[0])
+    lat_full, wq, misc, wo, w1c, w2c, wqkv, wos, w1s, w2s = wholes
+    key_t, value_t = misc[:, :384], misc[:, 384 : 384 + FROWS]
+    g_lat, g_cross, g_self, g_mlp = (misc[:, 768 + i].astype(f32) for i in range(4))
+    lat_f = lat_full.astype(f32)
+    normed_lat = layer_norm(lat_f, g_lat).astype(bf16)
+    queries = matmul(normed_lat, wq).astype(bf16)
+    query_t = (
+        lax.dot_general(key_t, queries, (((0,), (1,)), ((), ())), preferred_element_type=f32)
+        * cross_scale
+    ).astype(bf16)
+
+    lengths = image_sides[0] * image_sides[0]
+    ends = jnp.cumsum(lengths, 1)
+    firsts = position * capacity + PIECE * jnp.arange(capacity // PIECE, dtype=jnp.int32)
+    segs = jnp.sum((firsts[None, :, None] >= ends[:, None, :]).astype(jnp.int32), 2).reshape(-1)
+    gain_pix = pixel_gain.astype(f32)[None]
+    pix_weights, pix_tops, sums = pixel_forward(segs, pixels[0], gain_pix, query_t, images)
+    means, rows = to_owners(sums)
+    den, top = rows[:, 0], rows[:, 1]
+
+    att = jnp.einsum("mfr,df->mrd", means, value_t, preferred_element_type=f32)
+    att_low = att.astype(bf16).reshape(micros * latents, width)
+    start_rows = jnp.broadcast_to(lat_f[None], (micros, latents, width)).reshape(-1, width)
+    after_cross = start_rows + matmul(att_low, wo)
+    after_mlp, cross_kept = mlp_forward(after_cross, g_cross, w1c, w2c)
+    normed_self = layer_norm(after_mlp, g_self).astype(bf16)
+    packed = matmul(normed_self, wqkv).astype(bf16).reshape(micros, latents, 3 * width)
+    self_att = attention(packed, self_scale).reshape(-1, width)
+    after_self = after_mlp + matmul(self_att, wos)
+    final, final_kept = mlp_forward(after_self, g_mlp, w1s, w2s)
+    final = final.astype(bf16).reshape(micros, 8, row_count, width)
+
+    grad = cot_rows.astype(f32).reshape(-1, width)
+    grad, d_gm, d_w1s, d_w2s = mlp_backward(grad, after_self, g_mlp, w1s, w2s, final_kept)
+    grad_low = grad.astype(bf16)
+    d_wos = left_matmul(self_att, grad_low)
+    grad_att = right_matmul(grad_low, wos).reshape(micros, latents, width)
+    grad_packed = attention_back(packed, grad_att, self_scale).reshape(-1, 3 * width)
+    d_wqkv = left_matmul(normed_self, grad_packed)
+    grad_inputs, d_gs = norm_back(after_mlp, g_self, right_matmul(grad_packed, wqkv))
+    grad = grad + grad_inputs
+    grad, d_gc, d_w1c, d_w2c = mlp_backward(grad, after_cross, g_cross, w1c, w2c, cross_kept)
+    grad_lat = jnp.sum(grad.reshape(micros, latents, width), 0)
+    grad_low = grad.astype(bf16)
+    d_wo = left_matmul(att_low, grad_low)
+    grad_att = right_matmul(grad_low, wo).reshape(micros, latents, width)
+    grad_num = (grad_att / den[:, :, None]).astype(bf16)
+    grad_den = -jnp.sum(grad_att * att, 2) / den
+    grad_sums = jnp.einsum("mrd,df->mfr", grad_num, value_t, preferred_element_type=f32)
+    d_wv = jnp.einsum("mrd,mfr->df", grad_att.astype(bf16), means, preferred_element_type=f32)
+    all_grads = to_holders(grad_sums, jnp.stack([grad_den, top], 1))
+    pixel_grad, query_sums, pix_gain_sums = pixel_backward(
+        segs, pixels[0], gain_pix, query_t, pix_weights, pix_tops, all_grads
+    )
+
+    gain_grads = jnp.stack([d_gc, d_gs, d_gm], 1)
+    small = jnp.concatenate([widen(d_wv, 384), widen(gain_grads, 128)], 1)
+    halves = grad_lat.reshape(8, row_count, 2, width // 2).transpose(0, 2, 1, 3)
+    small = jnp.concatenate([small, halves.reshape(8 * 2 * row_count, width // 2)], 1)
+    query_rows = widen(query_sums.T, 384).reshape(8, row_count, 384)
+    pix_gain_rows = jnp.pad(
+        widen(pix_gain_sums, 384)[None], ((0, 7), (0, row_count - 1), (0, 0))
+    )
+    query_rows = jnp.concatenate([query_rows, pix_gain_rows], 1).reshape(-1, 384)
+    parts = (
+        d_w2s,
+        d_w1s,
+        d_wos,
+        d_wqkv,
+        d_w2c,
+        d_w1c,
+        d_wo,
+        small,
+        query_rows,
+    )
+    splits = (True, False, True, True, False, True, False, True, True)
+    reduced, latent_out = reduce_grads(parts, splits, final)
+    f_w2s, f_w1s, f_wos, f_wqkv, f_w2c, f_w1c, f_wo, small, query_rows = reduced
+    query_all = spread(query_rows)
+    d_gpix = query_all[0, row_count, :features].astype(f32)
+    query_all = query_all[:, :row_count].reshape(latents, 384)
+
+    grad_queries = (right_matmul(query_all, key_t) * cross_scale).astype(bf16)
+    columns = lax.dynamic_slice_in_dim(normed_lat, position * (width // 8), width // 8, 1)
+    d_wq = left_matmul(columns, grad_queries)
+    query_columns = lax.dynamic_slice_in_dim(queries, position * (width // 8), width // 8, 1)
+    d_wk = (left_matmul(query_all, query_columns) * cross_scale)[:features]
+    grad_norm_lat, d_glat = norm_back(lat_f, g_lat, right_matmul(grad_queries, wq))
+    d_glat = lax.dynamic_slice_in_dim(d_glat, position * (width // 8), width // 8, 0)
+    grad_norm_rows = lax.dynamic_slice_in_dim(grad_norm_lat, position * row_count, row_count, 0)
+    grad_lat = small[:, width // 2 :].astype(f32).reshape(2, row_count, width // 2)
+    grad_lat = grad_lat.transpose(1, 0, 2).reshape(row_count, width)
+    return (
+        latent_out[None],
+        pixel_grad[None],
+        grad_lat + grad_norm_rows,
+        d_gpix,
+        d_glat,
+        d_wq,
+        d_wk,
+        small[:, :features].astype(f32).T,
+        f_wo.astype(f32),
+        small[:, 384].astype(f32),
+        f_w1c.astype(f32),
+        f_w2c.astype(f32),
+        small[:, 385].astype(f32),
+        f_wqkv.astype(f32),
+        f_wos.astype(f32),
+        small[:, 386].astype(f32),
+        f_w1s.astype(f32),
+        f_w2s.astype(f32),
+    )
+
+
 def solution(mesh):
+    fits = dict(mesh.shape) == {"dp": 4, "pix": 8}
     return jax.shard_map(
-        body,
+        image_body if fits else starting_body,
         mesh=mesh,
         in_specs=(
             P("dp", None, None),

time: 3270 us -> 818 us (0.25)
  waiting for transfers between devices: 2000 us -> 0 us
  Pallas kernels: 0 us -> 564 us
  matrix products: 593 us -> 121 us
  blocking collectives: 334 us -> 0 us
  other arithmetic: 136 us -> 39.3 us
  starting transfers between devices: 51.2 us -> 0 us
  local copies, waits for them, and re-layouts: 126 us -> 78.1 us
    reduce_scatter x19 -> x0, waiting for transfers between devices: 1090 us -> none  [the longest x2 273 us: body(): lax.psum_scatter(full_num.astype(jnp.bfloat16), 'pix', scatter_dimension=...]
    pallas_call x0 -> x9, Pallas kernels: none -> 564 us  [the longest x1 158 us: reduce_grads(): pl.pallas_call(functools.partial(reduce_kernel, splits), out_shape=[jax.S...]
    all_gather x11 -> x0, waiting for transfers between devices: 388 us -> none  [the longest x2 158 us: body(): lax.all_gather(cross_gnum, 'pix', axis=1, tiled=True)]
    all_to_all x8 -> x0, waiting for transfers between devices: 349 us -> none  [the longest x2 165 us: body(): lax.all_to_all(packed, 'pix', split_axis=0, concat_axis=2, tiled=True)[0]]
    dot_general x28 -> x4, matrix products: 302 us -> 8.53 us  [the longest x1 3.94 us: image_body(): att = jnp.einsum('mfr,df->mrd', means, value_t, preferred_element_type=f32)]
    all_gather x8 -> x0, blocking collectives: 207 us -> none  [the longest x2 52.1 us: body(): lax.all_gather(cross_gden, 'pix', axis=1, tiled=True)]
    unnamed x43 -> x0, waiting for transfers between devices: 120 us -> none
    dot_general x21 -> x9, matrix products: 107 us -> 41.3 us  [right_matmul(): lax.dot_general(left, right, (((1,), (1,)), ((), ())), preferred_element_...]
  transfers between devices with their start and end apart: 45 -> 0, of which waited for: 29 -> 0; matrix products, arithmetic and copies ran while one was open for 22% -> 0% of each run, Pallas kernels for 0% -> 0%
where the time goes in v1:
time: 818 us; the launch traced here: 805 us
  Pallas kernels  564 us (69%)
  matrix products  121 us (15%)
  local copies, waits for them, and re-layouts  78.1 us (10%)
  other arithmetic  39.3 us (5%)
    pallas_call x1, Pallas kernels, reduce_grads(): pl.pallas_call(functools.partial(reduce_kernel, splits), out_shape=[jax.S...  158 us
    pallas_call x1, Pallas kernels, gather_weights(): pl.pallas_call(functools.partial(gather_kernel, splits), out_shape=[*outs...  158 us
    pallas_call x1, Pallas kernels, to_owners(): pl.pallas_call(owner_kernel, out_shape=[jax.ShapeDtypeStruct((micros, row...  68.7 us
    pallas_call x1, Pallas kernels, to_holders(): pl.pallas_call(holder_kernel, out_shape=jax.ShapeDtypeStruct((micros, 4,...  65.1 us
    unnamed x148, local copies, waits for them, and re-layouts  51 us
    dot_general x9, matrix products, right_matmul(): lax.dot_general(left, right, (((1,), (1,)), ((), ())), preferred_element_...  41.3 us
    dot_general x9, matrix products, left_matmul(): lax.dot_general(left, right, (((0,), (0,)), ((), ())), preferred_element_...  36.7 us
    dot_general x8, matrix products, matmul(): return jnp.dot(left, right, preferred_element_type=jnp.float32)  34.6 us

profile of v1, /device:TPU:0, one launch (start us, length us, event | category | flops | bytes accessed | tf_op | source)
XLA Modules:
  0.0 804.8 jit_solution(6017764728574657535)
XLA Ops:
  4.3 12.0 %copy.84 = bf16[1,2,4096,261]{3,2,1,0:T(8,128)(2,1)} copy(bf16[1,2,4096,261]{2,1,3,0:T(2,128)(2,1)} %param.20) | data formatting | bytes 8552448 | tf_op args[1]
  18.2 157.5 %gather_weights.1 = (bf16[4,2,2,2,16,1024]{5,4,3,2,1,0:T(8,128)(2,1)S(1)}, bf16[4,2,2,2,32,1024]{5,4,3,2,1,0:T(8,128)(2,1)S(1)}, bf16[4,2,2,2,32,1024]{5,4,3,2,1...) custom-call(bf16[2,2,16,1024]{3,2,1,0:T(8,128)(2,1)S(1)} %bitcast.24, ...), custom_call_target="tpu_custom_call" | custom-call | tf_op jit(solution)/shard_map/gather_weights/pallas_call | solution.py:589
  180.7 3.1 slice_convert_fusion
  191.6 28.7 %pixel_forward.1 = (bf16[2,4096,512]{2,1,0:T(8,128)(2,1)}, f32[2,16,1,512]{3,2,1,0:T(1,128)S(1)}, bf16[2,8,272,512]{3,2,1,0:T(8,128)(2,1)S(1)}) custom-call(s32[32]{0:T(128)S(1)} %reshape.430.segs, bf16[2,4096,261]{2,1,0:T(8,128)(2,1)} %bitcast.244, f32[1,261]{1,0:T(1,128)S(1)} %reshape.458.gain, bf16[384,512]{1,0:T(8,128)(2,1)S(1)} %fusion.52.queries), custom_call_target="tpu_custom_call" | custom-call | tf_op jit(solution)/shard_map/pixel_forward/pallas_call | solution.py:702
  220.4 68.7 %to_owners.1 = (bf16[2,272,512]{2,1,0:T(8,128)(2,1)S(1)}, f32[2,2,512]{2,1,0:T(2,128)S(1)}) custom-call(bf16[2,4,2,272,512]{4,3,2,1,0:T(8,128)(2,1)S(1)} %bitcast.230), custom_call_target="tpu_custom_call" | custom-call | tf_op jit(solution)/shard_map/to_owners/pallas_call | solution.py:886
  289.8 3.9 fusion.99
  293.8 4.4 copy.97
  298.2 4.6 fusion.24
  306.6 2.3 fusion.102
  308.9 2.9 fusion.100
  312.4 8.9 %convolution_convert_fusion.1 = bf16[1024,3072]{1,0:T(8,128)(2,1)} fusion(bf16[1024,3072]{1,0:T(8,128)(2,1)S(1)} %bitcast.317, f32[1024,1024]{1,0:T(8,128)S(1)} %get-tuple-element.167, f32[1024]{0:T(1024)S(1)} %bitcast.302, f32[1024]{0:T(1024)S(1)} %fusion.82, f32[1024]{0:T(1024)S(1)} %broadcast_multiply_fusion.2), kind=kOutput, calls=%fused_computation.9 | convolution fusion | flops 6449790976 | bytes 16789504 | tf_op jit(solution)/shard_map/dot_general | solution.py:25
  321.3 15.7 %attention.1 = bf16[2,512,1024]{2,1,0:T(8,128)(2,1)S(1)} custom-call(bf16[2,512,3072]{2,1,0:T(8,128)(2,1)} %bitcast.246), custom_call_target="tpu_custom_call" | custom-call | tf_op jit(solution)/shard_map/attention/pallas_call | solution.py:994
  337.0 2.8 copy.95
  339.8 5.2 fusion.101
  345.6 2.5 copy-done.61
  348.1 5.3 fusion.21
  353.5 3.7 convolution_convert_fusion.5.refs_0_
  357.1 5.4 copy.93
  362.5 7.3 fusion.13
  369.8 4.1 add_convert_fusion
  373.9 4.3 convolution_convert_fusion.4
  378.2 2.9 multiply_reduce_fusion.1
  381.1 2.2 fusion.97
  384.9 3.7 fusion.38.refs_2_
  388.6 2.4 fusion.103.grad
  391.0 26.4 %attention_back.1 = bf16[2,512,3072]{2,1,0:T(8,128)(2,1)} custom-call(bf16[2,512,3072]{2,1,0:T(8,128)(2,1)} %bitcast.247, f32[2,512,1024]{2,1,0:T(8,128)S(1)} %fusion.103.grad), custom_call_target="tpu_custom_call" | custom-call | tf_op jit(solution)/shard_map/attention_back/pallas_call | solution.py:1008
  417.4 11.4 %multiply_reduce_fusion.2 = (bf16[1024]{0:T(1024)(128)(2,1)S(1)}, f32[1024]{0:T(1024)S(1)}, f32[1024,1024]{1,0:T(8,128)S(1)}) fusion(f32[1024,1024]{1,0:T(8,128)S(1)} %copy-done.24, f32[1024]{0:T(1024)S(1)} %fusion.82, f32[1024]{0:T(1024)S(1)} %broadcast_multiply_fusion.2, f32[1024]{0:T(1024)S(1)} %bitcast.303, bf16[1024,3072]{1,0:T(8,128)(2,1)} %bitcast.254, ...), kind=kOutput, calls=%fused_computation.38 | convolution fusion | flops 6449788928 | bytes 20989952 | tf_op jit(solution)/shard_map/dot_general | solution.py:35
  428.8 2.1 fusion.96
  433.8 4.9 fusion.6
  438.7 4.1 convolution_convert_fusion.3
  442.8 3.7 convolution_convert_fusion.2
  446.5 3.0 multiply_reduce_fusion.3
  451.8 3.2 fusion.94
  455.0 3.9 reduce_sum.232
  458.8 2.0 reshape.447
  462.1 6.0 multiply_reduce_fusion
  470.5 3.7 fusion.41.refs_6_
  474.9 2.4 fusion.48.grads
  477.3 2.2 copy.123
  479.5 2.1 pad.39.clone
  482.6 3.1 pad_maximum_fusion.refs_7_
  485.7 2.5 copy.96
  488.3 11.1 %convolution_convert_fusion.refs_3_ = bf16[4,2,2,2,32,3072]{5,4,3,2,1,0:T(8,128)(2,1)} fusion(bf16[4,2,2,2,32,1024]{5,4,3,2,1,0:T(8,128)(2,1)} %bitcast.274, bf16[1024,3072,1,1,1,1]{1,0,5,4,3,2:T(8,128)(2,1)} %bitcast.255), kind=kOutput, calls=%fused_computation.8 | convolution fusion | flops 6445596672 | bytes 14680064 | tf_op jit(solution)/shard_map/dot_general | solution.py:29
  499.4 65.1 %to_holders.1 = bf16[2,4,2,272,512]{4,3,2,1,0:T(8,128)(2,1)S(1)} custom-call(f32[2,272,512]{2,1,0:T(8,128)S(1)} %fusion.48.grads, f32[2,2,512]{2,1,0:T(2,128)S(1)} %pad_maximum_fusion.2.rows_in), custom_call_target="tpu_custom_call" | custom-call | tf_op jit(solution)/shard_map/to_holders/pallas_call | solution.py:943
  564.5 27.6 %pixel_backward.1 = (f32[2,4096,261]{2,1,0:T(8,128)}, f32[272,512]{1,0:T(8,128)S(1)}, f32[1,261]{1,0:T(1,128)S(1)}) custom-call(s32[32]{0:T(128)S(1)} %reshape.430.segs, bf16[2,4096,261]{2,1,0:T(8,128)(2,1)} %bitcast.245, f32[1,261]{1,0:T(1,128)S(1)} %reshape.458.gain, bf16[384,512]{1,0:T(8,128)(2,1)S(1)} %copy-done.5, ...), custom_call_target="tpu_custom_call" | custom-call | tf_op jit(solution)/shard_map/pixel_backward/pallas_call | solution.py:798
  593.4 158.4 %reduce_grads.1 = (bf16[2,2,32,1024]{3,2,1,0:T(8,128)(2,1)}, bf16[2,2,32,1024]{3,2,1,0:T(8,128)(2,1)}, bf16[2,2,32,1024]{3,2,1,0:T(8,128)(2,1)}, bf16[2,2,32,307...) custom-call(bf16[4,2,2,2,32,1024]{5,4,3,2,1,0:T(8,128)(2,1)} %convol, ...), custom_call_target="tpu_custom_call" | custom-call | tf_op jit(solution)/shard_map/reduce_grads/pallas_call | solution.py:1161
  757.9 16.1 %spread.1 = bf16[8,128,384]{2,1,0:T(8,128)(2,1)S(1)} custom-call(bf16[128,384]{1,0:T(8,128)(2,1)S(1)} %bitcast.241), custom_call_target="tpu_custom_call" | custom-call | tf_op jit(solution)/shard_map/spread/pallas_call | solution.py:1200
  788.4 14.6 %copy.108 = f32[1,2,4096,261]{2,1,3,0:T(2,128)} copy(f32[1,2,4096,261]{3,2,1,0:T(8,128)} %bitcast.251) | data formatting | bytes 17104896
  (224 shorter events, 58.6 us)
Async XLA Ops:
  4.2 12.1 %copy-start.6 = (bf16[128,3072]{1,0:T(8,128)(2,1)S(1)}, bf16[128,3072]{1,0:T(8,128)(2,1)}, u32[]{:S(2)}) copy-start(bf16[128,3072]{1,0:T(8,128)(2,1)} %param.32) | copy-start | bytes 2359300
  4.2 12.1 %copy-start.7 = (bf16[128,1024]{1,0:T(8,128)(2,1)S(1)}, bf16[128,1024]{1,0:T(8,128)(2,1)}, u32[]{:S(2)}) copy-start(bf16[128,1024]{1,0:T(8,128)(2,1)} %param.24) | copy-start | bytes 786436
  4.2 12.1 %copy-start.8 = (bf16[128,1024]{1,0:T(8,128)(2,1)S(1)}, bf16[128,1024]{1,0:T(8,128)(2,1)}, u32[]{:S(2)}) copy-start(bf16[128,1024]{1,0:T(8,128)(2,1)} %param.27) | copy-start | bytes 786436
  4.2 12.0 %copy-start.9 = (bf16[128,1024]{1,0:T(8,128)(2,1)S(1)}, bf16[128,1024]{1,0:T(8,128)(2,1)}, u32[]{:S(2)}) copy-start(bf16[128,1024]{1,0:T(8,128)(2,1)} %param.29) | copy-start | bytes 786436
  4.3 12.0 %copy-start.10 = (bf16[128,1024]{1,0:T(8,128)(2,1)S(1)}, bf16[128,1024]{1,0:T(8,128)(2,1)}, u32[]{:S(2)}) copy-start(bf16[128,1024]{1,0:T(8,128)(2,1)} %param.30) | copy-start | bytes 786436
  4.3 12.0 %copy-start.11 = (bf16[128,1024]{1,0:T(8,128)(2,1)S(1)}, bf16[128,1024]{1,0:T(8,128)(2,1)}, u32[]{:S(2)}) copy-start(bf16[128,1024]{1,0:T(8,128)(2,1)} %param.33) | copy-start | bytes 786436
  4.3 12.0 %copy-start.14 = (bf16[64,1024]{1,0:T(8,128)(2,1)S(1)}, bf16[64,1024]{1,0:T(8,128)(2,1)}, u32[]{:S(2)}) copy-start(bf16[64,1024]{1,0:T(8,128)(2,1)} %param.21) | copy-start | bytes 393220
  177.1 12.2 %copy-start = (bf16[4,2,2,2,16,1024]{5,4,3,2,1,0:T(8,128)(2,1)}, bf16[4,2,2,2,16,1024]{5,4,3,2,1,0:T(8,128)(2,1)S(1)}, u32[]{:S(2)}) copy-start(bf16[4,2,2,2,16,1024]{5,4,3,2,1,0:T(8,128)(2,1)S(1)} %get-tuple-element.47) | copy-start | bytes 3145732
  180.7 9.0 %copy-start.17 = (bf16[4,2,2,2,32,1024]{5,4,3,2,1,0:T(8,128)(2,1)S(1)}, bf16[4,2,2,2,32,1024]{5,4,3,2,1,0:T(8,128)(2,1)}, u32[]{:S(2)}) copy-start(bf16[4,2,2,2,32,1024]{5,4,3,2,1,0:T(8,128)(2,1)} %copy-done.16) | copy-start | bytes 6291460
  191.0 29.4 %copy-start.56 = (bf16[512,1024]{1,0:T(8,128)(2,1)}, bf16[512,1024]{1,0:T(8,128)(2,1)S(1)}, u32[]{:S(2)}) copy-start(bf16[512,1024]{1,0:T(8,128)(2,1)S(1)} %convolution_convert_fusion.6) | copy-start | bytes 3145732
  191.6 28.7 %copy-start.4 = (bf16[384,512]{1,0:T(8,128)(2,1)}, bf16[384,512]{1,0:T(8,128)(2,1)S(1)}, u32[]{:S(2)}) copy-start(bf16[384,512]{1,0:T(8,128)(2,1)S(1)} %fusion.52.queries) | copy-start | bytes 1179652
  289.8 8.3 %copy-start.21 = (f32[512,1024]{1,0:T(8,128)S(1)}, f32[512,1024]{1,0:T(8,128)}, u32[]{:S(2)}) copy-start(f32[512,1024]{1,0:T(8,128)} %convert.95) | copy-start | bytes 6291460
  302.8 6.1 copy-start.19
  303.5 3.1 copy-start.34
  306.6 5.9 slice-start
  308.9 2.9 copy-start.31
  308.9 3.5 slice-start.1
  311.8 9.5 %copy-start.23 = (f32[1024,1024]{1,0:T(8,128)}, f32[1024,1024]{1,0:T(8,128)S(1)}, u32[]{:S(2)}) copy-start(f32[1024,1024]{1,0:T(8,128)S(1)} %get-tuple-element.167) | copy-start | bytes 12582916
  345.0 8.4 %copy-start.25 = (f32[1024,1024]{1,0:T(8,128)}, f32[1024,1024]{1,0:T(8,128)S(1)}, u32[]{:S(2)}) copy-start(f32[1024,1024]{1,0:T(8,128)S(1)} %get-tuple-element.169) | copy-start | bytes 12582916
  345.0 3.1 copy-start.61
  348.1 5.3 copy-start.29
  362.5 7.3 copy-start.26
  362.5 7.3 copy-start.33
  362.5 7.3 copy-start.63
  373.9 4.4 copy-start.62
  384.9 3.7 copy-start.60
  391.0 26.4 %copy-start.24 = (f32[1024,1024]{1,0:T(8,128)S(1)}, f32[1024,1024]{1,0:T(8,128)}, u32[]{:S(2)}) copy-start(f32[1024,1024]{1,0:T(8,128)} %copy-done.23) | copy-start | bytes 12582916
  430.9 2.9 copy-start.37
  433.8 4.9 copy-start.27
  438.7 4.1 copy-start.39
  442.8 3.8 copy-start.20
  442.8 3.8 copy-start.22
  442.8 3.8 copy-start.35
  462.1 6.0 copy-start.3
  499.4 65.1 %copy-start.5 = (bf16[384,512]{1,0:T(8,128)(2,1)S(1)}, bf16[384,512]{1,0:T(8,128)(2,1)}, u32[]{:S(2)}) copy-start(bf16[384,512]{1,0:T(8,128)(2,1)} %copy-done.4) | copy-start | bytes 1179652
  593.4 185.0 %copy-start.18 = (bf16[4,2,2,2,32,1024]{5,4,3,2,1,0:T(8,128)(2,1)S(1)}, bf16[4,2,2,2,32,1024]{5,4,3,2,1,0:T(8,128)(2,1)}, u32[]{:S(2)}) copy-start(bf16[4,2,2,2,32,1024]{5,4,3,2,1,0:T(8,128)(2,1)} %copy-done.16) | copy-start | bytes 6291460
  751.8 26.6 %copy-start.1 = (bf16[4,2,2,2,16,1024]{5,4,3,2,1,0:T(8,128)(2,1)S(1)}, bf16[4,2,2,2,16,1024]{5,4,3,2,1,0:T(8,128)(2,1)}, u32[]{:S(2)}) copy-start(bf16[4,2,2,2,16,1024]{5,4,3,2,1,0:T(8,128)(2,1)} %copy-done) | copy-start | bytes 3145732
  751.8 26.6 %copy-start.53 = (f32[1024,1]{0,1:T(1,128)S(1)}, f32[1024,1]{0,1:T(1,128)}, u32[]{:S(2)}) copy-start(f32[1024,1]{0,1:T(1,128)} %copy-done.52) | copy-start | bytes 12292
  751.8 26.6 %copy-start.57 = (f32[512]{0:T(512)S(1)}, f32[512]{0:T(512)}, u32[]{:S(2)}) copy-start(f32[512]{0:T(512)} %div.117) | copy-start | bytes 6148
  751.8 26.6 %copy-start.58 = (f32[512]{0:T(512)S(1)}, f32[512]{0:T(512)}, u32[]{:S(2)}) copy-start(f32[512]{0:T(512)} %rsqrt.51) | copy-start | bytes 6148
  780.7 3.0 copy-start.50
  780.7 2.9 copy-start.51
  780.7 4.1 copy-start.48
  780.7 4.0 copy-start.49
  781.6 4.3 copy-start.46
  781.6 4.3 copy-start.47
  781.6 5.4 copy-start.45
  788.4 14.6 %copy-start.41 = (bf16[2,8,64,1024]{3,2,1,0:T(8,128)(2,1)S(1)}, bf16[2,8,64,1024]{3,2,1,0:T(8,128)(2,1)}, u32[]{:S(2)}) copy-start(bf16[2,8,64,1024]{3,2,1,0:T(8,128)(2,1)} %get-tuple-element.65) | copy-start | bytes 6291460
  (18 other events, 29.0 us)

commit v2 on v1

--- a/solution.py
+++ b/solution.py
@@ -451,6 +451,7 @@
 FROWS = 272
 DEN_ROW = 261
 TOP_ROW = 263
+GAIN_LANE = 264
 
 
 def place():
@@ -484,128 +485,6 @@
     return pltpu.CompilerParams(
         collective_id=collective_id, has_side_effects=True, vmem_limit_bytes=vmem
     )
-
-
-def gather_kernel(splits, *refs):
-    count = len(splits)
-    shards, cot = refs[:count], refs[count]
-    wholes, cot_rows = refs[count + 1 : 2 * count + 1], refs[2 * count + 1]
-    send, recv, local, cot_send, cot_recv = refs[2 * count + 2 :]
-    x, c, z, y = place()
-    pix = lax.axis_index("pix")
-    sems = (send, recv)
-    others = [(pix + i) % 8 for i in range(1, 8)]
-    core, across, beside = device(x, 1 - c, z, y), device(1 - x, c, z, y), device(x, c, z, 1 - y)
-    greet([{"dp": x * 2 + c, "pix": other} for other in others] + [core, across])
-
-    def part(ref, split):
-        return ref.at[x, c] if split else ref.at[:, c]
-
-    locals_ = []
-    for k in range(count):
-        copy = pltpu.make_async_copy(shards[k], wholes[k].at[z, y], local.at[k])
-        copy.start()
-        locals_.append(copy)
-    copy = pltpu.make_async_copy(cot.at[:, pix], cot_rows.at[:, pix], local.at[count])
-    copy.start()
-    locals_.append(copy)
-    along, side, over, between = {}, {}, {}, {}
-    for k in range(count):
-        mine, home = part(shards[k], splits[k]), part(wholes[k].at[z, y], splits[k])
-        for i in (1, 2, 3):
-            along[k, i] = remote(mine, home, sems, (k, i - 1), device(x, c, (z + i) % 4, y))
-            along[k, i].start()
-        side[k, 0] = remote(mine, home, sems, (k, 3), beside)
-        side[k, 0].start()
-    cots = []
-    for i, other in enumerate(others):
-        copy = remote(
-            cot.at[:, other],
-            cot_rows.at[:, pix],
-            (cot_send, cot_recv),
-            i,
-            {"dp": x * 2 + c, "pix": other},
-        )
-        copy.start()
-        cots.append(copy)
-
-    def to_side(k):
-        for i in (1, 2, 3):
-            along[k, i].wait_recv()
-            block = part(wholes[k].at[(z + 4 - i) % 4, y], splits[k])
-            side[k, i] = remote(block, block, sems, (k, 3 + i), beside)
-            side[k, i].start()
-
-    def over_part(k, i):
-        if i == 0:
-            return wholes[k].at[z, 1 - y, x, c]
-        return wholes[k].at[(z + 4 - i) % 4, :, x, c]
-
-    def core_part(k, i):
-        if i == 0:
-            return wholes[k].at[z, 1 - y, :, c]
-        return wholes[k].at[(z + 4 - i) % 4, :, :, c]
-
-    def to_over(k):
-        for i in range(4):
-            side[k, i].wait_recv()
-            if splits[k]:
-                over[k, i] = remote(
-                    over_part(k, i), over_part(k, i), sems, (k, 7 + i), across
-                )
-                over[k, i].start()
-
-    def to_core(k):
-        for i in range(4):
-            if splits[k]:
-                over[k, i].wait_recv()
-            between[k, i] = remote(core_part(k, i), core_part(k, i), sems, (k, 11 + i), core)
-            between[k, i].start()
-
-    for step in range(count + 2):
-        if step < count:
-            to_side(step)
-        if 1 <= step <= count:
-            to_over(step - 1)
-        if step >= 2:
-            to_core(step - 2)
-    for copy in locals_:
-        copy.wait()
-    for copy in cots:
-        copy.wait()
-    for copy in between.values():
-        copy.wait()
-    for group in (along, side, over):
-        for copy in group.values():
-            copy.wait_send()
-
-
-def gather_weights(shards, splits, cot):
-    count = len(shards)
-    views = [
-        shard.reshape(2, 2, shard.shape[0] // 4, shard.shape[1]) for shard in shards
-    ]
-    outs = [jax.ShapeDtypeStruct((4, 2, *view.shape), view.dtype) for view in views]
-    results = pl.pallas_call(
-        functools.partial(gather_kernel, splits),
-        out_shape=[*outs, jax.ShapeDtypeStruct(cot.shape, cot.dtype)],
-        in_specs=[HBM] * (count + 1),
-        out_specs=[HBM] * (count + 1),
-        scratch_shapes=[
-            pltpu.SemaphoreType.DMA((count, 15)),
-            pltpu.SemaphoreType.DMA((count, 15)),
-            pltpu.SemaphoreType.DMA((count + 1,)),
-            pltpu.SemaphoreType.DMA((7,)),
-            pltpu.SemaphoreType.DMA((7,)),
-        ],
-        compiler_params=remote_params(0),
-        name="gather_weights",
-    )(*views, cot)
-    wholes = [
-        whole.reshape(8 * shard.shape[0], shard.shape[1])
-        for whole, shard in zip(results[:-1], shards, strict=True)
-    ]
-    return wholes, results[-1]
 
 
 def normed_block(raw, gain, wide_ref):
@@ -647,87 +526,354 @@
     return den, top
 
 
-def pixel_forward_kernel(
-    segs, pixels, gain, queries, weights, tops, sums, wide_ref, total, largest
-):
-    micro, block = pl.program_id(0), pl.program_id(1)
-    pieces = BLOCK // PIECE
-    per_micro = pieces * pl.num_programs(1)
-    images = total.shape[0]
-
-    @pl.when(block == 0)
-    def _():
+def merge(pieces):
+    bodies = [piece[: FROWS - 16].astype(jnp.float32) for piece in pieces]
+    tails = [piece[FROWS - 16 :].astype(jnp.float32) for piece in pieces]
+    read = [read_rows(tail) for tail in tails]
+    top = functools.reduce(jnp.maximum, [row for unused, row in read])
+    factors = [jnp.exp(row - top) for unused, row in read]
+    body = sum(values * factor for values, factor in zip(bodies, factors, strict=True))
+    tail = sum(values * factor for values, factor in zip(tails, factors, strict=True))
+    den = sum(row * factor for (row, unused), factor in zip(read, factors, strict=True))
+    return body, tail, den, top
+
+
+class Gather:
+    def __init__(self, shards, wholes, splits, send, recv, local):
+        self.shards, self.wholes, self.splits = shards, wholes, splits
+        self.sems, self.local = (send, recv), local
+        self.place = place()
+        x, c, z, y = self.place
+        self.core, self.across = device(x, 1 - c, z, y), device(1 - x, c, z, y)
+        self.beside = device(x, c, z, 1 - y)
+        self.along, self.side, self.over, self.between, self.keep = {}, {}, {}, {}, {}
+
+    def part(self, k, ref):
+        x, c, z, y = self.place
+        return ref.at[x, c] if self.splits[k] else ref.at[:, c]
+
+    def start(self, k):
+        x, c, z, y = self.place
+        mine, home = self.part(k, self.shards[k]), self.part(k, self.wholes[k].at[z, y])
+        for i in (1, 2, 3):
+            target = device(x, c, (z + i) % 4, y)
+            self.along[k, i] = remote(mine, home, self.sems, (k, i - 1), target)
+            self.along[k, i].start()
+        self.side[k, 0] = remote(mine, home, self.sems, (k, 3), self.beside)
+        self.side[k, 0].start()
+        self.keep[k] = pltpu.make_async_copy(
+            self.shards[k], self.wholes[k].at[z, y], self.local.at[k]
+        )
+        self.keep[k].start()
+
+    def to_side(self, k):
+        x, c, z, y = self.place
+        for i in (1, 2, 3):
+            self.along[k, i].wait_recv()
+            block = self.part(k, self.wholes[k].at[(z + 4 - i) % 4, y])
+            self.side[k, i] = remote(block, block, self.sems, (k, 3 + i), self.beside)
+            self.side[k, i].start()
+
+    def to_over(self, k):
+        x, c, z, y = self.place
+        for i in range(4):
+            self.side[k, i].wait_recv()
+            if self.splits[k]:
+                if i == 0:
+                    block = self.wholes[k].at[z, 1 - y, x, c]
+                else:
+                    block = self.wholes[k].at[(z + 4 - i) % 4, :, x, c]
+                self.over[k, i] = remote(block, block, self.sems, (k, 7 + i), self.across)
+                self.over[k, i].start()
+
+    def to_core(self, k):
+        x, c, z, y = self.place
+        for i in range(4):
+            if self.splits[k]:
+                self.over[k, i].wait_recv()
+            if i == 0:
+                block = self.wholes[k].at[z, 1 - y, :, c]
+            else:
+                block = self.wholes[k].at[(z + 4 - i) % 4, :, :, c]
+            self.between[k, i] = remote(block, block, self.sems, (k, 11 + i), self.core)
+            self.between[k, i].start()
+
+    def arrive(self, k):
+        self.keep[k].wait()
+        for i in range(4):
+            self.between[k, i].wait_recv()
+
+    def finish(self):
+        for group in (self.along, self.side, self.over, self.between):
+            for copy in group.values():
+                copy.wait_send()
+
+
+def opening_kernel(splits, scale, *refs):
+    count = len(splits)
+    same, last = refs[:2]
+    shards, cot, pixels, pix_gain = refs[2 : count + 2], *refs[count + 2 : count + 5]
+    refs = refs[count + 5 :]
+    wholes, cot_rows, weights_out = refs[:count], refs[count], refs[count + 1]
+    normed_out, queries_out, query_out, tops, means, rows_out = refs[count + 2 : count + 8]
+    refs = refs[count + 8 :]
+    raw, wide, weights, scores_ref, lat, wq, key, total, largest, pieces, sums = refs[:11]
+    side_in, own, along_in = refs[11:14]
+    send, recv, local, cot_send, cot_recv, own_send, own_recv, load = refs[14:]
+    x, c, z, y = place()
+    dp, pix = lax.axis_index("dp"), lax.axis_index("pix")
+    micros, slots, features = pixels.shape
+    blocks = slots // BLOCK
+    per_block = BLOCK // PIECE
+    images = sums.shape[1]
+    others = [{"dp": dp, "pix": (pix + i) % 8} for i in range(1, 8)]
+    gather = Gather(shards, wholes, splits, send, recv, local)
+    greet([*others, gather.core, gather.across])
+
+    fetch = pltpu.make_async_copy(pixels, raw, load.at[0])
+    fetch.start()
+    for k in range(count):
+        gather.start(k)
+    gain = pix_gain[...]
+
+    def norm(start, stop):
+        def one(i, carry):
+            rows = pl.ds(pl.multiple_of((i % blocks) * BLOCK, BLOCK), BLOCK)
+            normed_block(raw[i // blocks, rows, :], gain, wide.at[i // blocks, rows])
+            return carry
+
+        lax.fori_loop(start, stop, one, 0)
+
+    fetch.wait()
+    norm(0, 2)
+    for k in range(3):
+        gather.to_side(k)
+    norm(2, 4)
+    for k in range(3):
+        gather.to_over(k)
+    norm(4, 6)
+    for k in range(3):
+        gather.to_core(k)
+    gather.to_side(3)
+    gather.to_side(4)
+    norm(6, 2 * blocks)
+    gather.to_over(3)
+    fetches = []
+    for k, target in enumerate((lat, wq, key)):
+        gather.arrive(k)
+        fetches.append(pltpu.make_async_copy(wholes[k], target, load.at[1 + k]))
+        fetches[k].start()
+    gather.to_side(5)
+    gather.to_over(4)
+    for copy in fetches:
+        copy.wait()
+
+    lat_values = lat[...].reshape(sums.shape[3], -1).astype(jnp.float32)
+    key_values = key[...].reshape(lat_values.shape[1], -1)
+    columns = key_values[:, 256:384].astype(jnp.float32).T
+    normed = layer_norm(lat_values, columns[GAIN_LANE - 256 : GAIN_LANE - 255])
+    normed_out[...] = normed.astype(jnp.bfloat16)
+    wq_values = wq[...].reshape(lat_values.shape[1], -1)
+    queries_out[...] = matmul(normed_out[...], wq_values).astype(jnp.bfloat16)
+    query_t = (
+        lax.dot_general(
+            key_values, queries_out[...], (((0,), (1,)), ((), ())),
+            preferred_element_type=jnp.float32,
+        )
+        * scale
+    )
+    rows = lax.broadcasted_iota(jnp.int32, query_t.shape, 0)
+    query_out[...] = jnp.where(rows < features, query_t, 0.0).astype(jnp.bfloat16)
+
+    gather.to_side(6)
+    gather.to_over(5)
+    gather.to_core(3)
+    gather.to_core(4)
+
+    def forward(m):
         total[...] = jnp.zeros_like(total)
         largest[...] = jnp.full(largest.shape, -big_value, jnp.float32)
 
-    normed_block(pixels[0], gain[...], wide_ref)
-    for k in range(pieces):
-        rows = pl.ds(k * PIECE, PIECE)
-        wide = wide_ref[rows, :]
-        scores = jnp.dot(wide, queries[...], preferred_element_type=jnp.float32)
-        top = jnp.max(scores, 0, keepdims=True)
-        low = jnp.exp(scores - top).astype(jnp.bfloat16)
-        weights[0, rows, :] = low
-        tops[0, k] = top
-        added = lax.dot_general(
-            wide[:, :FROWS], low, (((0,), (0,)), ((), ())), preferred_element_type=jnp.float32
-        )
-        seg = segs[micro * per_micro + block * pieces + k]
-
-        @pl.when(seg < images)
-        def _():
-            before = largest[seg, 0:1]
-            now = jnp.maximum(before, top)
-            total[seg] = total[seg] * jnp.exp(before - now) + added * jnp.exp(top - now)
-            largest[seg, 0:1] = now
-
-    @pl.when(block == pl.num_programs(1) - 1)
-    def _():
-        def finish(image, carry):
-            sums[0, image, : FROWS - 16] = total[image, : FROWS - 16].astype(jnp.bfloat16)
-            tail = total[image, FROWS - 16 :]
-            den = total[image, DEN_ROW : DEN_ROW + 1]
-            sums[0, image, FROWS - 16 :] = with_rows(tail, den, largest[image, 0:1]).astype(
+        def one(b, carry):
+            rows = pl.ds(pl.multiple_of(b * BLOCK, BLOCK), BLOCK)
+            scores_ref[...] = matmul(wide[m, rows, :], query_out[...])
+            for k in range(per_block):
+                rows = pl.ds(pl.multiple_of(b * BLOCK + k * PIECE, PIECE), PIECE)
+                scores = scores_ref[k * PIECE : (k + 1) * PIECE]
+                top = jnp.max(scores, 0, keepdims=True)
+                low = jnp.exp(scores - top).astype(jnp.bfloat16)
+                weights[m, rows, :] = low
+                piece = b * per_block + k
+                tops[m, piece] = top
+                added = left_matmul(wide[m, rows, :FROWS], low)
+                before = jnp.where(
+                    same[m * blocks * per_block + piece] > 0, largest[...], -big_value
+                )
+                now = jnp.maximum(before, top)
+                largest[...] = now
+                older, newer = jnp.exp(before - now), jnp.exp(top - now)
+                summed = total[...] * older + added * newer
+                total[...] = summed
+                pieces[piece, : FROWS - 16] = summed[: FROWS - 16].astype(jnp.bfloat16)
+                at = DEN_ROW - (FROWS - 16)
+                tail = summed[FROWS - 16 :]
+                pieces[piece, FROWS - 16 :] = with_rows(tail, tail[at : at + 1], now).astype(
+                    jnp.bfloat16
+                )
+            return carry
+
+        lax.fori_loop(0, blocks, one, 0)
+        for image in range(images):
+            index = last[m * images + image]
+            present = index >= 0
+            piece = pieces[jnp.maximum(index, 0)].astype(jnp.float32)
+            sums[m, image, : FROWS - 16] = jnp.where(present, piece[: FROWS - 16], 0.0).astype(
                 jnp.bfloat16
             )
-            return carry
-
-        lax.fori_loop(0, images, finish, 0)
-
-
-def pixel_forward(segs, pixels, gain, queries, images):
+            nothing = jnp.zeros((1, piece.shape[1]), jnp.float32)
+            absent = with_rows(
+                jnp.zeros((16, piece.shape[1]), jnp.float32), nothing, nothing - big_value
+            )
+            sums[m, image, FROWS - 16 :] = jnp.where(
+                present, piece[FROWS - 16 :], absent
+            ).astype(jnp.bfloat16)
+
+    own_sems = (own_send, own_recv)
+    sides, alongs, keeps = {}, {}, []
+
+    def send_sums(m):
+        for i in (1, 2, 3, 0):
+            source = sums.at[m, ((z + i) % 4) * 2 + 1 - y]
+            sides[m, i] = remote(source, side_in.at[m, i], own_sems, (m, i), gather.beside)
+            sides[m, i].start()
+        keeps.append(pltpu.make_async_copy(weights.at[m], weights_out.at[m], load.at[4 + m]))
+        keeps[-1].start()
+
+    def pass_sums(m):
+        for i in (1, 2, 3, 0):
+            sides[m, i].wait_recv()
+            body, tail, den, top = merge([sums[m, ((z + i) % 4) * 2 + y], side_in[m, i]])
+            own[m, i, : FROWS - 16] = body.astype(jnp.bfloat16)
+            own[m, i, FROWS - 16 :] = with_rows(tail, den, top).astype(jnp.bfloat16)
+            if i:
+                target = device(x, c, (z + i) % 4, y)
+                alongs[m, i] = remote(
+                    own.at[m, i], along_in.at[m, i - 1], own_sems, (m, 3 + i), target
+                )
+                alongs[m, i].start()
+
+    def finish_sums(m):
+        for i in (1, 2, 3):
+            alongs[m, i].wait_recv()
+        body, tail, den, top = merge([own[m, 0]] + [along_in[m, i] for i in range(3)])
+        rows = lax.broadcasted_iota(jnp.int32, tail.shape, 0) + (FROWS - 16)
+        means[m, : FROWS - 16] = (body / den).astype(jnp.bfloat16)
+        means[m, FROWS - 16 :] = jnp.where(rows < DEN_ROW, tail / den, 0.0).astype(jnp.bfloat16)
+        rows_out[m, 0:1] = den
+        rows_out[m, 1:2] = top
+
+    forward(0)
+    send_sums(0)
+    gather.to_side(7)
+    gather.to_over(6)
+    gather.to_core(5)
+    forward(1)
+    send_sums(1)
+    pass_sums(0)
+    gather.to_side(8)
+    gather.to_over(7)
+    gather.to_core(6)
+    pass_sums(1)
+    cots = [pltpu.make_async_copy(cot.at[:, pix], cot_rows.at[:, pix], local.at[count])]
+    for i, other in enumerate(others):
+        cots.append(
+            remote(
+                cot.at[:, (pix + i + 1) % 8],
+                cot_rows.at[:, pix],
+                (cot_send, cot_recv),
+                i,
+                other,
+            )
+        )
+    for copy in cots:
+        copy.start()
+    gather.to_side(9)
+    gather.to_side(10)
+    gather.to_over(8)
+    gather.to_core(7)
+    gather.to_over(9)
+    finish_sums(0)
+    gather.to_over(10)
+    gather.to_core(8)
+    finish_sums(1)
+    gather.to_core(9)
+    gather.to_core(10)
+    for k in range(3, count):
+        gather.arrive(k)
+    for copy in (*cots, *keeps):
+        copy.wait()
+    gather.finish()
+    for copy in (*sides.values(), *alongs.values()):
+        copy.wait_send()
+
+
+def opening(same, last, shards, splits, cot, pixels, gain, scale):
+    count = len(shards)
+    bf16, f32 = jnp.bfloat16, jnp.float32
     micros, slots, features = pixels.shape
-    latents = queries.shape[1]
-    blocks = slots // BLOCK
-    return pl.pallas_call(
-        pixel_forward_kernel,
-        grid_spec=pltpu.PrefetchScalarGridSpec(
-            num_scalar_prefetch=1,
-            grid=(micros, blocks),
-            in_specs=[
-                pl.BlockSpec((1, BLOCK, features), lambda m, b, s: (m, b, 0)),
-                pl.BlockSpec((1, features), lambda m, b, s: (0, 0)),
-                pl.BlockSpec(queries.shape, lambda m, b, s: (0, 0)),
-            ],
-            out_specs=[
-                pl.BlockSpec((1, BLOCK, latents), lambda m, b, s: (m, b, 0)),
-                pl.BlockSpec((1, BLOCK // PIECE, 1, latents), lambda m, b, s: (m, b, 0, 0)),
-                pl.BlockSpec((1, images, FROWS, latents), lambda m, b, s: (m, 0, 0, 0)),
-            ],
-            scratch_shapes=[
-                pltpu.VMEM((BLOCK, queries.shape[0]), jnp.bfloat16),
-                pltpu.VMEM((images, FROWS, latents), jnp.float32),
-                pltpu.VMEM((images, 8, latents), jnp.float32),
-            ],
-        ),
+    latents, width = 8 * shards[0].shape[0], shards[0].shape[1]
+    images = cot.shape[1]
+    views = [shard.reshape(2, 2, shard.shape[0] // 4, shard.shape[1]) for shard in shards]
+    outs = [jax.ShapeDtypeStruct((4, 2, *view.shape), view.dtype) for view in views]
+    piece = (FROWS, latents)
+    smem = pl.BlockSpec(memory_space=pltpu.SMEM)
+    results = pl.pallas_call(
+        functools.partial(opening_kernel, splits, scale),
         out_shape=[
-            jax.ShapeDtypeStruct((micros, slots, latents), jnp.bfloat16),
-            jax.ShapeDtypeStruct((micros, slots // PIECE, 1, latents), jnp.float32),
-            jax.ShapeDtypeStruct((micros, images, FROWS, latents), jnp.bfloat16),
+            *outs,
+            jax.ShapeDtypeStruct(cot.shape, cot.dtype),
+            jax.ShapeDtypeStruct((micros, slots, latents), bf16),
+            jax.ShapeDtypeStruct((latents, width), bf16),
+            jax.ShapeDtypeStruct((latents, width), bf16),
+            jax.ShapeDtypeStruct((384, latents), bf16),
+            jax.ShapeDtypeStruct((micros, slots // PIECE, 1, latents), f32),
+            jax.ShapeDtypeStruct((micros, *piece), bf16),
+            jax.ShapeDtypeStruct((micros, 2, latents), f32),
         ],
-        compiler_params=pltpu.CompilerParams(vmem_limit_bytes=48 * MIB),
-        name="pixel_forward",
-    )(segs, pixels, gain, queries)
+        in_specs=[smem, smem] + [HBM] * (count + 2) + [VMEM],
+        out_specs=[HBM] * (count + 2) + [VMEM] * 6,
+        scratch_shapes=[
+            pltpu.VMEM(pixels.shape, bf16),
+            pltpu.VMEM((micros, slots, 384), bf16),
+            pltpu.VMEM((micros, slots, latents), bf16),
+            pltpu.VMEM((BLOCK, latents), f32),
+            pltpu.VMEM(outs[0].shape, bf16),
+            pltpu.VMEM(outs[1].shape, bf16),
+            pltpu.VMEM(outs[2].shape, bf16),
+            pltpu.VMEM(piece, f32),
+            pltpu.VMEM((1, latents), f32),
+            pltpu.VMEM((slots // PIECE, *piece), bf16),
+            pltpu.VMEM((micros, images, *piece), bf16),
+            pltpu.VMEM((micros, 4, *piece), bf16),
+            pltpu.VMEM((micros, 4, *piece), bf16),
+            pltpu.VMEM((micros, 3, *piece), bf16),
+            pltpu.SemaphoreType.DMA((count, 15)),
+            pltpu.SemaphoreType.DMA((count, 15)),
+            pltpu.SemaphoreType.DMA((count + 1,)),
+            pltpu.SemaphoreType.DMA((7,)),
+            pltpu.SemaphoreType.DMA((7,)),
+            pltpu.SemaphoreType.DMA((micros, 7)),
+            pltpu.SemaphoreType.DMA((micros, 7)),
+            pltpu.SemaphoreType.DMA((4 + micros,)),
+        ],
+        compiler_params=remote_params(0, 60 * MIB),
+        name="opening",
+    )(same, last, *views, cot, pixels, gain)
+    wholes = [
+        whole.reshape(8 * shard.shape[0], shard.shape[1])
+        for whole, shard in zip(results[:count], shards, strict=True)
+    ]
+    return wholes, results[count:]
 
 
 def pixel_backward_kernel(
@@ -827,81 +973,6 @@
         compiler_params=pltpu.CompilerParams(vmem_limit_bytes=48 * MIB),
         name="pixel_backward",
     )(segs, pixels, gain, queries, weights, tops, grads)
-
-
-def merge(pieces):
-    bodies = [piece[: FROWS - 16].astype(jnp.float32) for piece in pieces]
-    tails = [piece[FROWS - 16 :].astype(jnp.float32) for piece in pieces]
-    read = [read_rows(tail) for tail in tails]
-    top = functools.reduce(jnp.maximum, [row for unused, row in read])
-    factors = [jnp.exp(row - top) for unused, row in read]
-    body = sum(values * factor for values, factor in zip(bodies, factors, strict=True))
-    tail = sum(values * factor for values, factor in zip(tails, factors, strict=True))
-    den = sum(row * factor for (row, unused), factor in zip(read, factors, strict=True))
-    return body, tail, den, top
-
-
-def owner_kernel(sums, out, rows_out, own, side_in, along_in, send, recv, local):
-    x, c, z, y = place()
-    sems = (send, recv)
-    micros = out.shape[0]
-    beside = device(x, c, z, 1 - y)
-    greet([device(x, c, (z + i) % 4, y) for i in (1, 2, 3)] + [beside])
-    sides, loads = {}, {}
-    for i in (1, 2, 3, 0):
-        sides[i] = remote(sums.at[:, (z + i) % 4, 1 - y], side_in.at[i], sems, i, beside)
-        sides[i].start()
-        loads[i] = pltpu.make_async_copy(sums.at[:, (z + i) % 4, y], own.at[i], local.at[i])
-        loads[i].start()
-    alongs = []
-    for i in (1, 2, 3, 0):
-        loads[i].wait()
-        sides[i].wait_recv()
-        for m in range(micros):
-            body, tail, den, top = merge([own[i, m], side_in[i, m]])
-            own[i, m, : FROWS - 16] = body.astype(jnp.bfloat16)
-            own[i, m, FROWS - 16 :] = with_rows(tail, den, top).astype(jnp.bfloat16)
-        if i:
-            copy = remote(own.at[i], along_in.at[i - 1], sems, 3 + i, device(x, c, (z + i) % 4, y))
-            copy.start()
-            alongs.append(copy)
-    for copy in alongs:
-        copy.wait_recv()
-    for m in range(micros):
-        body, tail, den, top = merge([own[0, m]] + [along_in[i, m] for i in range(3)])
-        rows = lax.broadcasted_iota(jnp.int32, tail.shape, 0) + (FROWS - 16)
-        out[m, : FROWS - 16] = (body / den).astype(jnp.bfloat16)
-        out[m, FROWS - 16 :] = jnp.where(rows < DEN_ROW, tail / den, 0.0).astype(jnp.bfloat16)
-        rows_out[m, 0:1] = den
-        rows_out[m, 1:2] = top
-    for copy in alongs:
-        copy.wait_send()
-    for copy in sides.values():
-        copy.wait_send()
-
-
-def to_owners(sums):
-    micros, images, rows, latents = sums.shape
-    views = sums.reshape(micros, 4, 2, rows, latents)
-    return pl.pallas_call(
-        owner_kernel,
-        out_shape=[
-            jax.ShapeDtypeStruct((micros, rows, latents), jnp.bfloat16),
-            jax.ShapeDtypeStruct((micros, 2, latents), jnp.float32),
-        ],
-        in_specs=[HBM],
-        out_specs=[VMEM, VMEM],
-        scratch_shapes=[
-            pltpu.VMEM((4, micros, rows, latents), jnp.bfloat16),
-            pltpu.VMEM((4, micros, rows, latents), jnp.bfloat16),
-            pltpu.VMEM((3, micros, rows, latents), jnp.bfloat16),
-            pltpu.SemaphoreType.DMA((7,)),
-            pltpu.SemaphoreType.DMA((7,)),
-            pltpu.SemaphoreType.DMA((4,)),
-        ],
-        compiler_params=remote_params(1),
-        name="to_owners",
-    )(views)
 
 
 def holder_kernel(grads, rows_in, out, packed, send, recv, local):
@@ -1243,13 +1314,12 @@
         return jnp.pad(values, ((0, 0), (0, columns - values.shape[1])))
 
     gains = jnp.stack([latent_gain, cross_mlp_gain, self_gain, self_mlp_gain], 1)
-    misc = jnp.concatenate(
-        [widen(key_weight.T, 384), widen(value_weight.T, 384), widen(gains, 256)], 1
-    )
+    gains = jnp.pad(gains, ((0, 0), (GAIN_LANE, 384 - GAIN_LANE - 4)))
     shards = (
         latent_array,
         query_weight,
-        misc,
+        widen(key_weight.T, 384) + gains,
+        widen(value_weight.T, 384),
         cross_out_weight,
         cross_mlp_in,
         cross_mlp_out,
@@ -1258,26 +1328,25 @@
         self_mlp_in,
         self_mlp_out,
     )
-    splits = (True, True, True, True, True, True, True, True, True, True)
-    wholes, cot_rows = gather_weights(shards, splits, cotangent[0])
-    lat_full, wq, misc, wo, w1c, w2c, wqkv, wos, w1s, w2s = wholes
-    key_t, value_t = misc[:, :384], misc[:, 384 : 384 + FROWS]
-    g_lat, g_cross, g_self, g_mlp = (misc[:, 768 + i].astype(f32) for i in range(4))
-    lat_f = lat_full.astype(f32)
-    normed_lat = layer_norm(lat_f, g_lat).astype(bf16)
-    queries = matmul(normed_lat, wq).astype(bf16)
-    query_t = (
-        lax.dot_general(key_t, queries, (((0,), (1,)), ((), ())), preferred_element_type=f32)
-        * cross_scale
-    ).astype(bf16)
-
+    splits = (True,) * len(shards)
     lengths = image_sides[0] * image_sides[0]
     ends = jnp.cumsum(lengths, 1)
     firsts = position * capacity + PIECE * jnp.arange(capacity // PIECE, dtype=jnp.int32)
-    segs = jnp.sum((firsts[None, :, None] >= ends[:, None, :]).astype(jnp.int32), 2).reshape(-1)
+    segs = jnp.sum((firsts[None, :, None] >= ends[:, None, :]).astype(jnp.int32), 2)
+    same = jnp.pad((segs[:, 1:] == segs[:, :-1]).astype(jnp.int32), ((0, 0), (1, 0))).reshape(-1)
+    here = segs[:, :, None] == jnp.arange(images, dtype=jnp.int32)[None, None, :]
+    order = jnp.arange(capacity // PIECE, dtype=jnp.int32)[None, :, None]
+    last = jnp.max(jnp.where(here, order, -1), 1).reshape(-1)
+    segs = segs.reshape(-1)
     gain_pix = pixel_gain.astype(f32)[None]
-    pix_weights, pix_tops, sums = pixel_forward(segs, pixels[0], gain_pix, query_t, images)
-    means, rows = to_owners(sums)
+    wholes, results = opening(
+        same, last, shards, splits, cotangent[0], pixels[0], gain_pix, cross_scale
+    )
+    lat_full, wq, key_t, value_t, wo, w1c, w2c, wqkv, wos, w1s, w2s = wholes
+    cot_rows, pix_weights, normed_lat, queries, query_t, pix_tops, means, rows = results
+    g_lat, g_cross, g_self, g_mlp = (key_t[:, GAIN_LANE + i].astype(f32) for i in range(4))
+    value_t = value_t[:, :FROWS]
+    lat_f = lat_full.astype(f32)
     den, top = rows[:, 0], rows[:, 1]
 
     att = jnp.einsum("mfr,df->mrd", means, value_t, preferred_element_type=f32)

time: 818 us -> 736 us (0.90)
  Pallas kernels: 564 us -> 487 us
    pallas_call x3 -> x1, Pallas kernels: 255 us -> 172 us  [opening(): pl.pallas_call(functools.partial(opening_kernel, splits, scale), out_shap...]
    pallas_call x1, Pallas kernels: 65.1 us -> 73.8 us  [to_holders(): pl.pallas_call(holder_kernel, out_shape=jax.ShapeDtypeStruct((micros, 4,...]
    unnamed x148 -> x119, local copies, waits for them, and re-layouts: 51 us -> 45.6 us
    dot_general x8 -> x7, matrix products: 34.6 us -> 33.7 us  [matmul(): return jnp.dot(left, right, preferred_element_type=jnp.float32)]
where the time goes in v2:
time: 736 us; the launch traced here: 725 us
  Pallas kernels  487 us (66%)
  matrix products  121 us (16%)
  local copies, waits for them, and re-layouts  75.1 us (10%)
  other arithmetic  40.4 us (5%)
    pallas_call x1, Pallas kernels, opening(): pl.pallas_call(functools.partial(opening_kernel, splits, scale), out_shap...  172 us
    pallas_call x1, Pallas kernels, reduce_grads(): pl.pallas_call(functools.partial(reduce_kernel, splits), out_shape=[jax.S...  155 us
    pallas_call x1, Pallas kernels, to_holders(): pl.pallas_call(holder_kernel, out_shape=jax.ShapeDtypeStruct((micros, 4,...  73.8 us
    unnamed x119, local copies, waits for them, and re-layouts  45.6 us
    dot_general x9, matrix products, right_matmul(): lax.dot_general(left, right, (((1,), (1,)), ((), ())), preferred_element_...  41.8 us
    dot_general x9, matrix products, left_matmul(): lax.dot_general(left, right, (((0,), (0,)), ((), ())), preferred_element_...  37.4 us
    dot_general x7, matrix products, matmul(): return jnp.dot(left, right, preferred_element_type=jnp.float32)  33.7 us
    pallas_call x1, Pallas kernels, pixel_backward(): pl.pallas_call(pixel_backward_kernel, grid_spec=pltpu.PrefetchScalarGridS...  26.9 us

profile of v2, /device:TPU:0, one launch (start us, length us, event | category | flops | bytes accessed | tf_op | source)
XLA Modules:
  0.0 724.8 jit_solution(3103024796316016610)
XLA Ops:
  7.8 11.8 %copy.87 = bf16[1,2,4096,261]{3,2,1,0:T(8,128)(2,1)} copy(bf16[1,2,4096,261]{2,1,3,0:T(2,128)(2,1)} %param.20) | data formatting | bytes 8552448 | tf_op args[1]
  19.6 172.2 %opening.1 = (bf16[4,2,2,2,16,1024]{5,4,3,2,1,0:T(8,128)(2,1)}, bf16[4,2,2,2,32,1024]{5,4,3,2,1,0:T(8,128)(2,1)}, bf16[4,2,2,2,32,384]{5,4,3,2,1,0:T(8,128)(2,1)...) custom-call(s32[32]{0:T(128)} %reshape.458.refs_0_, ...), custom_call_target="tpu_custom_call" | custom-call | tf_op jit(solution)/shard_map/opening/pallas_call | solution.py:830
  198.4 3.4 slice_convert_fusion
  201.8 1.8 copy.134
  206.3 5.2 fusion.86
  211.5 4.1 copy.99
  215.6 4.7 fusion.24
  224.0 2.3 fusion.89
  226.4 3.1 fusion.87
  230.1 9.0 %convolution_convert_fusion.1 = bf16[1024,3072]{1,0:T(8,128)(2,1)} fusion(bf16[1024,3072]{1,0:T(8,128)(2,1)S(1)} %bitcast.307, f32[1024,1024]{1,0:T(8,128)S(1)} %get-tuple-element.170, f32[1024]{0:T(1024)S(1)} %bitcast.290, f32[1024]{0:T(1024)S(1)} %fusion.70, f32[1024]{0:T(1024)S(1)} %broadcast_multiply_fusion.2), kind=kOutput, calls=%fused_computation.9 | convolution fusion | flops 6449790976 | bytes 16789504 | tf_op jit(solution)/shard_map/dot_general | solution.py:25
  239.2 15.7 %attention.1 = bf16[2,512,1024]{2,1,0:T(8,128)(2,1)S(1)} custom-call(bf16[2,512,3072]{2,1,0:T(8,128)(2,1)} %bitcast.228), custom_call_target="tpu_custom_call" | custom-call | tf_op jit(solution)/shard_map/attention/pallas_call | solution.py:1065
  254.9 2.8 copy.97
  257.7 5.3 fusion.88
  263.6 2.5 copy-done.46
  266.1 5.2 fusion.21
  271.3 3.7 convolution_convert_fusion.5.refs_0_
  275.0 5.4 copy.95
  280.4 7.5 %fusion.13 = bf16[1024,1024]{1,0:T(8,128)(2,1)S(1)} fusion(f32[1024,1024]{1,0:T(8,128)} %copy.95, bf16[1024,1024]{1,0:T(8,128)(2,1)S(1)} %bitcast.236, bf16[1024,1024]{1,0:T(8,128)(2,1)} %bitcast.313), kind=kOutput, calls=%fused_computation.23 | convolution fusion | flops 2168455168 | bytes 10485760 | tf_op jit(solution)/shard_map/dot_general | solution.py:35
  287.9 4.1 add_convert_fusion
  292.0 4.1 convolution_convert_fusion.4
  296.1 2.9 multiply_reduce_fusion.1
  299.0 1.9 fusion.84
  302.6 3.7 fusion.38.refs_2_
  306.2 2.4 fusion.90.grad
  308.6 26.4 %attention_back.1 = bf16[2,512,3072]{2,1,0:T(8,128)(2,1)} custom-call(bf16[2,512,3072]{2,1,0:T(8,128)(2,1)} %bitcast.229, f32[2,512,1024]{2,1,0:T(8,128)S(1)} %fusion.90.grad), custom_call_target="tpu_custom_call" | custom-call | tf_op jit(solution)/shard_map/attention_back/pallas_call | solution.py:1079
  335.0 11.4 %multiply_reduce_fusion.2 = (bf16[1024]{0:T(1024)(128)(2,1)S(1)}, f32[1024]{0:T(1024)S(1)}, f32[1024,1024]{1,0:T(8,128)S(1)}) fusion(f32[1024,1024]{1,0:T(8,128)S(1)} %copy-done.9, f32[1024]{0:T(1024)S(1)} %fusion.70, f32[1024]{0:T(1024)S(1)} %broadcast_multiply_fusion.2, f32[1024]{0:T(1024)S(1)} %bitcast.291, bf16[1024,3072]{1,0:T(8,128)(2,1)} %bitcast.237, ...), kind=kOutput, calls=%fused_computation.38 | convolution fusion | flops 6449788928 | bytes 20989952 | tf_op jit(solution)/shard_map/dot_general | solution.py:35
  346.4 2.1 fusion.83
  350.7 6.5 fusion.6
  357.2 4.1 convolution_convert_fusion.3
  361.3 3.8 convolution_convert_fusion.2
  365.1 2.8 multiply_reduce_fusion.3
  369.3 3.2 fusion.81
  372.5 3.9 reduce_sum.230
  376.4 2.2 reshape.445
  379.8 6.0 multiply_reduce_fusion
  388.2 3.6 fusion.41.refs_6_
  393.3 2.3 copy.127
  395.5 2.1 pad.45.clone
  397.9 3.1 pad_maximum_fusion.refs_7_
  401.0 2.6 copy.98
  403.6 11.2 %convolution_convert_fusion.refs_3_ = bf16[4,2,2,2,32,3072]{5,4,3,2,1,0:T(8,128)(2,1)} fusion(bf16[4,2,2,2,32,1024]{5,4,3,2,1,0:T(8,128)(2,1)} %bitcast.257, bf16[1024,3072,1,1,1,1]{1,0,5,4,3,2:T(8,128)(2,1)} %bitcast.238), kind=kOutput, calls=%fused_computation.8 | convolution fusion | flops 6445596672 | bytes 14680064 | tf_op jit(solution)/shard_map/dot_general | solution.py:29
  414.8 73.8 %to_holders.1 = bf16[2,4,2,272,512]{4,3,2,1,0:T(8,128)(2,1)S(1)} custom-call(f32[2,272,512]{2,1,0:T(8,128)S(1)} %fusion.48.grads, f32[2,2,512]{2,1,0:T(2,128)S(1)} %pad_maximum_fusion.2.rows_in), custom_call_target="tpu_custom_call" | custom-call | tf_op jit(solution)/shard_map/to_holders/pallas_call | solution.py:1014
  488.6 26.9 %pixel_backward.1 = (f32[2,4096,261]{2,1,0:T(8,128)}, f32[272,512]{1,0:T(8,128)S(1)}, f32[1,261]{1,0:T(1,128)S(1)}) custom-call(s32[32]{0:T(128)S(1)} %reshape.446.segs, bf16[2,4096,261]{2,1,0:T(8,128)(2,1)} %bitcast.227, f32[1,261]{1,0:T(1,128)S(1)} %copy-done.3, bf16[384,512]{1,0:T(8,128)(2,1)S(1)} %copy-done, ...), custom_call_target="tpu_custom_call" | custom-call | tf_op jit(solution)/shard_map/pixel_backward/pallas_call | solution.py:944
  516.8 155.3 %reduce_grads.1 = (bf16[2,2,32,1024]{3,2,1,0:T(8,128)(2,1)}, bf16[2,2,32,1024]{3,2,1,0:T(8,128)(2,1)}, bf16[2,2,32,1024]{3,2,1,0:T(8,128)(2,1)}, bf16[2,2,32,307...) custom-call(bf16[4,2,2,2,32,1024]{5,4,3,2,1,0:T(8,128)(2,1)} %convol, ...), custom_call_target="tpu_custom_call" | custom-call | tf_op jit(solution)/shard_map/reduce_grads/pallas_call | solution.py:1232
  678.2 16.4 %spread.1 = bf16[8,128,384]{2,1,0:T(8,128)(2,1)S(1)} custom-call(bf16[128,384]{1,0:T(8,128)(2,1)S(1)} %bitcast.225), custom_call_target="tpu_custom_call" | custom-call | tf_op jit(solution)/shard_map/spread/pallas_call | solution.py:1271
  697.2 2.0 fusion.63
  699.3 1.7 multiply_reduce_fusion.10
  708.7 14.6 %copy.111 = f32[1,2,4096,261]{2,1,3,0:T(2,128)} copy(f32[1,2,4096,261]{3,2,1,0:T(8,128)} %bitcast.234) | data formatting | bytes 17104896
  (194 shorter events, 50.5 us)
Async XLA Ops:
  196.9 9.4 %copy-start.18 = (bf16[2,272,512]{2,1,0:T(8,128)(2,1)S(1)}, bf16[2,272,512]{2,1,0:T(8,128)(2,1)}, u32[]{:S(2)}) copy-start(bf16[2,272,512]{2,1,0:T(8,128)(2,1)} %get-tuple-element.51) | copy-start | bytes 1671172
  198.4 27.9 %copy-start.6 = (f32[512,1024]{1,0:T(8,128)}, f32[512,1024]{1,0:T(8,128)S(1)}, u32[]{:S(2)}) copy-start(f32[512,1024]{1,0:T(8,128)S(1)} %convert.98) | copy-start | bytes 6291460
  220.2 6.1 copy-start.4
  221.1 2.9 copy-start.20
  224.0 2.4 copy-start.22
  224.0 6.1 slice-start
  226.4 3.2 copy-start.15
  226.4 3.8 slice-start.1
  229.5 9.7 %copy-start.8 = (f32[1024,1024]{1,0:T(8,128)}, f32[1024,1024]{1,0:T(8,128)S(1)}, u32[]{:S(2)}) copy-start(f32[1024,1024]{1,0:T(8,128)S(1)} %get-tuple-element.170) | copy-start | bytes 12582916
  263.0 8.3 %copy-start.10 = (f32[1024,1024]{1,0:T(8,128)}, f32[1024,1024]{1,0:T(8,128)S(1)}, u32[]{:S(2)}) copy-start(f32[1024,1024]{1,0:T(8,128)S(1)} %get-tuple-element.172) | copy-start | bytes 12582916
  263.0 3.1 copy-start.46
  266.1 5.2 copy-start.13
  280.4 7.5 %copy-start.11 = (f32[1024,1024]{1,0:T(8,128)S(1)}, f32[1024,1024]{1,0:T(8,128)}, u32[]{:S(2)}) copy-start(f32[1024,1024]{1,0:T(8,128)} %copy-done.10) | copy-start | bytes 12582916
  280.4 7.5 %copy-start.17 = (f32[1024,1024]{1,0:T(8,128)S(1)}, f32[1024,1024]{1,0:T(8,128)}, u32[]{:S(2)}) copy-start(f32[1024,1024]{1,0:T(8,128)} %copy.95) | copy-start | bytes 12582916
  280.4 7.5 %copy-start.48 = (bf16[4,2,2,2,32,1024]{5,4,3,2,1,0:T(8,128)(2,1)S(1)}, bf16[4,2,2,2,32,1024]{5,4,3,2,1,0:T(8,128)(2,1)}, u32[]{:S(2)}) copy-start(bf16[4,2,2,2,32,1024]{5,4,3,2,1,0:T(8,128)(2,1)} %get-tuple-element.61) | copy-start | bytes 6291460
  292.0 4.1 copy-start.47
  301.0 1.6 copy-start.27
  302.6 3.7 copy-start.45
  308.6 26.4 %copy-start.9 = (f32[1024,1024]{1,0:T(8,128)S(1)}, f32[1024,1024]{1,0:T(8,128)}, u32[]{:S(2)}) copy-start(f32[1024,1024]{1,0:T(8,128)} %copy-done.8) | copy-start | bytes 12582916
  346.4 2.1 copy-start.14
  348.5 2.2 copy-start.16
  357.2 4.1 copy-start.24
  361.3 3.8 copy-start.5
  361.3 3.8 copy-start.7
  361.3 3.8 copy-start.21
  379.8 6.0 copy-start.19
  385.7 1.6 copy-start.25
  385.7 2.4 copy-start.28
  388.2 3.6 copy-start.43
  388.2 3.7 copy-start.30
  414.8 73.8 %copy-start = (bf16[384,512]{1,0:T(8,128)(2,1)S(1)}, bf16[384,512]{1,0:T(8,128)(2,1)}, u32[]{:S(2)}) copy-start(bf16[384,512]{1,0:T(8,128)(2,1)} %get-tuple-element.62.queries) | copy-start | bytes 1179652
  414.8 73.8 %copy-start.2 = (f32[2,16,1,512]{3,2,1,0:T(1,128)S(1)}, f32[2,16,1,512]{3,2,1,0:T(1,128)}, u32[]{:S(2)}) copy-start(f32[2,16,1,512]{3,2,1,0:T(1,128)} %get-tuple-element.64.tops) | copy-start | bytes 196612
  414.8 73.8 %copy-start.3 = (f32[1,261]{1,0:T(1,128)S(1)}, f32[1,261]{1,0:T(1,128)}, u32[]{:S(2)}) copy-start(f32[1,261]{1,0:T(1,128)} %reshape.459.refs_15_.gain) | copy-start | bytes 3136
  672.1 24.4 %copy-start.29 = (bf16[4,2,2,2,32,384]{5,4,3,2,1,0:T(8,128)(2,1)S(1)}, bf16[4,2,2,2,32,384]{5,4,3,2,1,0:T(8,128)(2,1)}, u32[]{:S(2)}) copy-start(bf16[4,2,2,2,32,384]{5,4,3,2,1,0:T(8,128)(2,1)} %get-tuple-element.54) | copy-start | bytes 2359300
  673.1 26.2 %copy-start.12 = (bf16[4,2,2,2,16,1024]{5,4,3,2,1,0:T(8,128)(2,1)S(1)}, bf16[4,2,2,2,16,1024]{5,4,3,2,1,0:T(8,128)(2,1)}, u32[]{:S(2)}) copy-start(bf16[4,2,2,2,16,1024]{5,4,3,2,1,0:T(8,128)(2,1)} %get-tuple-element.50) | copy-start | bytes 3145732
  673.1 26.2 %copy-start.40 = (f32[1024,1]{0,1:T(1,128)S(1)}, f32[1024,1]{0,1:T(1,128)}, u32[]{:S(2)}) copy-start(f32[1024,1]{0,1:T(1,128)} %copy.134) | copy-start | bytes 12292
  673.1 26.2 %copy-start.41 = (f32[512]{0:T(512)S(1)}, f32[512]{0:T(512)}, u32[]{:S(2)}) copy-start(f32[512]{0:T(512)} %div.115) | copy-start | bytes 6148
  673.1 26.2 %copy-start.42 = (f32[512]{0:T(512)S(1)}, f32[512]{0:T(512)}, u32[]{:S(2)}) copy-start(f32[512]{0:T(512)} %rsqrt.46) | copy-start | bytes 6148
  678.2 21.1 %copy-start.44 = (bf16[4,2,2,2,32,1024]{5,4,3,2,1,0:T(8,128)(2,1)S(1)}, bf16[4,2,2,2,32,1024]{5,4,3,2,1,0:T(8,128)(2,1)}, u32[]{:S(2)}) copy-start(bf16[4,2,2,2,32,1024]{5,4,3,2,1,0:T(8,128)(2,1)} %get-tuple-element.72) | copy-start | bytes 6291460
  699.3 3.0 copy-start.39
  701.0 3.0 copy-start.36
  701.0 3.0 copy-start.37
  701.0 4.1 copy-start.34
  701.0 4.1 copy-start.35
  702.3 3.9 copy-start.32
  702.3 3.9 copy-start.33
  702.3 5.0 copy-start.31
  708.7 14.6 %copy-start.26 = (bf16[2,8,64,1024]{3,2,1,0:T(8,128)(2,1)S(1)}, bf16[2,8,64,1024]{3,2,1,0:T(8,128)(2,1)}, u32[]{:S(2)}) copy-start(bf16[2,8,64,1024]{3,2,1,0:T(8,128)(2,1)} %get-tuple-element.68) | copy-start | bytes 6291460
  (3 other events, 2.8 us)

commit v3 on v2

--- a/solution.py
+++ b/solution.py
@@ -452,6 +452,7 @@
 DEN_ROW = 261
 TOP_ROW = 263
 GAIN_LANE = 264
+GAIN_ROW = 262
 
 
 def place():
@@ -487,17 +488,15 @@
     )
 
 
-def normed_block(raw, gain, wide_ref):
-    features = raw.shape[1]
+def normed_block(raw, gain, features):
     values = raw.astype(jnp.float32)
-    average = jnp.sum(values, 1, keepdims=True) * (1.0 / features)
-    centered = values - average
-    scale = lax.rsqrt(jnp.sum(centered * centered, 1, keepdims=True) * (1.0 / features) + 1e-05)
+    rows = lax.broadcasted_iota(jnp.int32, values.shape, 0)
+    average = jnp.sum(values, 0, keepdims=True) * (1.0 / features)
+    centered = jnp.where(rows < features, values - average, 0.0)
+    scale = lax.rsqrt(jnp.sum(centered * centered, 0, keepdims=True) * (1.0 / features) + 1e-05)
     unit = centered * scale
-    lanes = lax.broadcasted_iota(jnp.int32, wide_ref.shape, 1)
-    wide_ref[...] = jnp.where(lanes == DEN_ROW, 1.0, 0.0).astype(jnp.bfloat16)
-    wide_ref[:, :features] = (unit * gain).astype(jnp.bfloat16)
-    return unit, scale
+    wide = jnp.where(rows == DEN_ROW, 1.0, unit * gain)
+    return wide.astype(jnp.bfloat16), unit, scale
 
 
 def three_parts(row):
@@ -609,28 +608,27 @@
                 copy.wait_send()
 
 
-def opening_kernel(splits, scale, *refs):
+def opening_kernel(splits, scale, features, *refs):
     count = len(splits)
     same, last = refs[:2]
-    shards, cot, pixels, pix_gain = refs[2 : count + 2], *refs[count + 2 : count + 5]
-    refs = refs[count + 5 :]
-    wholes, cot_rows, weights_out = refs[:count], refs[count], refs[count + 1]
-    normed_out, queries_out, query_out, tops, means, rows_out = refs[count + 2 : count + 8]
-    refs = refs[count + 8 :]
-    raw, wide, weights, scores_ref, lat, wq, key, total, largest, pieces, sums = refs[:11]
-    side_in, own, along_in = refs[11:14]
-    send, recv, local, cot_send, cot_recv, own_send, own_recv, load = refs[14:]
+    shards, pixels, pix_gain = refs[2 : count + 2], *refs[count + 2 : count + 4]
+    refs = refs[count + 4 :]
+    wholes, weights_out = refs[:count], refs[count]
+    normed_out, queries_out, query_out, tops, means, rows_out = refs[count + 1 : count + 7]
+    refs = refs[count + 7 :]
+    wide, weights, scores_ref, lat, wq, key, total, largest, pieces, sums = refs[:10]
+    side_in, own, along_in = refs[10:13]
+    send, recv, local, own_send, own_recv, load = refs[13:]
     x, c, z, y = place()
-    dp, pix = lax.axis_index("dp"), lax.axis_index("pix")
-    micros, slots, features = pixels.shape
+    micros, unused, slots = pixels.shape
     blocks = slots // BLOCK
     per_block = BLOCK // PIECE
     images = sums.shape[1]
-    others = [{"dp": dp, "pix": (pix + i) % 8} for i in range(1, 8)]
     gather = Gather(shards, wholes, splits, send, recv, local)
-    greet([*others, gather.core, gather.across])
-
-    fetch = pltpu.make_async_copy(pixels, raw, load.at[0])
+    along = [device(x, c, (z + i) % 4, y) for i in (1, 2, 3)]
+    greet([*along, gather.beside, gather.across, gather.core])
+
+    fetch = pltpu.make_async_copy(pixels, wide, load.at[0])
     fetch.start()
     for k in range(count):
         gather.start(k)
@@ -638,11 +636,13 @@
 
     def norm(start, stop):
         def one(i, carry):
-            rows = pl.ds(pl.multiple_of((i % blocks) * BLOCK, BLOCK), BLOCK)
-            normed_block(raw[i // blocks, rows, :], gain, wide.at[i // blocks, rows])
+            half = BLOCK // 2
+            columns = pl.ds(pl.multiple_of((i % (2 * blocks)) * half, half), half)
+            micro = i // (2 * blocks)
+            wide[micro, :, columns] = normed_block(wide[micro, :, columns], gain, features)[0]
             return carry
 
-        lax.fori_loop(start, stop, one, 0)
+        lax.fori_loop(2 * start, 2 * stop, one, 0)
 
     fetch.wait()
     norm(0, 2)
@@ -682,6 +682,7 @@
         )
         * scale
     )
+    query_t = query_t[:FROWS]
     rows = lax.broadcasted_iota(jnp.int32, query_t.shape, 0)
     query_out[...] = jnp.where(rows < features, query_t, 0.0).astype(jnp.bfloat16)
 
@@ -696,7 +697,7 @@
 
         def one(b, carry):
             rows = pl.ds(pl.multiple_of(b * BLOCK, BLOCK), BLOCK)
-            scores_ref[...] = matmul(wide[m, rows, :], query_out[...])
+            scores_ref[...] = left_matmul(wide[m, :, rows], query_out[...])
             for k in range(per_block):
                 rows = pl.ds(pl.multiple_of(b * BLOCK + k * PIECE, PIECE), PIECE)
                 scores = scores_ref[k * PIECE : (k + 1) * PIECE]
@@ -705,7 +706,7 @@
                 weights[m, rows, :] = low
                 piece = b * per_block + k
                 tops[m, piece] = top
-                added = left_matmul(wide[m, rows, :FROWS], low)
+                added = matmul(wide[m, :, rows], low)
                 before = jnp.where(
                     same[m * blocks * per_block + piece] > 0, largest[...], -big_value
                 )
@@ -784,19 +785,6 @@
     gather.to_over(7)
     gather.to_core(6)
     pass_sums(1)
-    cots = [pltpu.make_async_copy(cot.at[:, pix], cot_rows.at[:, pix], local.at[count])]
-    for i, other in enumerate(others):
-        cots.append(
-            remote(
-                cot.at[:, (pix + i + 1) % 8],
-                cot_rows.at[:, pix],
-                (cot_send, cot_recv),
-                i,
-                other,
-            )
-        )
-    for copy in cots:
-        copy.start()
     gather.to_side(9)
     gather.to_side(10)
     gather.to_over(8)
@@ -810,41 +798,38 @@
     gather.to_core(10)
     for k in range(3, count):
         gather.arrive(k)
-    for copy in (*cots, *keeps):
+    for copy in keeps:
         copy.wait()
     gather.finish()
     for copy in (*sides.values(), *alongs.values()):
         copy.wait_send()
 
 
-def opening(same, last, shards, splits, cot, pixels, gain, scale):
+def opening(same, last, shards, splits, pixels, gain, features, images, scale):
     count = len(shards)
     bf16, f32 = jnp.bfloat16, jnp.float32
-    micros, slots, features = pixels.shape
+    micros, unused, slots = pixels.shape
     latents, width = 8 * shards[0].shape[0], shards[0].shape[1]
-    images = cot.shape[1]
     views = [shard.reshape(2, 2, shard.shape[0] // 4, shard.shape[1]) for shard in shards]
     outs = [jax.ShapeDtypeStruct((4, 2, *view.shape), view.dtype) for view in views]
     piece = (FROWS, latents)
     smem = pl.BlockSpec(memory_space=pltpu.SMEM)
     results = pl.pallas_call(
-        functools.partial(opening_kernel, splits, scale),
+        functools.partial(opening_kernel, splits, scale, features),
         out_shape=[
             *outs,
-            jax.ShapeDtypeStruct(cot.shape, cot.dtype),
             jax.ShapeDtypeStruct((micros, slots, latents), bf16),
             jax.ShapeDtypeStruct((latents, width), bf16),
             jax.ShapeDtypeStruct((latents, width), bf16),
-            jax.ShapeDtypeStruct((384, latents), bf16),
+            jax.ShapeDtypeStruct(piece, bf16),
             jax.ShapeDtypeStruct((micros, slots // PIECE, 1, latents), f32),
             jax.ShapeDtypeStruct((micros, *piece), bf16),
             jax.ShapeDtypeStruct((micros, 2, latents), f32),
         ],
-        in_specs=[smem, smem] + [HBM] * (count + 2) + [VMEM],
-        out_specs=[HBM] * (count + 2) + [VMEM] * 6,
+        in_specs=[smem, smem] + [HBM] * (count + 1) + [VMEM],
+        out_specs=[HBM] * (count + 1) + [VMEM] * 6,
         scratch_shapes=[
             pltpu.VMEM(pixels.shape, bf16),
-            pltpu.VMEM((micros, slots, 384), bf16),
             pltpu.VMEM((micros, slots, latents), bf16),
             pltpu.VMEM((BLOCK, latents), f32),
             pltpu.VMEM(outs[0].shape, bf16),
@@ -859,173 +844,19 @@
             pltpu.VMEM((micros, 3, *piece), bf16),
             pltpu.SemaphoreType.DMA((count, 15)),
             pltpu.SemaphoreType.DMA((count, 15)),
-            pltpu.SemaphoreType.DMA((count + 1,)),
-            pltpu.SemaphoreType.DMA((7,)),
-            pltpu.SemaphoreType.DMA((7,)),
+            pltpu.SemaphoreType.DMA((count,)),
             pltpu.SemaphoreType.DMA((micros, 7)),
             pltpu.SemaphoreType.DMA((micros, 7)),
             pltpu.SemaphoreType.DMA((4 + micros,)),
         ],
         compiler_params=remote_params(0, 60 * MIB),
         name="opening",
-    )(same, last, *views, cot, pixels, gain)
+    )(same, last, *views, pixels, gain)
     wholes = [
         whole.reshape(8 * shard.shape[0], shard.shape[1])
         for whole, shard in zip(results[:count], shards, strict=True)
     ]
     return wholes, results[count:]
-
-
-def pixel_backward_kernel(
-    segs,
-    pixels,
-    gain,
-    queries,
-    weights,
-    tops,
-    grads,
-    out,
-    query_sums,
-    gain_sums,
-    wide_ref,
-    scores_ref,
-    back_ref,
-):
-    micro, block = pl.program_id(0), pl.program_id(1)
-    pieces = BLOCK // PIECE
-    per_micro = pieces * pl.num_programs(1)
-    images = grads.shape[1]
-    features = pixels.shape[2]
-
-    @pl.when((block == 0) & (micro == 0))
-    def _():
-        query_sums[...] = jnp.zeros_like(query_sums)
-        gain_sums[...] = jnp.zeros_like(gain_sums)
-
-    unit, scale = normed_block(pixels[0], gain[...], wide_ref)
-    for k in range(pieces):
-        rows = pl.ds(k * PIECE, PIECE)
-        seg = segs[micro * per_micro + block * pieces + k]
-        image = jnp.minimum(seg, images - 1)
-        grad = grads[0, image]
-        unused, top = read_rows(grads[0, image, FROWS - 16 :].astype(jnp.float32))
-        factor = jnp.where(seg < images, jnp.exp(tops[0, k] - top), 0.0)
-        full = weights[0, rows, :].astype(jnp.float32) * factor
-        slopes = jnp.dot(
-            wide_ref[rows, :FROWS], grad, preferred_element_type=jnp.float32
-        )
-        scores_ref[rows, :] = (full * slopes).astype(jnp.bfloat16)
-        back_ref[rows, :] = lax.dot_general(
-            full.astype(jnp.bfloat16),
-            grad,
-            (((1,), (1,)), ((), ())),
-            preferred_element_type=jnp.float32,
-        )
-    scores = scores_ref[...]
-    query_sums[...] += lax.dot_general(
-        wide_ref[:, :FROWS], scores, (((0,), (0,)), ((), ())), preferred_element_type=jnp.float32
-    )
-    back = back_ref[...] + lax.dot_general(
-        scores, queries[:FROWS], (((1,), (1,)), ((), ())), preferred_element_type=jnp.float32
-    )
-    back = back[:, :features]
-    gain_sums[...] += jnp.sum(back * unit, 0, keepdims=True)
-    back = back * gain[...]
-    mean = jnp.sum(back, 1, keepdims=True) * (1.0 / features)
-    slope = jnp.sum(back * unit, 1, keepdims=True) * (1.0 / features)
-    out[0] = (back - mean - unit * slope) * scale
-
-
-def pixel_backward(segs, pixels, gain, queries, weights, tops, grads):
-    micros, slots, features = pixels.shape
-    latents = queries.shape[1]
-    blocks = slots // BLOCK
-    images = grads.shape[1]
-    return pl.pallas_call(
-        pixel_backward_kernel,
-        grid_spec=pltpu.PrefetchScalarGridSpec(
-            num_scalar_prefetch=1,
-            grid=(micros, blocks),
-            in_specs=[
-                pl.BlockSpec((1, BLOCK, features), lambda m, b, s: (m, b, 0)),
-                pl.BlockSpec((1, features), lambda m, b, s: (0, 0)),
-                pl.BlockSpec(queries.shape, lambda m, b, s: (0, 0)),
-                pl.BlockSpec((1, BLOCK, latents), lambda m, b, s: (m, b, 0)),
-                pl.BlockSpec((1, BLOCK // PIECE, 1, latents), lambda m, b, s: (m, b, 0, 0)),
-                pl.BlockSpec((1, images, FROWS, latents), lambda m, b, s: (m, 0, 0, 0)),
-            ],
-            out_specs=[
-                pl.BlockSpec((1, BLOCK, features), lambda m, b, s: (m, b, 0)),
-                pl.BlockSpec((FROWS, latents), lambda m, b, s: (0, 0)),
-                pl.BlockSpec((1, features), lambda m, b, s: (0, 0)),
-            ],
-            scratch_shapes=[
-                pltpu.VMEM((BLOCK, queries.shape[0]), jnp.bfloat16),
-                pltpu.VMEM((BLOCK, latents), jnp.bfloat16),
-                pltpu.VMEM((BLOCK, FROWS), jnp.float32),
-            ],
-        ),
-        out_shape=[
-            jax.ShapeDtypeStruct((micros, slots, features), jnp.float32),
-            jax.ShapeDtypeStruct((FROWS, latents), jnp.float32),
-            jax.ShapeDtypeStruct((1, features), jnp.float32),
-        ],
-        compiler_params=pltpu.CompilerParams(vmem_limit_bytes=48 * MIB),
-        name="pixel_backward",
-    )(segs, pixels, gain, queries, weights, tops, grads)
-
-
-def holder_kernel(grads, rows_in, out, packed, send, recv, local):
-    x, c, z, y = place()
-    sems = (send, recv)
-    micros = grads.shape[0]
-    beside = device(x, c, z, 1 - y)
-    greet([device(x, c, (z + i) % 4, y) for i in (1, 2, 3)] + [beside])
-    for m in range(micros):
-        packed[m, : FROWS - 16] = grads[m, : FROWS - 16].astype(jnp.bfloat16)
-        tail = grads[m, FROWS - 16 :]
-        rows = lax.broadcasted_iota(jnp.int32, tail.shape, 0) + (FROWS - 16)
-        tail = with_rows(tail, rows_in[m, 0:1], rows_in[m, 1:2])
-        tail = jnp.where(rows == DEN_ROW + 1, 0.0, tail)
-        packed[m, FROWS - 16 :] = tail.astype(jnp.bfloat16)
-    home = out.at[:, z, y]
-    alongs, sides = {}, {}
-    for i in (1, 2, 3):
-        alongs[i] = remote(packed, home, sems, i, device(x, c, (z + i) % 4, y))
-        alongs[i].start()
-    sides[0] = remote(packed, home, sems, 0, beside)
-    sides[0].start()
-    keep = pltpu.make_async_copy(packed, home, local)
-    keep.start()
-    for i in (1, 2, 3):
-        alongs[i].wait_recv()
-        block = out.at[:, (z + 4 - i) % 4, y]
-        sides[i] = remote(block, block, sems, 3 + i, beside)
-        sides[i].start()
-    for copy in sides.values():
-        copy.wait()
-    for copy in alongs.values():
-        copy.wait_send()
-    keep.wait()
-
-
-def to_holders(grads, rows):
-    micros, frows, latents = grads.shape
-    out = pl.pallas_call(
-        holder_kernel,
-        out_shape=jax.ShapeDtypeStruct((micros, 4, 2, frows, latents), jnp.bfloat16),
-        in_specs=[VMEM, VMEM],
-        out_specs=HBM,
-        scratch_shapes=[
-            pltpu.VMEM((micros, frows, latents), jnp.bfloat16),
-            pltpu.SemaphoreType.DMA((7,)),
-            pltpu.SemaphoreType.DMA((7,)),
-            pltpu.SemaphoreType.DMA,
-        ],
-        compiler_params=remote_params(2),
-        name="to_holders",
-    )(grads, rows)
-    return out.reshape(micros, 8, frows, latents)
 
 
 def softmax_parts(packed, scale):
@@ -1039,20 +870,6 @@
 def attention_kernel(scale, packed, out):
     query, key, value, weights, den = softmax_parts(packed[0], scale)
     out[0] = (matmul(weights.astype(jnp.bfloat16), value) / den).astype(jnp.bfloat16)
-
-
-def attention_back_kernel(scale, packed, grad, out):
-    width = grad.shape[2]
-    query, key, value, weights, den = softmax_parts(packed[0], scale)
-    grad_num = (grad[0] / den).astype(jnp.bfloat16)
-    slopes = right_matmul(grad_num, value)
-    grad_den = -jnp.sum(weights * slopes, 1, keepdims=True) / den
-    scores = (weights * (slopes + grad_den)).astype(jnp.bfloat16)
-    out[0, :, :width] = (matmul(scores, key) * scale).astype(jnp.bfloat16)
-    out[0, :, width : 2 * width] = (left_matmul(scores, query) * scale).astype(jnp.bfloat16)
-    out[0, :, 2 * width :] = left_matmul(weights.astype(jnp.bfloat16), grad_num).astype(
-        jnp.bfloat16
-    )
 
 
 def head_spec(rows, width):
@@ -1073,210 +890,720 @@
     )(packed)
 
 
-def attention_back(packed, grad, scale):
-    micros, rows, columns = packed.shape
-    width = columns // HEADS
-    return pl.pallas_call(
-        functools.partial(attention_back_kernel, scale),
-        grid=(micros, HEADS),
-        in_specs=[head_spec(rows, width), head_spec(rows, width // 3)],
-        out_specs=head_spec(rows, width),
-        out_shape=jax.ShapeDtypeStruct(packed.shape, jnp.bfloat16),
-        compiler_params=pltpu.CompilerParams(vmem_limit_bytes=48 * MIB),
-        name="attention_back",
-    )(packed, grad)
-
-
-def reduce_kernel(splits, *refs):
-    count = len(splits)
-    grads, rows_in = refs[:count], refs[count]
-    finals, rows_out = refs[count + 1 : 2 * count + 1], refs[2 * count + 1]
-    rest = refs[2 * count + 2 :]
-    own, core_in, over_in, side_in, along_in = (
-        rest[i * count : (i + 1) * count] for i in range(5)
+def normed_rows(values, gain):
+    average = jnp.mean(values, -1, keepdims=True)
+    centered = values - average
+    scale = lax.rsqrt(jnp.mean(centered * centered, -1, keepdims=True) + 1e-05)
+    return (centered * scale * gain).astype(jnp.bfloat16), scale
+
+
+def feed(inputs, gain, w_in, w_out):
+    normed, scale = normed_rows(inputs, gain)
+    hidden = matmul(normed, w_in)
+    square = hidden * hidden
+    const = (2 / jnp.pi) ** 0.5
+    bent = jnp.tanh(const * hidden * (1 + 0.044715 * square))
+    half = 0.5 * (1 + bent)
+    active = (hidden * half).astype(jnp.bfloat16)
+    slope = half + 0.5 * hidden * (1 - bent * bent) * const * (1 + 3 * 0.044715 * square)
+    return inputs + matmul(active, w_out), (scale, normed, active, slope.astype(jnp.bfloat16))
+
+
+STRIP = 256
+CHUNK = 64
+
+
+class Reduce:
+    def __init__(self, staging, own, core_in, over_in, side_in, along_in, finals, temps, sems, local):
+        self.staging, self.own = staging, own
+        self.core_in, self.over_in, self.side_in = core_in, over_in, side_in
+        self.along_in, self.finals, self.temps = along_in, finals, temps
+        self.sems, self.local = sems, local
+        self.place = place()
+        x, c, z, y = self.place
+        self.core, self.across = device(x, 1 - c, z, y), device(1 - x, c, z, y)
+        self.beside = device(x, c, z, 1 - y)
+        self.copies, self.loads, self.keeps, self.slots = {}, {}, {}, {}
+
+    def send(self, k, number, source, target, partner):
+        self.copies[k, number] = remote(source, target, self.sems, (k, number), partner)
+        self.copies[k, number].start()
+
+    def release(self, slot):
+        for k, used in self.slots.items():
+            if used == slot:
+                self.copies[k, 0].wait_send()
+                self.keeps[k].wait()
+        self.slots = {k: used for k, used in self.slots.items() if used != slot}
+
+    def push(self, k, slot):
+        x, c, z, y = self.place
+        staged = self.staging[slot]
+        rows, columns = self.own[k].shape[-2:]
+        away = staged.at[:, :, :, 1 - c, :rows, :columns]
+        self.send(k, 0, away, self.core_in[k], self.core)
+        self.keeps[k] = pltpu.make_async_copy(
+            staged.at[:, :, :, c, :rows, :columns], self.own[k], self.local.at[k, 0]
+        )
+        self.keeps[k].start()
+        self.slots[k] = slot
+
+    def c1(self, k):
+        self.copies[k, 0].wait_recv()
+        rows, columns = self.own[k].shape[-2:]
+        temp = self.temps[k][0].at[:, :, :, :rows, :columns]
+        self.loads[k] = pltpu.make_async_copy(self.core_in[k], temp, self.local.at[k, 1])
+        self.loads[k].start()
+
+    def add(self, count, one):
+        def step(i, carry):
+            one(i)
+            return carry
+
+        lax.fori_loop(0, count, step, 0)
+
+    def c2(self, k):
+        x, c, z, y = self.place
+        own, temp = self.own[k], self.temps[k][0]
+        rows, columns = own.shape[-2:]
+        if k in self.slots:
+            self.keeps[k].wait()
+            self.copies[k, 0].wait_send()
+            del self.slots[k]
+        self.loads[k].wait()
+
+        def one(i):
+            own[i // 2, i % 2] = own[i // 2, i % 2] + temp[i // 2, i % 2, :, :rows, :columns]
+
+        self.add(8, one)
+        self.send(k, 1, own.at[:, :, 1 - x], self.over_in[k], self.across)
+
+    def x1(self, k):
+        self.copies[k, 1].wait_recv()
+        rows, columns = self.own[k].shape[-2:]
+        temp = self.temps[k][1].at[:, :, :rows, :columns]
+        self.loads[k] = pltpu.make_async_copy(self.over_in[k], temp, self.local.at[k, 2])
+        self.loads[k].start()
+
+    def x2(self, k):
+        x, c, z, y = self.place
+        own, temp = self.own[k], self.temps[k][1]
+        rows, columns = own.shape[-2:]
+        self.loads[k].wait()
+
+        def one(i):
+            own[i // 2, i % 2, x] = own[i // 2, i % 2, x] + temp[i // 2, i % 2, :rows, :columns]
+
+        self.add(8, one)
+        self.send(k, 2, own.at[:, 1 - y, x], self.side_in[k], self.beside)
+
+    def y(self, k):
+        x, c, z, y = self.place
+        own, side_in = self.own[k], self.side_in[k]
+        self.copies[k, 2].wait_recv()
+
+        def one(i):
+            own[i, y, x] = own[i, y, x] + side_in[i]
+
+        self.add(4, one)
+        for i in (1, 2, 3):
+            target = device(x, c, (z + i) % 4, y)
+            self.send(
+                k, 2 + i, own.at[(z + i) % 4, y, x], self.along_in[k].at[i - 1], target
+            )
+
+    def z(self, k):
+        x, c, z, y = self.place
+        for i in (1, 2, 3):
+            self.copies[k, 2 + i].wait_recv()
+        total = self.own[k][z, y, x].astype(jnp.float32)
+        for i in range(3):
+            total = total + self.along_in[k][i].astype(jnp.float32)
+        final = self.finals[k]
+        final[x, c] = total.astype(jnp.bfloat16)
+        self.send(k, 6, final.at[x, c], final.at[x, c], self.across)
+
+    def b(self, k):
+        x, c, z, y = self.place
+        final = self.finals[k]
+        self.copies[k, 6].wait_recv()
+        self.send(k, 7, final.at[:, c], final.at[:, c], self.core)
+
+    def run(self, *stages):
+        for name, number in stages:
+            getattr(self, name)(number)
+
+    def finish(self):
+        for (k, number), copy in self.copies.items():
+            if number == 7:
+                copy.wait_recv()
+            if number or k in self.slots:
+                copy.wait_send()
+        for k in self.slots:
+            self.keeps[k].wait()
+
+
+def closing_kernel(scale, images, features, *refs):
+    segs, pixels, pix_weights, cot, final = refs[:5]
+    normed_m, active_s, slope_s, self_att, packed, normed_self, normed_c, active_c, slope_c = refs[5:14]
+    att_low, w2s, w1s, wos, wqkv, w2c, w1c, wo = refs[14:22]
+    row_scales, gains, means, rows_in, value_n, queries, tops, pix_gain = refs[22:30]
+    refs = refs[30:]
+    count = 12
+    finals, core_in, over_in = refs[:count], refs[count : 2 * count], refs[2 * count : 3 * count]
+    out_rows, pixel_out, query_out = refs[3 * count : 3 * count + 3]
+    refs = refs[3 * count + 3 :]
+    own, side_in, along_in = refs[:count], refs[count : 2 * count], refs[2 * count : 3 * count]
+    refs = refs[3 * count :]
+    staging, temps = refs[:3], refs[3:7]
+    grad, acc, low, back_low, first, second, third, fourth, slope, head_grad = refs[7:17]
+    gain_grads, packed_grads = refs[17], refs[18]
+    all_grads = refs[19:21]
+    raw, out_tile, query_sums, gain_sums = refs[21:25]
+    sum_parts, sum_core, sum_over, sum_side, sum_along = refs[25:30]
+    send, recv, local, load, row_send, row_recv, grad_send, grad_recv = refs[30:38]
+    block_load, block_out, sum_send, sum_recv = refs[38:]
+    tile = acc
+
+    x, c, z, y = place()
+    pix, dp = lax.axis_index("pix"), lax.axis_index("dp")
+    others = [{"dp": dp, "pix": (pix + i) % 8} for i in range(1, 8)]
+    temp_of = [temps[0:2]] * 10 + [temps[2:4], temps[0:2]]
+    reduce = Reduce(
+        staging, own, core_in, over_in, side_in, along_in, finals, temp_of, (send, recv), local
     )
-    send, recv, local, row_send, row_recv = rest[5 * count :]
-    x, c, z, y = place()
-    pix = lax.axis_index("pix")
-    sems = (send, recv)
-    others = [(pix + i) % 8 for i in range(1, 8)]
-    core, across, beside = device(x, 1 - c, z, y), device(1 - x, c, z, y), device(x, c, z, 1 - y)
-    greet([{"dp": x * 2 + c, "pix": other} for other in others] + [core, across])
-    loads, between, over, side, along, back, last = [], [], {}, {}, {}, {}, {}
-    for k in range(count):
-        between.append(remote(grads[k].at[:, :, :, 1 - c], core_in[k], sems, (k, 0), core))
-        between[k].start()
-        loads.append(pltpu.make_async_copy(grads[k].at[:, :, :, c], own[k], local.at[k]))
-        loads[k].start()
-    keep = pltpu.make_async_copy(rows_in.at[:, pix], rows_out.at[:, pix], local.at[count])
-    keep.start()
-    rows = []
+    greet([*others, reduce.core, reduce.across])
+
+    loads = {}
+
+    def fetch(number, source, target):
+        loads[number] = pltpu.make_async_copy(source, target, load.at[number])
+        loads[number].start()
+
+    def ready(*numbers):
+        for number in numbers:
+            loads.pop(number).wait()
+
+    fetch(0, cot, low)
+    fetch(1, active_s, first)
+    fetch(2, w2s, third)
+    fetch(3, slope_s, slope)
+    fetch(4, normed_m, second)
+    fetch(5, w1s, fourth)
+    homes = [pltpu.make_async_copy(final.at[:, pix], out_rows.at[:, pix], load.at[31])]
     for i, other in enumerate(others):
-        copy = remote(
-            rows_in.at[:, other],
-            rows_out.at[:, pix],
-            (row_send, row_recv),
-            i,
-            {"dp": x * 2 + c, "pix": other},
-        )
+        source, target = final.at[:, (pix + i + 1) % 8], out_rows.at[:, pix]
+        homes.append(remote(source, target, (row_send, row_recv), i, other))
+    for copy in homes:
         copy.start()
-        rows.append(copy)
-
-    def after_core(k):
-        loads[k].wait()
-        between[k].wait()
-
-        def add(i, carry):
-            own[k][i // 2, i % 2] = own[k][i // 2, i % 2] + core_in[k][i // 2, i % 2]
+    gain_grads[...] = jnp.zeros_like(gain_grads)
+
+    def strips(one):
+        def step(i, carry):
+            one(i, pl.ds(pl.multiple_of(i * STRIP, STRIP), STRIP))
             return carry
 
-        lax.fori_loop(0, 8, add, 0)
-        if splits[k]:
-            over[k] = remote(own[k].at[:, :, 1 - x], over_in[k], sems, (k, 1), across)
-            over[k].start()
-
-    def after_over(k):
-        if splits[k]:
-            over[k].wait()
-
-            def add(i, carry):
-                own[k][i // 2, i % 2, x] = own[k][i // 2, i % 2, x] + over_in[k][i // 2, i % 2]
+        lax.fori_loop(0, grad.shape[0] // STRIP, step, 0)
+
+    def chunks(one):
+        def step(j, carry):
+            one(pl.ds(pl.multiple_of(j * CHUNK, CHUNK), CHUNK))
+            return carry
+
+        lax.fori_loop(0, STRIP // CHUNK, step, 0)
+
+    def weight_grad(k, slot, left, right, columns):
+        reduce.release(slot)
+        staged = staging[slot]
+
+        def one(i, strip):
+            product = left_matmul(left[:, strip], right[:, :columns])
+            staged[i, :, :, :, :, :columns] = (
+                product.reshape(2, 2, 2, STRIP // 8, columns).astype(jnp.bfloat16)
+            )
+
+        strips(one)
+        reduce.push(k, slot)
+
+    def through_slope(weight):
+        def one(i, strip):
+            tile[:STRIP] = right_matmul(low[strip, :], weight[...])
+
+            def chunk(part):
+                at = pl.ds(pl.multiple_of(i * STRIP, STRIP) + part.start, CHUNK)
+                back_low[at, :] = (tile[part, :] * slope[at, :].astype(jnp.float32)).astype(
+                    jnp.bfloat16
+                )
+
+            chunks(chunk)
+
+        strips(one)
+
+    def through_norm(number, normed, product, fresh=False):
+        gain = gains[number : number + 1]
+        inverse = 1.0 / gain
+        width = gain.shape[1]
+
+        def one(i, strip):
+            source = tile
+            if product is None:
+                source = acc
+            else:
+                tile[:STRIP] = product(strip)
+
+            def chunk(part):
+                at = pl.ds(pl.multiple_of(i * STRIP, STRIP) + part.start, CHUNK)
+                upper = source[at if product is None else part, :]
+                unit = normed[at, :].astype(jnp.float32) * inverse
+                gain_grads[number : number + 1] += jnp.sum(upper * unit, 0, keepdims=True)
+                upper = upper * gain
+                mean = jnp.sum(upper, 1, keepdims=True) * (1.0 / width)
+                tilt = jnp.sum(upper * unit, 1, keepdims=True) * (1.0 / width)
+                before = low[at, :].astype(jnp.float32) if fresh else grad[at, :]
+                row_scale = row_scales[at, number : number + 1]
+                after = before + (upper - mean - unit * tilt) * row_scale
+                grad[at, :] = after
+                low[at, :] = after.astype(jnp.bfloat16)
+
+            chunks(chunk)
+
+        strips(one)
+
+    ready(0, 1)
+    weight_grad(0, 0, first, low, 1024)
+    fetch(6, self_att, first)
+    ready(2, 3)
+    through_slope(third)
+    fetch(7, wos, third)
+    fetch(8, slope_c, slope)
+    reduce.run(("c1", 0))
+    ready(4)
+    weight_grad(1, 1, second, back_low, 1024)
+    reduce.run(("c2", 0), ("c1", 1))
+    ready(5)
+    through_norm(0, second, lambda strip: right_matmul(back_low[strip, :], fourth[...]), True)
+    fetch(9, normed_self, second)
+    half = head_grad.shape[1]
+    fetch(10, wqkv.at[:, :half], fourth.at[:, :half])
+    fetch(11, packed.at[:, :half], back_low.at[:, :half])
+    reduce.run(("c2", 1))
+
+    ready(6)
+    weight_grad(2, 0, first, low, 1024)
+    fetch(12, packed.at[:, half : 2 * half], first.at[:, :half])
+    reduce.run(("c1", 2))
+    ready(7, 9)
+    acc[...] = jnp.zeros_like(acc)
+    rows_of_image = means.shape[2]
+    width = half // 6
+    for pair in range(4):
+        ready(11 + pair)
+        block = (back_low, first)[pair % 2]
+
+        def unit(i, carry, pair=pair, block=block):
+            image, head = i // 2, i % 2
+            rows = pl.ds(pl.multiple_of(image * rows_of_image, rows_of_image), rows_of_image)
+
+            def columns(part):
+                start = pl.multiple_of(head * (3 * width) + part * width, width)
+                return pl.ds(start, width)
+
+            query, key, value = (block[rows, columns(part)] for part in range(3))
+            out_rows_ = pl.ds(pl.multiple_of((pair * 2 + head) * width, width), width)
+            upper = right_matmul(low[rows, :], third[out_rows_, :])
+            scores = right_matmul(query, key) * scale
+            weights = jnp.exp(scores - jnp.max(scores, 1, keepdims=True))
+            den = jnp.sum(weights, 1, keepdims=True)
+            grad_num = (upper / den).astype(jnp.bfloat16)
+            slopes = right_matmul(grad_num, value)
+            grad_den = -jnp.sum(weights * slopes, 1, keepdims=True) / den
+            grad_scores = (weights * (slopes + grad_den)).astype(jnp.bfloat16)
+            head_grad[rows, columns(0)] = (matmul(grad_scores, key) * scale).astype(jnp.bfloat16)
+            head_grad[rows, columns(1)] = (left_matmul(grad_scores, query) * scale).astype(
+                jnp.bfloat16
+            )
+            head_grad[rows, columns(2)] = left_matmul(
+                weights.astype(jnp.bfloat16), grad_num
+            ).astype(jnp.bfloat16)
+            return carry
+
+        lax.fori_loop(0, 4, unit, 0)
+        if pair < 2:
+            start = (pair + 2) * half
+            fetch(13 + pair, packed.at[:, start : start + half], block.at[:, :half])
+        reduce.run(
+            *((("c2", 2), ("x1", 0)), (("c2", 3), ("y", 0), ("x1", 1)), (("c2", 4), ("z", 0), ("y", 1), ("x1", 2)), (("c2", 5), ("b", 0), ("z", 1), ("y", 2), ("x1", 3)))[pair]
+        )
+        weight_grad(3 + pair, (pair + 1) % 2, second, head_grad, half)
+        ready(10 if pair == 0 else 15 + pair)
+
+        def spread(i, strip):
+            acc[strip, :] += right_matmul(head_grad[strip, :], fourth[:, :half])
+
+        strips(spread)
+        if pair < 3:
+            start = (pair + 1) * half
+            fetch(16 + pair, wqkv.at[:, start : start + half], fourth.at[:, :half])
+        reduce.run(
+            *((("c1", 3), ("x2", 0)), (("c1", 4), ("x2", 1)), (("c1", 5), ("x2", 2)), (("c1", 6), ("x2", 3)))[pair]
+        )
+    fetch(20, active_c, first)
+    fetch(21, w2c, third)
+    fetch(22, w1c, fourth)
+    through_norm(1, second, None)
+    fetch(23, normed_c, second)
+    reduce.run(("c2", 6), ("y", 3), ("b", 1), ("z", 2), ("x1", 4))
+
+    ready(20)
+    weight_grad(7, 1, first, low, 1024)
+    fetch(24, att_low, first)
+    reduce.run(("x2", 4))
+    ready(21, 8)
+    through_slope(third)
+    fetch(25, wo, third)
+    reduce.run(("c1", 7), ("y", 4), ("z", 3), ("b", 2), ("x1", 5))
+    ready(23)
+    weight_grad(8, 0, second, back_low, 1024)
+    reduce.run(("c2", 7), ("x2", 5), ("c1", 8))
+    ready(22)
+    through_norm(2, second, lambda strip: right_matmul(back_low[strip, :], fourth[...]))
+    reduce.run(("c2", 8), ("y", 5), ("z", 4), ("b", 3), ("x1", 6))
+
+    ready(25)
+
+    def upper_rows(i, strip):
+        back_low[strip, :] = right_matmul(low[strip, :], third[...]).astype(jnp.bfloat16)
+
+    strips(upper_rows)
+    micros = means.shape[0]
+    grad_sems = (grad_send, grad_recv)
+    along = {}
+    for m in range(micros):
+        rows = pl.ds(m * rows_of_image, rows_of_image)
+        sums = right_matmul(value_n[...], back_low[rows, :]) / rows_in[m, 0:1]
+        grad_den = -jnp.sum(sums * means[m].astype(jnp.float32), 0, keepdims=True)
+        packed_grads[m, : FROWS - 16] = sums[: FROWS - 16].astype(jnp.bfloat16)
+        at = lax.broadcasted_iota(jnp.int32, (16, sums.shape[1]), 0) + (FROWS - 16)
+        tail = with_rows(sums[FROWS - 16 :], grad_den, rows_in[m, 1:2])
+        packed_grads[m, FROWS - 16 :] = jnp.where(at == DEN_ROW + 1, 0.0, tail).astype(
+            jnp.bfloat16
+        )
+        mine, home = packed_grads.at[m], all_grads[m].at[z, y]
+        for i in (1, 2, 3):
+            along[m, i] = remote(
+                mine, home, grad_sems, (m, i - 1), device(x, c, (z + i) % 4, y)
+            )
+            along[m, i].start()
+        along[m, 4] = remote(mine, home, grad_sems, (m, 3), reduce.beside)
+        along[m, 4].start()
+        fetch(26 + m, mine, home)
+
+    def pass_grads(m):
+        for i in (1, 2, 3):
+            along[m, i].wait_recv()
+            block = all_grads[m].at[(z + 4 - i) % 4, y]
+            along[m, 4 + i] = remote(block, block, grad_sems, (m, 3 + i), reduce.beside)
+            along[m, 4 + i].start()
+
+    def grads_ready(m):
+        ready(26 + m)
+        for i in range(4, 8):
+            along[m, i].wait_recv()
+
+    ready(24)
+    weight_grad(9, 1, first, low, 1024)
+    reduce.run(("x2", 6), ("c1", 9))
+    value_grad = sum(
+        matmul(means[m], back_low[m * rows_of_image : (m + 1) * rows_of_image, :])
+        for m in range(micros)
+    )
+    staged = staging[2]
+    shards = [
+        jnp.concatenate(
+            [
+                value_grad[:, s * 128 : (s + 1) * 128],
+                gain_grads[:, s * 128 : (s + 1) * 128],
+                jnp.zeros((320 - FROWS - 8, 128), jnp.float32),
+            ],
+            0,
+        )
+        for s in range(8)
+    ]
+    for s in range(8):
+        staged[s // 2, s % 2] = shards[s].reshape(2, 2, 80, 128).astype(jnp.bfloat16)
+    reduce.push(10, 2)
+    reduce.release(0)
+    staged = staging[0]
+    for s in range(8):
+        at = s * 64
+        both = grad[at : at + 64, :] + grad[at + rows_of_image : at + rows_of_image + 64, :]
+        staged[s // 2, s % 2, :, :, :16] = both.reshape(2, 2, 16, both.shape[1]).astype(
+            jnp.bfloat16
+        )
+    reduce.push(11, 0)
+    reduce.run(("c2", 9), ("c1", 10), ("y", 6), ("c2", 10), ("c1", 11), ("z", 5), ("c2", 11), ("b", 4))
+
+    slots = pixels.shape[2]
+    blocks = slots // BLOCK
+    pieces = BLOCK // PIECE
+    halves = BLOCK // out_tile.shape[2]
+    query_sums[...] = jnp.zeros_like(query_sums)
+    gain_sums[...] = jnp.zeros_like(gain_sums)
+    scores_ref, back_ref, wide = low, acc, slope
+    weight_slots = (first, second)
+
+    def block_loads(m, b):
+        rows = pl.ds(b * BLOCK, BLOCK)
+        slot = b % 2
+        return (
+            pltpu.make_async_copy(pixels.at[m, :, rows], raw.at[slot], block_load.at[0, slot]),
+            pltpu.make_async_copy(
+                pix_weights.at[m, rows],
+                weight_slots[slot].at[:, :rows_of_image],
+                block_load.at[1, slot],
+            ),
+        )
+
+    def block_store(m, b, part):
+        rows = pl.ds(b * BLOCK + part * (BLOCK // halves), BLOCK // halves)
+        return pltpu.make_async_copy(
+            out_tile.at[part], pixel_out.at[m, :, rows], block_out.at[part]
+        )
+
+    def pixels_back(m, after):
+        for copy in block_loads(m, 0):
+            copy.start()
+        for b in range(blocks):
+            if b + 1 < blocks:
+                for copy in block_loads(m, b + 1):
+                    copy.start()
+            for copy in block_loads(m, b):
+                copy.wait()
+            normed, unit_, row_scale = normed_block(raw[b % 2], pix_gain[...], features)
+            wide[:FROWS, :] = normed
+            weights = weight_slots[b % 2]
+
+            def piece(k, carry, b=b, weights=weights):
+                rows = pl.ds(pl.multiple_of(k * PIECE, PIECE), PIECE)
+                number = b * pieces + k
+                seg = segs[m * blocks * pieces + number]
+                image = jnp.minimum(seg, images - 1)
+                upper = all_grads[m][image // 2, image % 2]
+                unused, top = read_rows(upper[FROWS - 16 :].astype(jnp.float32))
+                factor = jnp.where(seg < images, jnp.exp(tops[m, number] - top), 0.0)
+                full = weights[rows, :rows_of_image].astype(jnp.float32) * factor
+                slopes = left_matmul(wide[:FROWS, rows], upper)
+                scores_ref[rows, :rows_of_image] = (full * slopes).astype(jnp.bfloat16)
+                back_ref[:FROWS, rows] = right_matmul(upper, full.astype(jnp.bfloat16))
                 return carry
 
-            lax.fori_loop(0, 8, add, 0)
-            source = own[k].at[:, 1 - y, x]
-        else:
-            source = own[k].at[:, 1 - y]
-        side[k] = remote(source, side_in[k], sems, (k, 2), beside)
-        side[k].start()
-
-    def after_side(k):
-        side[k].wait()
-
-        def add(i, carry):
-            if splits[k]:
-                own[k][i, y, x] = own[k][i, y, x] + side_in[k][i]
-            else:
-                own[k][i, y] = own[k][i, y] + side_in[k][i]
-            return carry
-
-        lax.fori_loop(0, 4, add, 0)
-        for i in (1, 2, 3):
-            block = own[k].at[(z + i) % 4, y]
-            along[k, i] = remote(
-                block.at[x] if splits[k] else block,
-                along_in[k].at[i - 1],
-                sems,
-                (k, 2 + i),
-                device(x, c, (z + i) % 4, y),
+            lax.fori_loop(0, pieces, piece, 0)
+            scores = scores_ref[:, :rows_of_image]
+            query_sums[...] += matmul(wide[:FROWS, :], scores)
+            back = back_ref[:FROWS, :] + right_matmul(queries[...], scores)
+            at = lax.broadcasted_iota(jnp.int32, back.shape, 0)
+            back = jnp.where(at < features, back, 0.0)
+            product = back * unit_
+            gain_sums[:FROWS] += sum(
+                product[:, j * 128 : (j + 1) * 128] for j in range(BLOCK // 128)
             )
-            along[k, i].start()
-
-    def after_along(k):
-        for i in (1, 2, 3):
-            along[k, i].wait()
-        block = own[k][z, y, x] if splits[k] else own[k][z, y]
-        total = block.astype(jnp.float32)
-        for i in range(3):
-            total = total + along_in[k][i].astype(jnp.float32)
-        total = total.astype(jnp.bfloat16)
-        if splits[k]:
-            finals[k][x, c] = total
-            back[k] = remote(finals[k].at[x, c], finals[k].at[x, c], sems, (k, 6), across)
-        else:
-            own[k][z, y] = total
-            back[k] = remote(own[k].at[z, y], over_in[k], sems, (k, 6), across)
-        back[k].start()
-
-    def after_back(k):
-        back[k].wait()
-        if not splits[k]:
-            finals[k][:, c] = own[k][z, y] + over_in[k][...]
-        last[k] = remote(finals[k].at[:, c], finals[k].at[:, c], sems, (k, 7), core)
-        last[k].start()
-
-    stages = (after_core, after_over, after_side, after_along, after_back)
-    for step in range(count + len(stages) - 1):
-        for number, stage in enumerate(stages):
-            if 0 <= step - number < count:
-                stage(step - number)
-    for k in range(count):
-        last[k].wait()
-    for copy in rows:
+            back = back * pix_gain[...]
+            mean = jnp.sum(back, 0, keepdims=True) * (1.0 / features)
+            tilt = jnp.sum(back * unit_, 0, keepdims=True) * (1.0 / features)
+            result = (back - mean - unit_ * tilt) * row_scale
+            size = BLOCK // halves
+            for part in range(halves):
+                if m or b:
+                    block_store(m, b, part).wait()
+                out_tile[part] = result[:, part * size : (part + 1) * size]
+                block_store(m, b, part).start()
+            reduce.run(*after[b])
+
+    pass_grads(0)
+    reduce.run(("x1", 7), ("x2", 7))
+    pass_grads(1)
+    reduce.run(("y", 7), ("z", 6), ("b", 5))
+    grads_ready(0)
+    pixels_back(0, ((), (("x1", 8), ("x2", 8)), (("z", 7), ("b", 6)), (("y", 8),)))
+    grads_ready(1)
+    pixels_back(1, ((("x1", 9), ("x2", 9)), (("z", 8), ("b", 7)), (("x1", 10), ("x2", 10), ("x1", 11), ("x2", 11)), (("y", 9),)))
+    for part in range(halves):
+        block_store(0, 0, part).wait()
+
+    sums = query_sums[...]
+    at = lax.broadcasted_iota(jnp.int32, sums.shape, 0)
+    gain_row = jnp.sum(gain_sums[...].T, 0, keepdims=True)
+    gain_row = jnp.concatenate([gain_row, jnp.zeros((1, 128), jnp.float32)], 1)
+    sums = jnp.where(at == GAIN_ROW, gain_row, sums)
+    for j in range(4):
+        sum_parts[j // 2, j % 2] = sums[:, j * 128 : (j + 1) * 128].astype(jnp.bfloat16)
+    sum_sems = (sum_send, sum_recv)
+    copies = [remote(sum_parts.at[1 - c], sum_core, sum_sems, 0, reduce.core)]
+    copies[0].start()
+    reduce.run(("y", 10), ("y", 11), ("z", 9), ("b", 8))
+    copies[0].wait_recv()
+    sum_parts[c] = sum_parts[c] + sum_core[...]
+    copies.append(remote(sum_parts.at[c, 1 - x], sum_over, sum_sems, 1, reduce.across))
+    copies[1].start()
+    reduce.run(("z", 10), ("z", 11))
+    copies[1].wait_recv()
+    sum_parts[c, x] = sum_parts[c, x] + sum_over[...]
+    copies.append(remote(sum_parts.at[c, x], sum_side, sum_sems, 2, reduce.beside))
+    copies[2].start()
+    reduce.run(("b", 9))
+    copies[2].wait_recv()
+    sum_along[z] = sum_parts[c, x] + sum_side[...]
+    for i in (1, 2, 3):
+        target = device(x, c, (z + i) % 4, y)
+        copies.append(remote(sum_along.at[z], sum_along.at[z], sum_sems, 2 + i, target))
+        copies[2 + i].start()
+    reduce.run(("b", 10), ("b", 11))
+    for i in (1, 2, 3):
+        copies[2 + i].wait_recv()
+    total = sum(sum_along[i].astype(jnp.float32) for i in range(4))
+    query_out[c, x] = total.astype(jnp.bfloat16)
+    copies.append(remote(query_out.at[c, x], query_out.at[c, x], sum_sems, 6, reduce.across))
+    copies[6].start()
+    copies[6].wait_recv()
+    copies.append(remote(query_out.at[c], query_out.at[c], sum_sems, 7, reduce.core))
+    copies[7].start()
+    copies[7].wait_recv()
+    for copy in copies:
+        copy.wait_send()
+    for copy in along.values():
+        copy.wait_send()
+    for copy in homes:
         copy.wait()
-    keep.wait()
-
-
-def reduce_grads(grads, splits, rows):
-    count = len(grads)
-    views = [
-        grad.reshape(4, 2, 2, 2, grad.shape[0] // 32, grad.shape[1]).astype(jnp.bfloat16)
-        for grad in grads
-    ]
-    buffers = ([], [], [], [], [])
-    for view, split in zip(views, splits, strict=True):
-        block = view.shape[4:]
-        lead = () if split else (2,)
-        for group, shape in zip(
-            buffers,
-            (
-                (4, 2, 2, *block),
-                (4, 2, 2, *block),
-                (4, 2, *block) if split else (2, *block),
-                (4, *lead, *block),
-                (3, *lead, *block),
-            ),
-            strict=True,
-        ):
-            group.append(pltpu.VMEM(shape, jnp.bfloat16))
+    reduce.finish()
+
+
+def closing(
+    segs,
+    pixels,
+    pix_weights,
+    cot,
+    final,
+    final_kept,
+    self_att,
+    packed,
+    normed_self,
+    cross_kept,
+    att_low,
+    weights,
+    row_scales,
+    gains,
+    means,
+    rows,
+    value_n,
+    queries,
+    tops,
+    pix_gain,
+    features,
+    images,
+    scale,
+):
+    bf16, f32 = jnp.bfloat16, jnp.float32
+    total_rows, width = cot.shape
+    micros, unused, slots = pixels.shape
+    latents = means.shape[2]
+    half = 3 * width // 4
+    full, part = (STRIP // 8, width), (STRIP // 8, half)
+    shapes = [full] * 3 + [part] * 4 + [full] * 3 + [(80, 128), (16, width)]
+    count = len(shapes)
+
+    def grid(*lead):
+        return [(*lead, *shape) for shape in shapes]
+
+    def scratch(shape, dtype=bf16):
+        return pltpu.VMEM(shape, dtype)
+
+    def arrays(list_):
+        return [jax.ShapeDtypeStruct(shape, bf16) for shape in list_]
+
+    square = (total_rows, width)
+    quarter = (FROWS, 128)
+    smem = pl.BlockSpec(memory_space=pltpu.SMEM)
     results = pl.pallas_call(
-        functools.partial(reduce_kernel, splits),
-        out_shape=[jax.ShapeDtypeStruct((2, 2, *view.shape[4:]), jnp.bfloat16) for view in views]
-        + [jax.ShapeDtypeStruct(rows.shape, rows.dtype)],
-        in_specs=[HBM] * (count + 1),
-        out_specs=[VMEM] * count + [HBM],
+        functools.partial(closing_kernel, scale, images, features),
+        out_shape=[
+            *arrays(grid(2, 2)),
+            *arrays(grid(4, 2, 2)),
+            *arrays(grid(4, 2)),
+            jax.ShapeDtypeStruct(final.shape, bf16),
+            jax.ShapeDtypeStruct(pixels.shape, f32),
+            jax.ShapeDtypeStruct((2, 2, *quarter), bf16),
+        ],
+        in_specs=[smem] + [HBM] * 21 + [VMEM] * 8,
+        out_specs=[VMEM] * count + [HBM] * (2 * count + 2) + [VMEM],
         scratch_shapes=[
-            *(shape for group in buffers for shape in group),
+            *map(scratch, grid(4, 2, 2)),
+            *map(scratch, grid(4)),
+            *map(scratch, grid(3)),
+            *[scratch((4, 2, 2, 2, *shape)) for shape in (full, full, shapes[10])],
+            *[
+                scratch((4, 2, *lead, *shape))
+                for shape in (full, shapes[10])
+                for lead in ((2,), ())
+            ],
+            scratch(square, f32),
+            scratch(square, f32),
+            *[scratch(square) for _ in range(7)],
+            scratch((total_rows, half)),
+            scratch((8, width), f32),
+            scratch((micros, FROWS, latents)),
+            *[scratch((4, 2, FROWS, latents)) for _ in range(micros)],
+            scratch((2, FROWS, BLOCK)),
+            scratch((2, FROWS, BLOCK // 2), f32),
+            scratch((FROWS, latents), f32),
+            scratch((384, 128), f32),
+            scratch((2, 2, *quarter)),
+            scratch((2, *quarter)),
+            scratch(quarter),
+            scratch(quarter),
+            scratch((4, *quarter)),
             pltpu.SemaphoreType.DMA((count, 8)),
             pltpu.SemaphoreType.DMA((count, 8)),
-            pltpu.SemaphoreType.DMA((count + 1,)),
+            pltpu.SemaphoreType.DMA((count, 3)),
+            pltpu.SemaphoreType.DMA((32,)),
             pltpu.SemaphoreType.DMA((7,)),
             pltpu.SemaphoreType.DMA((7,)),
+            pltpu.SemaphoreType.DMA((micros, 7)),
+            pltpu.SemaphoreType.DMA((micros, 7)),
+            pltpu.SemaphoreType.DMA((2, 2)),
+            pltpu.SemaphoreType.DMA((2,)),
+            pltpu.SemaphoreType.DMA((8,)),
+            pltpu.SemaphoreType.DMA((8,)),
         ],
-        compiler_params=remote_params(3, 56 * MIB),
-        name="reduce_grads",
-    )(*views, rows)
+        compiler_params=remote_params(1, 64 * MIB - 1024),
+        name="closing",
+    )(
+        segs,
+        pixels,
+        pix_weights,
+        cot,
+        final,
+        *final_kept,
+        self_att,
+        packed,
+        normed_self,
+        *cross_kept,
+        att_low,
+        *weights,
+        row_scales,
+        gains,
+        means,
+        rows,
+        value_n,
+        queries,
+        tops,
+        pix_gain,
+    )
     shards = [
-        result.reshape(grad.shape[0] // 8, grad.shape[1])
-        for result, grad in zip(results[:-1], grads, strict=True)
+        result.reshape(4 * shape[0], shape[1])
+        for result, shape in zip(results[:count], shapes, strict=True)
     ]
-    return shards, results[-1]
-
-
-def spread_kernel(block, out, send, recv):
-    pix, dp = lax.axis_index("pix"), lax.axis_index("dp")
-    others = [(pix + i) % 8 for i in range(1, 8)]
-    greet([{"dp": dp, "pix": other} for other in others])
-    copies = []
-    for i, other in enumerate(others):
-        copy = remote(block, out.at[pix], (send, recv), i, {"dp": dp, "pix": other})
-        copy.start()
-        copies.append(copy)
-    out[pix] = block[...]
-    for copy in copies:
-        copy.wait()
-
-
-def spread(block):
-    return pl.pallas_call(
-        spread_kernel,
-        out_shape=jax.ShapeDtypeStruct((8, *block.shape), block.dtype),
-        in_specs=[VMEM],
-        out_specs=VMEM,
-        scratch_shapes=[pltpu.SemaphoreType.DMA((7,)), pltpu.SemaphoreType.DMA((7,))],
-        compiler_params=remote_params(4),
-        name="spread",
-    )(block)
+    query_sums = results[-1].reshape(4, *quarter).transpose(1, 0, 2).reshape(FROWS, latents)
+    return shards, results[-3], results[-2], query_sums
 
 
 def image_body(
@@ -1338,106 +1665,93 @@
     order = jnp.arange(capacity // PIECE, dtype=jnp.int32)[None, :, None]
     last = jnp.max(jnp.where(here, order, -1), 1).reshape(-1)
     segs = segs.reshape(-1)
-    gain_pix = pixel_gain.astype(f32)[None]
+    gain_pix = jnp.pad(pixel_gain.astype(f32), (0, FROWS - features))[:, None]
+    pixel_rows = jnp.pad(
+        pixels[0].transpose(0, 2, 1), ((0, 0), (0, FROWS - features), (0, 0))
+    )
     wholes, results = opening(
-        same, last, shards, splits, cotangent[0], pixels[0], gain_pix, cross_scale
+        same, last, shards, splits, pixel_rows, gain_pix, features, images, cross_scale
     )
     lat_full, wq, key_t, value_t, wo, w1c, w2c, wqkv, wos, w1s, w2s = wholes
-    cot_rows, pix_weights, normed_lat, queries, query_t, pix_tops, means, rows = results
+    pix_weights, normed_lat, queries, query_t, pix_tops, means, rows = results
+    cot_slots, means = lax.optimization_barrier((cotangent[0], means))
+    cot_rows = lax.all_to_all(cot_slots, "pix", split_axis=1, concat_axis=1, tiled=True)
     g_lat, g_cross, g_self, g_mlp = (key_t[:, GAIN_LANE + i].astype(f32) for i in range(4))
     value_t = value_t[:, :FROWS]
     lat_f = lat_full.astype(f32)
     den, top = rows[:, 0], rows[:, 1]
 
-    att = jnp.einsum("mfr,df->mrd", means, value_t, preferred_element_type=f32)
-    att_low = att.astype(bf16).reshape(micros * latents, width)
+    att_low = jnp.einsum("mfr,df->mrd", means, value_t, preferred_element_type=f32)
+    att_low = att_low.astype(bf16).reshape(micros * latents, width)
     start_rows = jnp.broadcast_to(lat_f[None], (micros, latents, width)).reshape(-1, width)
     after_cross = start_rows + matmul(att_low, wo)
-    after_mlp, cross_kept = mlp_forward(after_cross, g_cross, w1c, w2c)
-    normed_self = layer_norm(after_mlp, g_self).astype(bf16)
-    packed = matmul(normed_self, wqkv).astype(bf16).reshape(micros, latents, 3 * width)
-    self_att = attention(packed, self_scale).reshape(-1, width)
+    after_mlp, cross_kept = feed(after_cross, g_cross, w1c, w2c)
+    normed_self, self_scale_rows = normed_rows(after_mlp, g_self)
+    packed = matmul(normed_self, wqkv).astype(bf16)
+    self_att = attention(packed.reshape(micros, latents, 3 * width), head_size ** (-0.5))
+    self_att = self_att.reshape(-1, width)
     after_self = after_mlp + matmul(self_att, wos)
-    final, final_kept = mlp_forward(after_self, g_mlp, w1s, w2s)
+    final, final_kept = feed(after_self, g_mlp, w1s, w2s)
     final = final.astype(bf16).reshape(micros, 8, row_count, width)
-
-    grad = cot_rows.astype(f32).reshape(-1, width)
-    grad, d_gm, d_w1s, d_w2s = mlp_backward(grad, after_self, g_mlp, w1s, w2s, final_kept)
-    grad_low = grad.astype(bf16)
-    d_wos = left_matmul(self_att, grad_low)
-    grad_att = right_matmul(grad_low, wos).reshape(micros, latents, width)
-    grad_packed = attention_back(packed, grad_att, self_scale).reshape(-1, 3 * width)
-    d_wqkv = left_matmul(normed_self, grad_packed)
-    grad_inputs, d_gs = norm_back(after_mlp, g_self, right_matmul(grad_packed, wqkv))
-    grad = grad + grad_inputs
-    grad, d_gc, d_w1c, d_w2c = mlp_backward(grad, after_cross, g_cross, w1c, w2c, cross_kept)
-    grad_lat = jnp.sum(grad.reshape(micros, latents, width), 0)
-    grad_low = grad.astype(bf16)
-    d_wo = left_matmul(att_low, grad_low)
-    grad_att = right_matmul(grad_low, wo).reshape(micros, latents, width)
-    grad_num = (grad_att / den[:, :, None]).astype(bf16)
-    grad_den = -jnp.sum(grad_att * att, 2) / den
-    grad_sums = jnp.einsum("mrd,df->mfr", grad_num, value_t, preferred_element_type=f32)
-    d_wv = jnp.einsum("mrd,mfr->df", grad_att.astype(bf16), means, preferred_element_type=f32)
-    all_grads = to_holders(grad_sums, jnp.stack([grad_den, top], 1))
-    pixel_grad, query_sums, pix_gain_sums = pixel_backward(
-        segs, pixels[0], gain_pix, query_t, pix_weights, pix_tops, all_grads
+    row_scales = jnp.concatenate([final_kept[0], self_scale_rows, cross_kept[0]], 1)
+    row_scales = jnp.pad(row_scales, ((0, 0), (0, 125)))
+
+    shards, latent_out, pixel_grad, query_sums = closing(
+        segs,
+        pixel_rows,
+        pix_weights,
+        cot_rows.reshape(-1, width),
+        final,
+        final_kept[1:],
+        self_att,
+        packed,
+        normed_self,
+        cross_kept[1:],
+        att_low,
+        (w2s, w1s, wos, wqkv, w2c, w1c, wo),
+        row_scales,
+        jnp.stack([g_mlp, g_self, g_cross]),
+        means,
+        rows,
+        value_t.T,
+        query_t,
+        pix_tops,
+        gain_pix,
+        features,
+        images,
+        head_size ** (-0.5),
     )
-
-    gain_grads = jnp.stack([d_gc, d_gs, d_gm], 1)
-    small = jnp.concatenate([widen(d_wv, 384), widen(gain_grads, 128)], 1)
-    halves = grad_lat.reshape(8, row_count, 2, width // 2).transpose(0, 2, 1, 3)
-    small = jnp.concatenate([small, halves.reshape(8 * 2 * row_count, width // 2)], 1)
-    query_rows = widen(query_sums.T, 384).reshape(8, row_count, 384)
-    pix_gain_rows = jnp.pad(
-        widen(pix_gain_sums, 384)[None], ((0, 7), (0, row_count - 1), (0, 0))
+    f_w2s, f_w1s, f_wos, *f_qkv, f_w2c, f_w1c, f_wo, f_vec, f_lat = shards
+    d_gpix = query_sums[GAIN_ROW, :features].astype(f32)
+
+    grad_queries = lax.dot_general(
+        query_sums, key_t[:, :FROWS], (((0,), (1,)), ((), ())), preferred_element_type=f32
     )
-    query_rows = jnp.concatenate([query_rows, pix_gain_rows], 1).reshape(-1, 384)
-    parts = (
-        d_w2s,
-        d_w1s,
-        d_wos,
-        d_wqkv,
-        d_w2c,
-        d_w1c,
-        d_wo,
-        small,
-        query_rows,
-    )
-    splits = (True, False, True, True, False, True, False, True, True)
-    reduced, latent_out = reduce_grads(parts, splits, final)
-    f_w2s, f_w1s, f_wos, f_wqkv, f_w2c, f_w1c, f_wo, small, query_rows = reduced
-    query_all = spread(query_rows)
-    d_gpix = query_all[0, row_count, :features].astype(f32)
-    query_all = query_all[:, :row_count].reshape(latents, 384)
-
-    grad_queries = (right_matmul(query_all, key_t) * cross_scale).astype(bf16)
+    grad_queries = (grad_queries * cross_scale).astype(bf16)
     columns = lax.dynamic_slice_in_dim(normed_lat, position * (width // 8), width // 8, 1)
     d_wq = left_matmul(columns, grad_queries)
     query_columns = lax.dynamic_slice_in_dim(queries, position * (width // 8), width // 8, 1)
-    d_wk = (left_matmul(query_all, query_columns) * cross_scale)[:features]
+    d_wk = matmul(query_sums[:features], query_columns) * cross_scale
     grad_norm_lat, d_glat = norm_back(lat_f, g_lat, right_matmul(grad_queries, wq))
     d_glat = lax.dynamic_slice_in_dim(d_glat, position * (width // 8), width // 8, 0)
     grad_norm_rows = lax.dynamic_slice_in_dim(grad_norm_lat, position * row_count, row_count, 0)
-    grad_lat = small[:, width // 2 :].astype(f32).reshape(2, row_count, width // 2)
-    grad_lat = grad_lat.transpose(1, 0, 2).reshape(row_count, width)
     return (
         latent_out[None],
-        pixel_grad[None],
-        grad_lat + grad_norm_rows,
+        pixel_grad[:, :features].transpose(0, 2, 1)[None],
+        f_lat.astype(f32) + grad_norm_rows,
         d_gpix,
         d_glat,
         d_wq,
         d_wk,
-        small[:, :features].astype(f32).T,
+        f_vec[:features].astype(f32),
         f_wo.astype(f32),
-        small[:, 384].astype(f32),
+        f_vec[FROWS + 2].astype(f32),
         f_w1c.astype(f32),
         f_w2c.astype(f32),
-        small[:, 385].astype(f32),
-        f_wqkv.astype(f32),
+        f_vec[FROWS + 1].astype(f32),
+        jnp.concatenate(f_qkv, 1).astype(f32),
         f_wos.astype(f32),
-        small[:, 386].astype(f32),
+        f_vec[FROWS].astype(f32),
         f_w1s.astype(f32),
         f_w2s.astype(f32),
     )

time: 736 us -> 542 us (0.74)
  matrix products: 121 us -> 40.3 us
  Pallas kernels: 487 us -> 421 us
  local copies, waits for them, and re-layouts: 75.1 us -> 41.4 us
  other arithmetic: 40.4 us -> 23 us
  starting transfers between devices: 0 us -> 9.62 us
    pallas_call x6 -> x2, Pallas kernels: 471 us -> 405 us  [the longest x1 250 us: closing(): pl.pallas_call(functools.partial(closing_kernel, scale, images, features)...]
    dot_general x9 -> x1, matrix products: 41.8 us -> 1.64 us  [right_matmul(): lax.dot_general(left, right, (((1,), (1,)), ((), ())), preferred_element_...]
    dot_general x9 -> x1, matrix products: 37.4 us -> 2.28 us  [left_matmul(): lax.dot_general(left, right, (((0,), (0,)), ((), ())), preferred_element_...]
    unnamed x119 -> x99, local copies, waits for them, and re-layouts: 45.6 us -> 28.5 us
    dot_general x4 -> x0, local copies, waits for them, and re-layouts: 14.9 us -> none  [the longest x3 9.52 us: left_matmul(): lax.dot_general(left, right, (((0,), (0,)), ((), ())), preferred_element_...]
    all_to_all x0 -> x1, starting transfers between devices: none -> 9.62 us  [image_body(): lax.all_to_all(cot_slots, 'pix', split_axis=1, concat_axis=1, tiled=True)]
    dot_general x7 -> x8, matrix products: 33.7 us -> 33 us  [matmul(): return jnp.dot(left, right, preferred_element_type=jnp.float32)]
  transfers between devices with their start and end apart: 0 -> 1, of which waited for: 0 -> 0; matrix products, arithmetic and copies ran while one was open for 0% -> 10% of each run, Pallas kernels for 0% -> 3%
where the time goes in v3:
time: 542 us; the launch traced here: 537 us
  Pallas kernels  421 us (78%)
  local copies, waits for them, and re-layouts  41.4 us (8%)
  matrix products  40.3 us (7%)
  other arithmetic  23 us (4%)
  starting transfers between devices  9.62 us (2%)
    pallas_call x1, Pallas kernels, closing(): pl.pallas_call(functools.partial(closing_kernel, scale, images, features)...  250 us
    pallas_call x1, Pallas kernels, opening(): pl.pallas_call(functools.partial(opening_kernel, splits, scale, features)...  155 us
    dot_general x8, matrix products, matmul(): return jnp.dot(left, right, preferred_element_type=jnp.float32)  33 us
    unnamed x99, local copies, waits for them, and re-layouts  28.5 us
    pallas_call x1, Pallas kernels, attention(): pl.pallas_call(functools.partial(attention_kernel, scale), grid=(micros,...  15.8 us
  transfers between devices with their start and end apart: 1, of which 0 were waited for; matrix products, arithmetic and copies ran while one was open for 10% of the time, Pallas kernels for 3%

profile of v3, /device:TPU:0, one launch (start us, length us, event | category | flops | bytes accessed | tf_op | source)
XLA Modules:
  0.0 536.6 jit_solution(1501374672804138027)
XLA Ops:
  3.8 1.0 fusion.9
  4.7 0.8 copy.73
  5.5 1.0 copy.92
  6.5 0.8 reshape.434.refs_14_.refs_29_
  7.2 3.6 copy.103
  10.8 3.0 copy.102
  14.5 2.7 pad.29.refs_13_.refs_1_
  17.1 155.3 %opening.1 = (bf16[4,2,2,2,16,1024]{5,4,3,2,1,0:T(8,128)(2,1)}, bf16[4,2,2,2,32,1024]{5,4,3,2,1,0:T(8,128)(2,1)}, bf16[4,2,2,2,32,384]{5,4,3,2,1,0:T(8,128)(2,1)...) custom-call(s32[32]{0:T(128)} %reshape.415.refs_0_, ...), custom_call_target="tpu_custom_call" | custom-call | tf_op jit(solution)/shard_map/opening/pallas_call | solution.py:817
  172.4 9.6 %all-to-all-start = ((bf16[2,8,64,1024]{3,2,0,1:T(8,128)(2,1)}), bf16[2,8,64,1024]{3,2,0,1:T(8,128)(2,1)S(1)}, u32[]{:S(2)}, u32[]{:S(2)}) async-start(bf16[2,8,64,1024]{3,2,0,1:T(8,128)(2,1)} %bitcast.147), calls=%async_computation | async-start | bytes 4194304 | tf_op jit(solution)/shard_map/all_to_all | solution.py:1678
  184.7 2.2 copy.87
  186.9 2.8 slice_convert_fusion
  189.7 1.8 copy.95
  191.5 1.1 copy.90
  192.6 1.1 copy.89
  194.1 0.9 copy-done.19
  195.1 1.3 convolution_convert_fusion.1
  196.7 2.4 fusion.1
  199.2 0.7 multiply_reduce_fusion.2
  199.9 0.7 multiply_convert_fusion.4.refs_11_
  200.6 0.8 copy-done.13
  201.5 5.6 %add_convert_fusion = (bf16[1024,1024]{1,0:T(8,128)(2,1)}, bf16[1024,1024]{1,0:T(8,128)(2,1)S(1)}) fusion(bf16[1024,1024]{1,0:T(8,128)(2,1)S(1)} %multiply_convert_fusion.4.refs_11_, bf16[1024,1024]{1,0:T(8,128)(2,1)S(1)} %bitcast.174), kind=kOutput, calls=%fused_computation.4 | convolution fusion | flops 2167406592 | bytes 8388608 | tf_op jit(solution)/shard_map/dot_general | solution.py:25
  207.0 2.5 fusion.21
  210.7 9.0 %convolution_convert_fusion.refs_9_ = bf16[1024,3072]{1,0:T(8,128)(2,1)} fusion(bf16[1024,1024]{1,0:T(8,128)(2,1)S(1)} %multiply_convert_fusion.2.refs_10_, bf16[1024,3072]{1,0:T(8,128)(2,1)S(1)} %bitcast.168), kind=kOutput, calls=%fused_computation.1 | convolution fusion | flops 6445596672 | bytes 14680064 | tf_op jit(solution)/shard_map/dot_general | solution.py:25
  219.7 15.8 %attention.1 = bf16[2,512,1024]{2,1,0:T(8,128)(2,1)S(1)} custom-call(bf16[2,512,3072]{2,1,0:T(8,128)(2,1)} %bitcast.153), custom_call_target="tpu_custom_call" | custom-call | tf_op jit(solution)/shard_map/attention/pallas_call | solution.py:882
  235.5 2.4 fusion.22
  238.5 1.4 copy-done.1
  240.2 0.8 pad.35.refs_22_
  241.6 2.9 multiply_convert_fusion.1.refs_5_
  244.6 5.6 %add_convert_fusion.1 = (bf16[1024,1024]{1,0:T(8,128)(2,1)}, bf16[1024,1024]{1,0:T(8,128)(2,1)S(1)}) fusion(bf16[1024,1024]{1,0:T(8,128)(2,1)S(1)} %multiply_convert_fusion.1.refs_5_, bf16[1024,1024]{1,0:T(8,128)(2,1)S(1)} %bitcast.178), kind=kOutput, calls=%fused_computation.5 | convolution fusion | flops 2167406592 | bytes 8388608 | tf_op jit(solution)/shard_map/dot_general | solution.py:25
  250.2 1.4 copy-done.17
  251.6 3.7 add_convert_fusion.2
  255.3 1.6 copy.77
  256.8 249.7 %closing.1 = (bf16[2,2,32,1024]{3,2,1,0:T(8,128)(2,1)}, bf16[2,2,32,1024]{3,2,1,0:T(8,128)(2,1)}, bf16[2,2,32,1024]{3,2,1,0:T(8,128)(2,1)}, bf16[2,2,32,768]{3,2...) custom-call(s32[32]{0:T(128)} %reshape.376.refs_0_, ...), custom_call_target="tpu_custom_call" | custom-call | tf_op jit(solution)/shard_map/closing/pallas_call | solution.py:1526
  506.6 1.3 fusion.16
  507.9 1.5 slice_convert_fusion.1
  509.5 1.1 copy.105
  510.6 2.1 multiply_convert_fusion.5
  512.7 2.3 fusion.7
  515.0 1.6 multiply_reduce_fusion.3
  517.3 0.8 fusion.20
  519.5 8.1 %copy.86 = f32[1,2,4096,261]{2,1,3,0:T(2,128)} copy(f32[1,2,4096,261]{2,3,1,0:T(8,128)S(1)} %slice_bitcast_fusion) | data formatting | bytes 17104896
  527.7 1.9 convolution_multiply_fusion
  529.6 1.1 bitcast_convert_fusion.4
  530.7 1.1 bitcast_convert_fusion.2
  531.8 1.1 bitcast_convert_fusion
  532.9 0.8 fusion.4
  533.7 1.3 maximum_convert_fusion
  535.0 1.3 copy.107
  (131 shorter events, 12.0 us)
Async XLA Ops:
  6.5 4.3 copy-start.12
  172.4 10.2 %copy-start.3 = (bf16[4,2,2,2,16,1024]{5,4,3,2,1,0:T(8,128)(2,1)S(1)}, bf16[4,2,2,2,16,1024]{5,4,3,2,1,0:T(8,128)(2,1)}, u32[]{:S(2)}) copy-start(bf16[4,2,2,2,16,1024]{5,4,3,2,1,0:T(8,128)(2,1)} %get-tuple-element.56) | copy-start | bytes 3145732
  172.4 82.8 %all-to-all-start = ((bf16[2,8,64,1024]{3,2,0,1:T(8,128)(2,1)}), bf16[2,8,64,1024]{3,2,0,1:T(8,128)(2,1)S(1)}, u32[]{:S(2)}, u32[]{:S(2)}) async-start(bf16[2,8,64,1024]{3,2,0,1:T(8,128)(2,1)} %bitcast.147), calls=%async_computation | async-start | bytes 4194304 | tf_op jit(solution)/shard_map/all_to_all | solution.py:1678
  184.1 2.8 copy-start.32
  193.8 1.1 copy-start.19
  193.8 1.3 copy-start.20
  195.1 1.6 copy-start.5
  196.4 2.7 copy-start.6
  199.9 1.6 copy-start.13
  199.9 10.8 %slice-start.3 = ((s8[6291456]{0:T(1024)(128)(4,1)}), s8[4194304]{0:T(1024)(128)(4,1)S(1)}, s32[]{:S(2)}) async-start(s8[6291456]{0:T(1024)(128)(4,1)} %bitcast.166), calls=%async_computation.4 | async-start | bytes 8388608
  200.6 6.4 %copy-start.7 = (bf16[1024,1024]{1,0:T(8,128)(2,1)}, bf16[1024,1024]{1,0:T(8,128)(2,1)S(1)}, u32[]{:S(2)}) copy-start(bf16[1024,1024]{1,0:T(8,128)(2,1)S(1)} %multiply_convert_fusion.4.refs_11_) | copy-start | bytes 6291460
  201.5 5.6 %copy-start.10 = (bf16[4,2,2,2,32,1024]{5,4,3,2,1,0:T(8,128)(2,1)S(1)}, bf16[4,2,2,2,32,1024]{5,4,3,2,1,0:T(8,128)(2,1)}, u32[]{:S(2)}) copy-start(bf16[4,2,2,2,32,1024]{5,4,3,2,1,0:T(8,128)(2,1)} %get-tuple-element.62) | copy-start | bytes 6291460
  201.5 9.2 %slice-start.4 = ((s8[6291456]{0:T(1024)(128)(4,1)}), s8[2097152]{0:T(1024)(128)(4,1)S(1)}, s32[]{:S(2)}) async-start(s8[6291456]{0:T(1024)(128)(4,1)} %bitcast.166), calls=%async_computation.5 | async-start | bytes 4194304
  207.0 2.5 copy-start.11
  210.7 9.0 %copy-start.8 = (bf16[1024,1024]{1,0:T(8,128)(2,1)}, bf16[1024,1024]{1,0:T(8,128)(2,1)S(1)}, u32[]{:S(2)}) copy-start(bf16[1024,1024]{1,0:T(8,128)(2,1)S(1)} %multiply_convert_fusion.2.refs_10_) | copy-start | bytes 6291460
  219.7 15.8 %copy-start.14 = (bf16[4,2,2,2,32,1024]{5,4,3,2,1,0:T(8,128)(2,1)S(1)}, bf16[4,2,2,2,32,1024]{5,4,3,2,1,0:T(8,128)(2,1)}, u32[]{:S(2)}) copy-start(bf16[4,2,2,2,32,1024]{5,4,3,2,1,0:T(8,128)(2,1)} %get-tuple-element.64) | copy-start | bytes 6291460
  235.5 2.4 copy-start
  238.0 2.0 copy-start.1
  241.6 2.9 copy-start.15
  244.6 5.6 %copy-start.9 = (bf16[1024,1024]{1,0:T(8,128)(2,1)}, bf16[1024,1024]{1,0:T(8,128)(2,1)S(1)}, u32[]{:S(2)}) copy-start(bf16[1024,1024]{1,0:T(8,128)(2,1)S(1)} %multiply_convert_fusion.1.refs_5_) | copy-start | bytes 6291460
  244.6 7.0 %copy-start.2 = (f32[1024,1024]{1,0:T(8,128)S(1)}, f32[1024,1024]{1,0:T(8,128)}, u32[]{:S(2)}) copy-start(f32[1024,1024]{1,0:T(8,128)} %copy-done.1) | copy-start | bytes 12582916
  244.6 7.0 %copy-start.16 = (bf16[4,2,2,2,32,1024]{5,4,3,2,1,0:T(8,128)(2,1)S(1)}, bf16[4,2,2,2,32,1024]{5,4,3,2,1,0:T(8,128)(2,1)}, u32[]{:S(2)}) copy-start(bf16[4,2,2,2,32,1024]{5,4,3,2,1,0:T(8,128)(2,1)} %get-tuple-element.66) | copy-start | bytes 6291460
  250.2 1.4 copy-start.17
  510.5 4.5 copy-start.34
  510.5 4.4 copy-start.35
  510.6 4.4 copy-start.36
  510.6 4.4 copy-start.37
  510.6 4.4 copy-start.4
  510.6 8.3 %slice-start = ((s8[8912896]{0:T(1024)(128)(4,1)}), s8[4194304]{0:T(1024)(128)(4,1)S(1)}, s32[]{:S(2)}) async-start(s8[8912896]{0:T(1024)(128)(4,1)} %bitcast.156), calls=%async_computation.1 | async-start | bytes 8388608
  515.0 2.3 copy-start.33
  515.0 3.9 slice-start.1
  515.0 3.9 slice-start.2
  519.5 10.0 %copy-start.25 = (bf16[2,2,32,1024]{3,2,1,0:T(8,128)(2,1)S(1)}, bf16[2,2,32,1024]{3,2,1,0:T(8,128)(2,1)}, u32[]{:S(2)}) copy-start(bf16[2,2,32,1024]{3,2,1,0:T(8,128)(2,1)} %get-tuple-element.79) | copy-start | bytes 786436
  519.5 10.0 %copy-start.26 = (bf16[2,2,32,1024]{3,2,1,0:T(8,128)(2,1)S(1)}, bf16[2,2,32,1024]{3,2,1,0:T(8,128)(2,1)}, u32[]{:S(2)}) copy-start(bf16[2,2,32,1024]{3,2,1,0:T(8,128)(2,1)} %get-tuple-element.78) | copy-start | bytes 786436
  527.6 3.1 copy-start.23
  527.6 3.1 copy-start.24
  527.6 4.2 copy-start.21
  527.6 4.2 copy-start.22
  529.5 3.4 copy-start.31
  530.7 3.1 copy-start.27
  530.7 3.1 copy-start.28
  530.7 3.1 copy-start.29
  530.7 3.1 copy-start.30
  531.8 3.2 copy-start.18

commit v4 on v3

--- a/solution.py
+++ b/solution.py
@@ -448,6 +448,8 @@
 MIB = 1024 * 1024
 PIECE = 256
 BLOCK = 1024
+STRIP = 256
+CHUNK = 64
 FROWS = 272
 DEN_ROW = 261
 TOP_ROW = 263
@@ -535,6 +537,15 @@
     tail = sum(values * factor for values, factor in zip(tails, factors, strict=True))
     den = sum(row * factor for (row, unused), factor in zip(read, factors, strict=True))
     return body, tail, den, top
+
+
+def gelu_and_slope(hidden):
+    const = (2 / jnp.pi) ** 0.5
+    square = hidden * hidden
+    bent = jnp.tanh(const * hidden * (1 + 0.044715 * square))
+    half = 0.5 * (1 + bent)
+    slope = half + 0.5 * hidden * (1 - bent * bent) * const * (1 + 3 * 0.044715 * square)
+    return hidden * half, slope
 
 
 class Gather:
@@ -611,26 +622,31 @@
 def opening_kernel(splits, scale, features, *refs):
     count = len(splits)
     same, last = refs[:2]
-    shards, pixels, pix_gain = refs[2 : count + 2], *refs[count + 2 : count + 4]
-    refs = refs[count + 4 :]
-    wholes, weights_out = refs[:count], refs[count]
-    normed_out, queries_out, query_out, tops, means, rows_out = refs[count + 1 : count + 7]
-    refs = refs[count + 7 :]
+    shards, pixels, cot, pix_gain = refs[2 : count + 2], *refs[count + 2 : count + 5]
+    refs = refs[count + 5 :]
+    wholes, weights_out, cot_rows = refs[:count], refs[count], refs[count + 1]
+    normed_c, active_c, slope_c, normed_s, packed, self_att = refs[count + 2 : count + 8]
+    normed_m, active_s, slope_s, att_low, final = refs[count + 8 : count + 13]
+    refs = refs[count + 13 :]
+    normed_out, queries_out, query_out, tops, means, rows_out, row_scales, gains = refs[:8]
+    refs = refs[8:]
     wide, weights, scores_ref, lat, wq, key, total, largest, pieces, sums = refs[:10]
     side_in, own, along_in = refs[10:13]
-    send, recv, local, own_send, own_recv, load = refs[13:]
+    value, stream, tile, first, second, third, fourth, left_w, right_w, heads = refs[13:23]
+    send, recv, local, own_send, own_recv, load, cot_send, cot_recv, fetch_sem, store_sem = refs[23:]
     x, c, z, y = place()
     micros, unused, slots = pixels.shape
     blocks = slots // BLOCK
     per_block = BLOCK // PIECE
     images = sums.shape[1]
     gather = Gather(shards, wholes, splits, send, recv, local)
-    along = [device(x, c, (z + i) % 4, y) for i in (1, 2, 3)]
-    greet([*along, gather.beside, gather.across, gather.core])
+    pix, dp = lax.axis_index("pix"), lax.axis_index("dp")
+    others = [{"dp": dp, "pix": (pix + i) % 8} for i in range(1, 8)]
+    greet([*others, gather.across, gather.core])
 
     fetch = pltpu.make_async_copy(pixels, wide, load.at[0])
     fetch.start()
-    for k in range(count):
+    for k in range(3):
         gather.start(k)
     gain = pix_gain[...]
 
@@ -648,9 +664,13 @@
     norm(0, 2)
     for k in range(3):
         gather.to_side(k)
+    for k in range(3, 6):
+        gather.start(k)
     norm(2, 4)
     for k in range(3):
         gather.to_over(k)
+    for k in range(6, count):
+        gather.start(k)
     norm(4, 6)
     for k in range(3):
         gather.to_core(k)
@@ -671,7 +691,8 @@
     lat_values = lat[...].reshape(sums.shape[3], -1).astype(jnp.float32)
     key_values = key[...].reshape(lat_values.shape[1], -1)
     columns = key_values[:, 256:384].astype(jnp.float32).T
-    normed = layer_norm(lat_values, columns[GAIN_LANE - 256 : GAIN_LANE - 255])
+    gains[...] = columns[GAIN_LANE - 256 : GAIN_LANE - 248]
+    normed = layer_norm(lat_values, gains[0:1])
     normed_out[...] = normed.astype(jnp.bfloat16)
     wq_values = wq[...].reshape(lat_values.shape[1], -1)
     queries_out[...] = matmul(normed_out[...], wq_values).astype(jnp.bfloat16)
@@ -786,48 +807,240 @@
     gather.to_core(6)
     pass_sums(1)
     gather.to_side(9)
+    gather.to_over(8)
     gather.to_side(10)
-    gather.to_over(8)
     gather.to_core(7)
+
+    loads, stores = {}, {}
+
+    def fetch(number, source, target):
+        loads[number] = pltpu.make_async_copy(source, target, fetch_sem.at[number])
+        loads[number].start()
+
+    def store(number, source, target):
+        stores[number] = pltpu.make_async_copy(source, target, store_sem.at[number])
+        stores[number].start()
+
+    def stored(*numbers):
+        for number in numbers:
+            stores.pop(number).wait()
+
+    def ready(*numbers):
+        for number in numbers:
+            loads.pop(number).wait()
+
+    gather.arrive(3)
+    fetch(0, wholes[3], value)
+    gather.arrive(4)
+    fetch(1, wholes[4], left_w)
+    gather.arrive(5)
+    fetch(2, wholes[5], right_w)
+    finish_sums(0)
     gather.to_over(9)
-    finish_sums(0)
+    finish_sums(1)
+    cots = [pltpu.make_async_copy(cot.at[:, pix], cot_rows.at[:, pix], local.at[count])]
+    for i, other in enumerate(others):
+        source, target = cot.at[:, (pix + i + 1) % 8], cot_rows.at[:, pix]
+        cots.append(remote(source, target, (cot_send, cot_recv), i, other))
+    for copy in cots:
+        copy.start()
+
+    latents, model = lat_values.shape
+    strip_count = stream.shape[0] // STRIP
+
+    def strips(one):
+        def step(i, carry):
+            one(i, pl.ds(pl.multiple_of(i * STRIP, STRIP), STRIP))
+            return carry
+
+        lax.fori_loop(0, strip_count, step, 0)
+
+    def chunks(one):
+        def step(j, carry):
+            one(pl.ds(pl.multiple_of(j * CHUNK, CHUNK), CHUNK))
+            return carry
+
+        lax.fori_loop(0, STRIP // CHUNK, step, 0)
+
+    def square(ref):
+        return ref[...].reshape(model, model)
+
+    def add_and_norm(left, weight, number, target, base=None, last_out=None):
+        def one(i, strip):
+            if base is None:
+                stream[strip, :] += matmul(left[strip, :], square(weight))
+            else:
+                stream[strip, :] = base(i) + matmul(left[strip, :], square(weight))
+
+            def chunk(part):
+                at = pl.ds(pl.multiple_of(i * STRIP, STRIP) + part.start, CHUNK)
+                values = stream[at, :]
+                centered = values - jnp.mean(values, 1, keepdims=True)
+                row_scale = lax.rsqrt(jnp.mean(centered * centered, 1, keepdims=True) + 1e-05)
+                row_scales[at, 3 - number : 4 - number] = row_scale
+                target[at, :] = (centered * row_scale * gains[number : number + 1]).astype(
+                    jnp.bfloat16
+                )
+
+            chunks(chunk)
+
+        strips(one)
+
+    def through_gelu(left, weight, active, slope):
+        def one(i, strip):
+            tile[...] = matmul(left[strip, :], square(weight))
+
+            def chunk(part):
+                at = pl.ds(pl.multiple_of(i * STRIP, STRIP) + part.start, CHUNK)
+                acted, sloped = gelu_and_slope(tile[part, :])
+                active[at, :] = acted.astype(jnp.bfloat16)
+                slope[at, :] = sloped.astype(jnp.bfloat16)
+
+            chunks(chunk)
+
+        strips(one)
+
+    ready(0)
+    for m in range(micros):
+        first[m * latents : (m + 1) * latents, :] = lax.dot_general(
+            means[m],
+            value[...].reshape(model, -1)[:, :FROWS],
+            (((0,), (1,)), ((), ())),
+            preferred_element_type=jnp.float32,
+        ).astype(jnp.bfloat16)
+    store(0, first, att_low)
     gather.to_over(10)
     gather.to_core(8)
-    finish_sums(1)
+    ready(1)
+
+    def lat_strip(i):
+        return lat[pl.ds((i % 2) * 2, 2)].reshape(STRIP, model).astype(jnp.float32)
+
+    add_and_norm(first, left_w, 1, second, lat_strip)
+    store(1, second, normed_c)
+    gather.arrive(6)
+    fetch(3, wholes[6], left_w)
+    ready(2)
+    through_gelu(second, right_w, third, fourth)
+    store(2, third, active_c)
+    store(3, fourth, slope_c)
     gather.to_core(9)
+    gather.arrive(7)
+    half = heads.shape[2]
+    fetch(4, wholes[7].at[:, :, :, :, :, :half], right_w.at[:, :, :, :, :, :half])
+    ready(3)
+    stored(0)
+    add_and_norm(third, left_w, 2, first)
+    store(4, first, normed_s)
+    fetch(5, wholes[7].at[:, :, :, :, :, half : 2 * half], left_w.at[:, :, :, :, :, :half])
     gather.to_core(10)
-    for k in range(3, count):
-        gather.arrive(k)
-    for copy in keeps:
+    stored(1)
+    width = half // 6
+    for pair in range(4):
+        block = heads.at[pair % 2]
+        weight = (right_w, left_w)[pair % 2]
+        ready(4 + pair)
+        if pair >= 2:
+            stored(3 + pair)
+
+        def project(i, strip, block=block, weight=weight):
+            product = matmul(first[strip, :], weight[:, :, :, :, :, :half].reshape(model, half))
+            block[strip, :] = product.astype(jnp.bfloat16)
+
+        strips(project)
+        store(5 + pair, block, packed.at[:, pair * half : (pair + 1) * half])
+        if pair < 2:
+            columns = pl.ds((pair + 2) * half, half)
+            fetch(
+                6 + pair,
+                wholes[7].at[:, :, :, :, :, columns],
+                weight.at[:, :, :, :, :, :half],
+            )
+
+        def unit(i, carry, pair=pair, block=block):
+            image, head = i // 2, i % 2
+            rows = pl.ds(pl.multiple_of(image * latents, latents), latents)
+
+            def columns(part):
+                start = pl.multiple_of(head * (3 * width) + part * width, width)
+                return pl.ds(start, width)
+
+            query, key_, value_ = (block[rows, columns(part)] for part in range(3))
+            scores = right_matmul(query, key_) * width ** (-0.5)
+            exps = jnp.exp(scores - jnp.max(scores, 1, keepdims=True))
+            den = jnp.sum(exps, 1, keepdims=True)
+            out = pl.ds(pl.multiple_of((pair * 2 + head) * width, width), width)
+            second[rows, out] = (matmul(exps.astype(jnp.bfloat16), value_) / den).astype(
+                jnp.bfloat16
+            )
+            return carry
+
+        lax.fori_loop(0, 4, unit, 0)
+    store(9, second, self_att)
+    gather.arrive(8)
+    fetch(8, wholes[8], right_w)
+    gather.arrive(9)
+    fetch(9, wholes[9], left_w)
+    ready(8)
+    stored(2)
+    add_and_norm(second, right_w, 3, third)
+    store(10, third, normed_m)
+    gather.arrive(10)
+    fetch(10, wholes[10], right_w)
+    ready(9)
+    stored(3, 4)
+    through_gelu(third, left_w, fourth, first)
+    store(11, fourth, active_s)
+    store(12, first, slope_s)
+    ready(10)
+    stored(9)
+
+    def finish_rows(i, strip):
+        second[strip, :] = (
+            stream[strip, :] + matmul(fourth[strip, :], square(right_w))
+        ).astype(jnp.bfloat16)
+
+    strips(finish_rows)
+    store(13, second, final)
+    stored(*list(stores))
+    for copy in (*keeps, *cots):
         copy.wait()
     gather.finish()
     for copy in (*sides.values(), *alongs.values()):
         copy.wait_send()
 
 
-def opening(same, last, shards, splits, pixels, gain, features, images, scale):
+def opening(same, last, shards, splits, pixels, cot, gain, features, scale):
     count = len(shards)
     bf16, f32 = jnp.bfloat16, jnp.float32
     micros, unused, slots = pixels.shape
     latents, width = 8 * shards[0].shape[0], shards[0].shape[1]
     views = [shard.reshape(2, 2, shard.shape[0] // 4, shard.shape[1]) for shard in shards]
     outs = [jax.ShapeDtypeStruct((4, 2, *view.shape), view.dtype) for view in views]
+    images = cot.shape[1]
     piece = (FROWS, latents)
+    total_rows = micros * latents
+    square, wide = (total_rows, width), (total_rows, 3 * width)
+    kept = [jax.ShapeDtypeStruct(wide if i == 4 else square, bf16) for i in range(11)]
     smem = pl.BlockSpec(memory_space=pltpu.SMEM)
     results = pl.pallas_call(
         functools.partial(opening_kernel, splits, scale, features),
         out_shape=[
             *outs,
             jax.ShapeDtypeStruct((micros, slots, latents), bf16),
+            jax.ShapeDtypeStruct(cot.shape, bf16),
+            *kept,
             jax.ShapeDtypeStruct((latents, width), bf16),
             jax.ShapeDtypeStruct((latents, width), bf16),
             jax.ShapeDtypeStruct(piece, bf16),
             jax.ShapeDtypeStruct((micros, slots // PIECE, 1, latents), f32),
             jax.ShapeDtypeStruct((micros, *piece), bf16),
             jax.ShapeDtypeStruct((micros, 2, latents), f32),
+            jax.ShapeDtypeStruct((total_rows, 128), f32),
+            jax.ShapeDtypeStruct((8, width), f32),
         ],
-        in_specs=[smem, smem] + [HBM] * (count + 1) + [VMEM],
-        out_specs=[HBM] * (count + 1) + [VMEM] * 6,
+        in_specs=[smem, smem] + [HBM] * (count + 2) + [VMEM],
+        out_specs=[HBM] * (count + 13) + [VMEM] * 8,
         scratch_shapes=[
             pltpu.VMEM(pixels.shape, bf16),
             pltpu.VMEM((micros, slots, latents), bf16),
@@ -842,75 +1055,31 @@
             pltpu.VMEM((micros, 4, *piece), bf16),
             pltpu.VMEM((micros, 4, *piece), bf16),
             pltpu.VMEM((micros, 3, *piece), bf16),
+            pltpu.VMEM(outs[3].shape, bf16),
+            pltpu.VMEM(square, f32),
+            pltpu.VMEM((STRIP, width), f32),
+            *[pltpu.VMEM(square, bf16) for _ in range(4)],
+            *[pltpu.VMEM(outs[4].shape, bf16) for _ in range(2)],
+            pltpu.VMEM((2, total_rows, 3 * width // 4), bf16),
             pltpu.SemaphoreType.DMA((count, 15)),
             pltpu.SemaphoreType.DMA((count, 15)),
-            pltpu.SemaphoreType.DMA((count,)),
+            pltpu.SemaphoreType.DMA((count + 1,)),
             pltpu.SemaphoreType.DMA((micros, 7)),
             pltpu.SemaphoreType.DMA((micros, 7)),
             pltpu.SemaphoreType.DMA((4 + micros,)),
+            pltpu.SemaphoreType.DMA((7,)),
+            pltpu.SemaphoreType.DMA((7,)),
+            pltpu.SemaphoreType.DMA((11,)),
+            pltpu.SemaphoreType.DMA((14,)),
         ],
-        compiler_params=remote_params(0, 60 * MIB),
+        compiler_params=remote_params(0, 64 * MIB - 1024),
         name="opening",
-    )(same, last, *views, pixels, gain)
+    )(same, last, *views, pixels, cot, gain)
     wholes = [
         whole.reshape(8 * shard.shape[0], shard.shape[1])
         for whole, shard in zip(results[:count], shards, strict=True)
     ]
     return wholes, results[count:]
-
-
-def softmax_parts(packed, scale):
-    width = packed.shape[1] // 3
-    query, key, value = packed[:, :width], packed[:, width : 2 * width], packed[:, 2 * width :]
-    scores = right_matmul(query, key) * scale
-    weights = jnp.exp(scores - jnp.max(scores, 1, keepdims=True))
-    return query, key, value, weights, jnp.sum(weights, 1, keepdims=True)
-
-
-def attention_kernel(scale, packed, out):
-    query, key, value, weights, den = softmax_parts(packed[0], scale)
-    out[0] = (matmul(weights.astype(jnp.bfloat16), value) / den).astype(jnp.bfloat16)
-
-
-def head_spec(rows, width):
-    return pl.BlockSpec((1, rows, width), lambda m, h: (m, 0, h))
-
-
-def attention(packed, scale):
-    micros, rows, columns = packed.shape
-    width = columns // HEADS
-    return pl.pallas_call(
-        functools.partial(attention_kernel, scale),
-        grid=(micros, HEADS),
-        in_specs=[head_spec(rows, width)],
-        out_specs=head_spec(rows, width // 3),
-        out_shape=jax.ShapeDtypeStruct((micros, rows, columns // 3), jnp.bfloat16),
-        compiler_params=pltpu.CompilerParams(vmem_limit_bytes=48 * MIB),
-        name="attention",
-    )(packed)
-
-
-def normed_rows(values, gain):
-    average = jnp.mean(values, -1, keepdims=True)
-    centered = values - average
-    scale = lax.rsqrt(jnp.mean(centered * centered, -1, keepdims=True) + 1e-05)
-    return (centered * scale * gain).astype(jnp.bfloat16), scale
-
-
-def feed(inputs, gain, w_in, w_out):
-    normed, scale = normed_rows(inputs, gain)
-    hidden = matmul(normed, w_in)
-    square = hidden * hidden
-    const = (2 / jnp.pi) ** 0.5
-    bent = jnp.tanh(const * hidden * (1 + 0.044715 * square))
-    half = 0.5 * (1 + bent)
-    active = (hidden * half).astype(jnp.bfloat16)
-    slope = half + 0.5 * hidden * (1 - bent * bent) * const * (1 + 3 * 0.044715 * square)
-    return inputs + matmul(active, w_out), (scale, normed, active, slope.astype(jnp.bfloat16))
-
-
-STRIP = 256
-CHUNK = 64
 
 
 class Reduce:
@@ -1140,7 +1309,7 @@
         strips(one)
 
     def through_norm(number, normed, product, fresh=False):
-        gain = gains[number : number + 1]
+        gain = gains[3 - number : 4 - number]
         inverse = 1.0 / gain
         width = gain.shape[1]
 
@@ -1670,31 +1839,23 @@
         pixels[0].transpose(0, 2, 1), ((0, 0), (0, FROWS - features), (0, 0))
     )
     wholes, results = opening(
-        same, last, shards, splits, pixel_rows, gain_pix, features, images, cross_scale
+        same,
+        last,
+        shards,
+        splits,
+        pixel_rows,
+        cotangent[0],
+        gain_pix,
+        features,
+        cross_scale,
     )
     lat_full, wq, key_t, value_t, wo, w1c, w2c, wqkv, wos, w1s, w2s = wholes
-    pix_weights, normed_lat, queries, query_t, pix_tops, means, rows = results
-    cot_slots, means = lax.optimization_barrier((cotangent[0], means))
-    cot_rows = lax.all_to_all(cot_slots, "pix", split_axis=1, concat_axis=1, tiled=True)
-    g_lat, g_cross, g_self, g_mlp = (key_t[:, GAIN_LANE + i].astype(f32) for i in range(4))
-    value_t = value_t[:, :FROWS]
+    pix_weights, cot_rows, *kept = results[:13]
+    normed_c, active_c, slope_c, normed_self, packed, self_att = kept[:6]
+    normed_m, active_s, slope_s, att_low, final = kept[6:]
+    normed_lat, queries, query_t, pix_tops, means, rows, row_scales, gain_rows = results[13:]
+    final = final.reshape(micros, 8, row_count, width)
     lat_f = lat_full.astype(f32)
-    den, top = rows[:, 0], rows[:, 1]
-
-    att_low = jnp.einsum("mfr,df->mrd", means, value_t, preferred_element_type=f32)
-    att_low = att_low.astype(bf16).reshape(micros * latents, width)
-    start_rows = jnp.broadcast_to(lat_f[None], (micros, latents, width)).reshape(-1, width)
-    after_cross = start_rows + matmul(att_low, wo)
-    after_mlp, cross_kept = feed(after_cross, g_cross, w1c, w2c)
-    normed_self, self_scale_rows = normed_rows(after_mlp, g_self)
-    packed = matmul(normed_self, wqkv).astype(bf16)
-    self_att = attention(packed.reshape(micros, latents, 3 * width), head_size ** (-0.5))
-    self_att = self_att.reshape(-1, width)
-    after_self = after_mlp + matmul(self_att, wos)
-    final, final_kept = feed(after_self, g_mlp, w1s, w2s)
-    final = final.astype(bf16).reshape(micros, 8, row_count, width)
-    row_scales = jnp.concatenate([final_kept[0], self_scale_rows, cross_kept[0]], 1)
-    row_scales = jnp.pad(row_scales, ((0, 0), (0, 125)))
 
     shards, latent_out, pixel_grad, query_sums = closing(
         segs,
@@ -1702,18 +1863,18 @@
         pix_weights,
         cot_rows.reshape(-1, width),
         final,
-        final_kept[1:],
+        (normed_m, active_s, slope_s),
         self_att,
         packed,
         normed_self,
-        cross_kept[1:],
+        (normed_c, active_c, slope_c),
         att_low,
         (w2s, w1s, wos, wqkv, w2c, w1c, wo),
         row_scales,
-        jnp.stack([g_mlp, g_self, g_cross]),
+        gain_rows,
         means,
         rows,
-        value_t.T,
+        value_t[:, :FROWS].T,
         query_t,
         pix_tops,
         gain_pix,
@@ -1732,7 +1893,7 @@
     d_wq = left_matmul(columns, grad_queries)
     query_columns = lax.dynamic_slice_in_dim(queries, position * (width // 8), width // 8, 1)
     d_wk = matmul(query_sums[:features], query_columns) * cross_scale
-    grad_norm_lat, d_glat = norm_back(lat_f, g_lat, right_matmul(grad_queries, wq))
+    grad_norm_lat, d_glat = norm_back(lat_f, gain_rows[0], right_matmul(grad_queries, wq))
     d_glat = lax.dynamic_slice_in_dim(d_glat, position * (width // 8), width // 8, 0)
     grad_norm_rows = lax.dynamic_slice_in_dim(grad_norm_lat, position * row_count, row_count, 0)
     return (

time: 542 us -> 510 us (0.941)
  matrix products: 40.3 us -> 8.4 us
  Pallas kernels: 421 us -> 452 us
  local copies, waits for them, and re-layouts: 41.4 us -> 30.9 us
  other arithmetic: 23 us -> 13 us
  starting transfers between devices: 9.62 us -> 0 us
    pallas_call x1, Pallas kernels: 155 us -> 215 us  [opening(): pl.pallas_call(functools.partial(opening_kernel, splits, scale, features)...]
    dot_general x8 -> x1, matrix products: 33 us -> 1.8 us  [matmul(): return jnp.dot(left, right, preferred_element_type=jnp.float32)]
    pallas_call x1 -> x0, Pallas kernels: 15.8 us -> none  [attention(): pl.pallas_call(functools.partial(attention_kernel, scale), grid=(micros,...]
    pallas_call x1, Pallas kernels: 250 us -> 237 us  [closing(): pl.pallas_call(functools.partial(closing_kernel, scale, images, features)...]
    unnamed x99 -> x48, local copies, waits for them, and re-layouts: 28.5 us -> 17.2 us
    all_to_all x1 -> x0, starting transfers between devices: 9.62 us -> none  [image_body(): lax.all_to_all(cot_slots, 'pix', split_axis=1, concat_axis=1, tiled=True)]
    convert_element_type x8 -> x0, other arithmetic: 7.3 us -> none  [the longest x3 4.21 us: normed_rows(): return ((centered * scale * gain).astype(jnp.bfloat16), scale)]
  transfers between devices with their start and end apart: 1 -> 0, of which waited for: 0 -> 0; matrix products, arithmetic and copies ran while one was open for 10% -> 0% of each run, Pallas kernels for 3% -> 0%
where the time goes in v4:
time: 510 us; the launch traced here: 506 us
  Pallas kernels  452 us (89%)
  local copies, waits for them, and re-layouts  30.9 us (6%)
  other arithmetic  13 us (3%)
  matrix products  8.4 us (2%)
    pallas_call x1, Pallas kernels, closing(): pl.pallas_call(functools.partial(closing_kernel, scale, images, features)...  237 us
    pallas_call x1, Pallas kernels, opening(): pl.pallas_call(functools.partial(opening_kernel, splits, scale, features)...  215 us
    unnamed x48, local copies, waits for them, and re-layouts  17.2 us

profile of v4, /device:TPU:0, one launch (start us, length us, event | category | flops | bytes accessed | tf_op | source)
XLA Modules:
  0.0 505.6 jit_solution(9395028076794456149)
XLA Ops:
  0.7 0.7 multiply_bitcast_fusion
  1.4 0.2 reduce_window_sum.11
  1.5 0.1 convert_reduce_fusion.1
  1.6 0.1 slice_compare_fusion
  1.7 0.1 pad_convert_fusion
  1.8 0.6 reshape.267.refs_0_
  2.4 0.1 select_reduce_fusion
  2.5 0.6 reshape.235.refs_1_
  3.1 5.2 %copy.67 = bf16[1,2,4096,261]{2,3,1,0:T(8,128)(2,1)S(1)} copy(bf16[1,2,4096,261]{2,1,3,0:T(2,128)(2,1)} %param.20) | data formatting | bytes 8552448 | tf_op args[1]
  8.3 0.0 copy-start.14
  8.3 0.0 copy-start.8
  8.3 0.0 copy-start.16
  8.4 0.0 copy-start.17
  8.4 2.6 pad.25.refs_13_.refs_1_
  11.0 0.8 reshape.281.refs_15_.refs_29_
  11.8 0.8 copy.51
  12.6 0.1 copy.59
  12.7 0.7 pad.29.clone
  13.3 214.7 %opening.1 = (bf16[4,2,2,2,16,1024]{5,4,3,2,1,0:T(8,128)(2,1)}, bf16[4,2,2,2,32,1024]{5,4,3,2,1,0:T(8,128)(2,1)}, bf16[4,2,2,2,32,384]{5,4,3,2,1,0:T(8,128)(2,1)...) custom-call(s32[32]{0:T(128)} %reshape.267.refs_0_, ...), custom_call_target="tpu_custom_call" | custom-call | tf_op jit(solution)/shard_map/opening/pallas_call | solution.py:1026
  228.1 2.2 copy.58
  230.3 1.3 reshape.232.refs_0_
  231.5 237.5 %closing.1 = (bf16[2,2,32,1024]{3,2,1,0:T(8,128)(2,1)}, bf16[2,2,32,1024]{3,2,1,0:T(8,128)(2,1)}, bf16[2,2,32,1024]{3,2,1,0:T(8,128)(2,1)}, bf16[2,2,32,768]{3,2...) custom-call(s32[32]{0:T(128)} %reshape.232.refs_0_, ...), custom_call_target="tpu_custom_call" | custom-call | tf_op jit(solution)/shard_map/closing/pallas_call | solution.py:1695
  469.0 2.2 bitcast_convert_fusion
  471.2 2.6 maximum_convert_fusion
  473.8 1.1 bitcast_convert_fusion.2
  474.9 1.1 bitcast_convert_fusion.4
  476.0 0.1 copy.69
  476.1 0.1 slice.55
  476.2 0.1 pad.43
  476.4 1.8 convolution_multiply_fusion
  478.2 0.8 multiply_convert_fusion
  479.0 2.0 fusion.4
  481.0 0.2 convert_reduce_fusion
  481.2 0.4 multiply_reduce_fusion.2
  481.7 0.1 add.55
  481.8 0.1 div.22
  481.9 0.8 slice.44
  482.6 3.8 multiply_reduce_fusion
  486.5 1.5 fusion.16
  488.0 0.1 dynamic-slice.2
  488.1 0.8 fusion.1
  488.9 1.3 dynamic_slice.13
  490.1 4.0 slice_bitcast_fusion
  494.2 8.1 %copy.57 = f32[1,2,4096,261]{2,1,3,0:T(2,128)} copy(f32[1,2,4096,261]{2,3,1,0:T(8,128)S(1)} %slice_bitcast_fusion) | data formatting | bytes 17104896
  502.3 0.6 fusion.10
  502.9 0.7 slice_convert_fusion
  503.5 0.5 fusion.13
  504.1 1.3 copy.71
  (46 shorter events, 0.2 us)
Async XLA Ops:
  1.6 6.7 %copy-start.11 = (s32[2,16]{1,0:T(2,128)}, s32[2,16]{1,0:T(2,128)S(1)}, u32[]{:S(2)}) copy-start(s32[2,16]{1,0:T(2,128)S(1)} %convert_reduce_fusion.1) | copy-start | bytes 388
  8.3 2.7 copy-start.14
  8.3 3.4 copy-start.8
  8.3 3.4 copy-start.15
  8.3 3.4 copy-start.16
  8.4 3.4 copy-start.17
  8.4 3.4 copy-start.18
  8.4 4.2 copy-start.9
  469.0 4.8 copy-start.5
  469.0 4.8 copy-start.6
  471.2 3.7 copy-start.3
  471.2 3.7 copy-start.4
  473.8 2.2 copy-start.2
  474.9 3.3 copy-start.19
  478.2 2.8 copy-start
  481.8 4.7 copy-start.13
  481.9 4.6 copy-start.12
  486.5 1.6 copy-start.7
  494.1 8.7 %copy-start.10 = (bf16[2,2,80,128]{3,2,1,0:T(8,128)(2,1)S(1)}, bf16[2,2,80,128]{3,2,1,0:T(8,128)(2,1)}, u32[]{:S(2)}) copy-start(bf16[2,2,80,128]{3,2,1,0:T(8,128)(2,1)} %get-tuple-element.101) | copy-start | bytes 245764
  494.1 9.9 %copy-start.1 = (bf16[2,8,64,1024]{3,2,1,0:T(8,128)(2,1)S(1)}, bf16[2,8,64,1024]{3,2,1,0:T(8,128)(2,1)}, u32[]{:S(2)}) copy-start(bf16[2,8,64,1024]{3,2,1,0:T(8,128)(2,1)} %get-tuple-element.92) | copy-start | bytes 6291460

commit v5 on v4

--- a/solution.py
+++ b/solution.py
@@ -838,13 +838,6 @@
     finish_sums(0)
     gather.to_over(9)
     finish_sums(1)
-    cots = [pltpu.make_async_copy(cot.at[:, pix], cot_rows.at[:, pix], local.at[count])]
-    for i, other in enumerate(others):
-        source, target = cot.at[:, (pix + i + 1) % 8], cot_rows.at[:, pix]
-        cots.append(remote(source, target, (cot_send, cot_recv), i, other))
-    for copy in cots:
-        copy.start()
-
     latents, model = lat_values.shape
     strip_count = stream.shape[0] // STRIP
 
@@ -926,6 +919,13 @@
     store(3, fourth, slope_c)
     gather.to_core(9)
     gather.arrive(7)
+    cots = [pltpu.make_async_copy(cot.at[:, pix], cot_rows.at[:, pix], local.at[count])]
+    for i, other in enumerate(others):
+        source, target = cot.at[:, (pix + i + 1) % 8], cot_rows.at[:, pix]
+        cots.append(remote(source, target, (cot_send, cot_recv), i, other))
+    for copy in cots:
+        copy.start()
+
     half = heads.shape[2]
     fetch(4, wholes[7].at[:, :, :, :, :, :half], right_w.at[:, :, :, :, :, :half])
     ready(3)
@@ -1267,12 +1267,17 @@
         copy.start()
     gain_grads[...] = jnp.zeros_like(gain_grads)
 
-    def strips(one):
+    def strips(one, image=None):
         def step(i, carry):
             one(i, pl.ds(pl.multiple_of(i * STRIP, STRIP), STRIP))
             return carry
 
-        lax.fori_loop(0, grad.shape[0] // STRIP, step, 0)
+        count = grad.shape[0] // STRIP
+        if image is None:
+            lax.fori_loop(0, count, step, 0)
+        else:
+            per_image = count // means.shape[0]
+            lax.fori_loop(image * per_image, (image + 1) * per_image, step, 0)
 
     def chunks(one):
         def step(j, carry):
@@ -1294,7 +1299,7 @@
         strips(one)
         reduce.push(k, slot)
 
-    def through_slope(weight):
+    def through_slope(weight, image=None):
         def one(i, strip):
             tile[:STRIP] = right_matmul(low[strip, :], weight[...])
 
@@ -1306,9 +1311,9 @@
 
             chunks(chunk)
 
-        strips(one)
-
-    def through_norm(number, normed, product, fresh=False):
+        strips(one, image)
+
+    def through_norm(number, normed, product, fresh=False, image=None):
         gain = gains[3 - number : 4 - number]
         inverse = 1.0 / gain
         width = gain.shape[1]
@@ -1336,7 +1341,7 @@
 
             chunks(chunk)
 
-        strips(one)
+        strips(one, image)
 
     ready(0, 1)
     weight_grad(0, 0, first, low, 1024)
@@ -1352,7 +1357,7 @@
     ready(5)
     through_norm(0, second, lambda strip: right_matmul(back_low[strip, :], fourth[...]), True)
     fetch(9, normed_self, second)
-    half = head_grad.shape[1]
+    half = 3 * head_grad.shape[1] // 4
     fetch(10, wqkv.at[:, :half], fourth.at[:, :half])
     fetch(11, packed.at[:, :half], back_low.at[:, :half])
     reduce.run(("c2", 1))
@@ -1380,20 +1385,22 @@
             query, key, value = (block[rows, columns(part)] for part in range(3))
             out_rows_ = pl.ds(pl.multiple_of((pair * 2 + head) * width, width), width)
             upper = right_matmul(low[rows, :], third[out_rows_, :])
-            scores = right_matmul(query, key) * scale
-            weights = jnp.exp(scores - jnp.max(scores, 1, keepdims=True))
-            den = jnp.sum(weights, 1, keepdims=True)
-            grad_num = (upper / den).astype(jnp.bfloat16)
-            slopes = right_matmul(grad_num, value)
-            grad_den = -jnp.sum(weights * slopes, 1, keepdims=True) / den
-            grad_scores = (weights * (slopes + grad_den)).astype(jnp.bfloat16)
-            head_grad[rows, columns(0)] = (matmul(grad_scores, key) * scale).astype(jnp.bfloat16)
-            head_grad[rows, columns(1)] = (left_matmul(grad_scores, query) * scale).astype(
+            upper = upper.astype(jnp.bfloat16)
+            scores = right_matmul(key, query) * scale
+            weights = jnp.exp(scores - jnp.max(scores, 0, keepdims=True))
+            weights = weights * (1.0 / jnp.sum(weights, 0, keepdims=True))
+            slopes = right_matmul(value, upper)
+            lift = jnp.sum(weights * slopes, 0, keepdims=True)
+            grad_scores = (weights * (slopes - lift)).astype(jnp.bfloat16)
+            head_grad[rows, columns(0)] = (left_matmul(grad_scores, key) * scale).astype(
                 jnp.bfloat16
             )
-            head_grad[rows, columns(2)] = left_matmul(
-                weights.astype(jnp.bfloat16), grad_num
-            ).astype(jnp.bfloat16)
+            head_grad[rows, columns(1)] = (matmul(grad_scores, query) * scale).astype(
+                jnp.bfloat16
+            )
+            head_grad[rows, columns(2)] = matmul(weights.astype(jnp.bfloat16), upper).astype(
+                jnp.bfloat16
+            )
             return carry
 
         lax.fori_loop(0, 4, unit, 0)
@@ -1407,7 +1414,7 @@
         ready(10 if pair == 0 else 15 + pair)
 
         def spread(i, strip):
-            acc[strip, :] += right_matmul(head_grad[strip, :], fourth[:, :half])
+            acc[strip, :] += right_matmul(head_grad[strip, :half], fourth[:, :half])
 
         strips(spread)
         if pair < 3:
@@ -1425,31 +1432,24 @@
 
     ready(20)
     weight_grad(7, 1, first, low, 1024)
-    fetch(24, att_low, first)
+    fetch(25, wo, first)
     reduce.run(("x2", 4))
-    ready(21, 8)
-    through_slope(third)
-    fetch(25, wo, third)
-    reduce.run(("c1", 7), ("y", 4), ("z", 3), ("b", 2), ("x1", 5))
-    ready(23)
-    weight_grad(8, 0, second, back_low, 1024)
-    reduce.run(("c2", 7), ("x2", 5), ("c1", 8))
-    ready(22)
-    through_norm(2, second, lambda strip: right_matmul(back_low[strip, :], fourth[...]))
-    reduce.run(("c2", 8), ("y", 5), ("z", 4), ("b", 3), ("x1", 6))
-
-    ready(25)
-
-    def upper_rows(i, strip):
-        back_low[strip, :] = right_matmul(low[strip, :], third[...]).astype(jnp.bfloat16)
-
-    strips(upper_rows)
+    ready(21, 8, 22, 23, 25)
     micros = means.shape[0]
     grad_sems = (grad_send, grad_recv)
     along = {}
+
+    def upper_rows(i, strip):
+        head_grad[strip, :] = right_matmul(low[strip, :], first[...]).astype(jnp.bfloat16)
+
     for m in range(micros):
+        through_slope(third, m)
+        through_norm(
+            2, second, lambda strip: right_matmul(back_low[strip, :], fourth[...]), False, m
+        )
+        strips(upper_rows, m)
         rows = pl.ds(m * rows_of_image, rows_of_image)
-        sums = right_matmul(value_n[...], back_low[rows, :]) / rows_in[m, 0:1]
+        sums = right_matmul(value_n[...], head_grad[rows, :]) / rows_in[m, 0:1]
         grad_den = -jnp.sum(sums * means[m].astype(jnp.float32), 0, keepdims=True)
         packed_grads[m, : FROWS - 16] = sums[: FROWS - 16].astype(jnp.bfloat16)
         at = lax.broadcasted_iota(jnp.int32, (16, sums.shape[1]), 0) + (FROWS - 16)
@@ -1459,13 +1459,19 @@
         )
         mine, home = packed_grads.at[m], all_grads[m].at[z, y]
         for i in (1, 2, 3):
-            along[m, i] = remote(
-                mine, home, grad_sems, (m, i - 1), device(x, c, (z + i) % 4, y)
-            )
+            target = device(x, c, (z + i) % 4, y)
+            along[m, i] = remote(mine, home, grad_sems, (m, i - 1), target)
             along[m, i].start()
         along[m, 4] = remote(mine, home, grad_sems, (m, 3), reduce.beside)
         along[m, 4].start()
         fetch(26 + m, mine, home)
+        reduce.run(
+            *(
+                (("c1", 7), ("y", 4), ("z", 3), ("b", 2), ("x1", 5)),
+                (("c2", 7), ("x2", 5)),
+            )[m]
+        )
+    fetch(24, att_low, third)
 
     def pass_grads(m):
         for i in (1, 2, 3):
@@ -1479,11 +1485,14 @@
         for i in range(4, 8):
             along[m, i].wait_recv()
 
+    weight_grad(8, 0, second, back_low, 1024)
+    pass_grads(0)
+    reduce.run(("c1", 8), ("y", 5), ("z", 4), ("b", 3), ("x1", 6))
     ready(24)
-    weight_grad(9, 1, first, low, 1024)
-    reduce.run(("x2", 6), ("c1", 9))
+    weight_grad(9, 1, third, low, 1024)
+    reduce.run(("c2", 8), ("x2", 6), ("c1", 9))
     value_grad = sum(
-        matmul(means[m], back_low[m * rows_of_image : (m + 1) * rows_of_image, :])
+        matmul(means[m], head_grad[m * rows_of_image : (m + 1) * rows_of_image, :])
         for m in range(micros)
     )
     staged = staging[2]
@@ -1588,12 +1597,17 @@
                 block_store(m, b, part).start()
             reduce.run(*after[b])
 
-    pass_grads(0)
-    reduce.run(("x1", 7), ("x2", 7))
     pass_grads(1)
-    reduce.run(("y", 7), ("z", 6), ("b", 5))
     grads_ready(0)
-    pixels_back(0, ((), (("x1", 8), ("x2", 8)), (("z", 7), ("b", 6)), (("y", 8),)))
+    pixels_back(
+        0,
+        (
+            (("x1", 7), ("x2", 7)),
+            (("z", 6), ("b", 5), ("y", 7)),
+            (("x1", 8), ("x2", 8)),
+            (("z", 7), ("b", 6), ("y", 8)),
+        ),
+    )
     grads_ready(1)
     pixels_back(1, ((("x1", 9), ("x2", 9)), (("z", 8), ("b", 7)), (("x1", 10), ("x2", 10), ("x1", 11), ("x2", 11)), (("y", 9),)))
     for part in range(halves):
@@ -1717,7 +1731,7 @@
             scratch(square, f32),
             scratch(square, f32),
             *[scratch(square) for _ in range(7)],
-            scratch((total_rows, half)),
+            scratch(square),
             scratch((8, width), f32),
             scratch((micros, FROWS, latents)),
             *[scratch((4, 2, FROWS, latents)) for _ in range(micros)],

time: 510 us -> 502 us (0.984)
  Pallas kernels: 452 us -> 444 us
    pallas_call x1, Pallas kernels: 215 us -> 203 us  [opening(): pl.pallas_call(functools.partial(opening_kernel, splits, scale, features)...]
where the time goes in v5:
time: 502 us; the launch traced here: 497 us
  Pallas kernels  444 us (88%)
  local copies, waits for them, and re-layouts  30.9 us (6%)
  other arithmetic  13 us (3%)
  matrix products  8.4 us (2%)
    pallas_call x1, Pallas kernels, closing(): pl.pallas_call(functools.partial(closing_kernel, scale, images, features)...  241 us
    pallas_call x1, Pallas kernels, opening(): pl.pallas_call(functools.partial(opening_kernel, splits, scale, features)...  203 us
    unnamed x48, local copies, waits for them, and re-layouts  17.2 us

profile of v5, /device:TPU:0, one launch (start us, length us, event | category | flops | bytes accessed | tf_op | source)
XLA Modules:
  0.0 497.2 jit_solution(11625709621296005990)
XLA Ops:
  0.7 0.7 multiply_bitcast_fusion
  1.4 0.2 reduce_window_sum.11
  1.5 0.1 convert_reduce_fusion.1
  1.6 0.1 slice_compare_fusion
  1.7 0.1 pad_convert_fusion
  1.8 0.6 reshape.267.refs_0_
  2.4 0.1 select_reduce_fusion
  2.5 0.6 reshape.235.refs_1_
  3.1 5.2 %copy.67 = bf16[1,2,4096,261]{2,3,1,0:T(8,128)(2,1)S(1)} copy(bf16[1,2,4096,261]{2,1,3,0:T(2,128)(2,1)} %param.20) | data formatting | bytes 8552448 | tf_op args[1]
  8.3 0.0 copy-start.8
  8.3 0.0 copy-start.15
  8.4 0.0 copy-start.18
  8.4 0.0 copy-start.9
  8.4 2.6 pad.25.refs_13_.refs_1_
  11.0 0.8 reshape.281.refs_15_.refs_29_
  11.8 0.8 copy.51
  12.6 0.1 copy.59
  12.7 0.7 pad.29.clone
  13.3 202.7 %opening.1 = (bf16[4,2,2,2,16,1024]{5,4,3,2,1,0:T(8,128)(2,1)}, bf16[4,2,2,2,32,1024]{5,4,3,2,1,0:T(8,128)(2,1)}, bf16[4,2,2,2,32,384]{5,4,3,2,1,0:T(8,128)(2,1)...) custom-call(s32[32]{0:T(128)} %reshape.267.refs_0_, ...), custom_call_target="tpu_custom_call" | custom-call | tf_op jit(solution)/shard_map/opening/pallas_call | solution.py:1026
  216.1 2.2 copy.58
  218.3 1.3 reshape.232.refs_0_
  219.5 241.1 %closing.1 = (bf16[2,2,32,1024]{3,2,1,0:T(8,128)(2,1)}, bf16[2,2,32,1024]{3,2,1,0:T(8,128)(2,1)}, bf16[2,2,32,1024]{3,2,1,0:T(8,128)(2,1)}, bf16[2,2,32,768]{3,2...) custom-call(s32[32]{0:T(128)} %reshape.232.refs_0_, ...), custom_call_target="tpu_custom_call" | custom-call | tf_op jit(solution)/shard_map/closing/pallas_call | solution.py:1709
  460.7 2.2 bitcast_convert_fusion
  462.8 2.6 maximum_convert_fusion
  465.4 1.1 bitcast_convert_fusion.2
  466.5 1.1 bitcast_convert_fusion.4
  467.7 0.1 copy.69
  467.8 0.1 slice.55
  467.9 0.1 pad.43
  468.0 1.8 convolution_multiply_fusion
  469.8 0.8 multiply_convert_fusion
  470.6 2.0 fusion.4
  472.6 0.2 convert_reduce_fusion
  472.9 0.4 multiply_reduce_fusion.2
  473.3 0.1 add.55
  473.4 0.1 div.22
  473.5 0.8 slice.44
  474.3 3.8 multiply_reduce_fusion
  478.1 1.5 fusion.16
  479.6 0.1 dynamic-slice.2
  479.7 0.8 fusion.1
  480.5 1.3 dynamic_slice.13
  481.8 4.0 slice_bitcast_fusion
  485.8 8.1 %copy.57 = f32[1,2,4096,261]{2,1,3,0:T(2,128)} copy(f32[1,2,4096,261]{2,3,1,0:T(8,128)S(1)} %slice_bitcast_fusion) | data formatting | bytes 17104896
  493.9 0.6 fusion.10
  494.5 0.7 slice_convert_fusion
  495.2 0.5 fusion.13
  495.7 1.3 copy.71
  (46 shorter events, 0.2 us)
Async XLA Ops:
  1.6 6.7 %copy-start.11 = (s32[2,16]{1,0:T(2,128)}, s32[2,16]{1,0:T(2,128)S(1)}, u32[]{:S(2)}) copy-start(s32[2,16]{1,0:T(2,128)S(1)} %convert_reduce_fusion.1) | copy-start | bytes 388
  8.3 2.7 copy-start.14
  8.3 3.4 copy-start.8
  8.3 3.4 copy-start.15
  8.3 3.4 copy-start.16
  8.4 3.4 copy-start.17
  8.4 3.4 copy-start.18
  8.4 4.2 copy-start.9
  460.6 4.8 copy-start.5
  460.7 4.8 copy-start.6
  462.8 3.7 copy-start.3
  462.8 3.7 copy-start.4
  465.4 2.2 copy-start.2
  466.5 3.3 copy-start.19
  469.8 2.8 copy-start
  473.4 4.7 copy-start.13
  473.5 4.6 copy-start.12
  478.1 1.6 copy-start.7
  485.8 8.7 %copy-start.10 = (bf16[2,2,80,128]{3,2,1,0:T(8,128)(2,1)S(1)}, bf16[2,2,80,128]{3,2,1,0:T(8,128)(2,1)}, u32[]{:S(2)}) copy-start(bf16[2,2,80,128]{3,2,1,0:T(8,128)(2,1)} %get-tuple-element.101) | copy-start | bytes 245764
  485.8 9.9 %copy-start.1 = (bf16[2,8,64,1024]{3,2,1,0:T(8,128)(2,1)S(1)}, bf16[2,8,64,1024]{3,2,1,0:T(8,128)(2,1)}, u32[]{:S(2)}) copy-start(bf16[2,8,64,1024]{3,2,1,0:T(8,128)(2,1)} %get-tuple-element.92) | copy-start | bytes 6291460

commit v6 on v5

--- a/solution.py
+++ b/solution.py
@@ -729,7 +729,7 @@
                 tops[m, piece] = top
                 added = matmul(wide[m, :, rows], low)
                 before = jnp.where(
-                    same[m * blocks * per_block + piece] > 0, largest[...], -big_value
+                    same[m, piece] > 0, largest[...], -big_value
                 )
                 now = jnp.maximum(before, top)
                 largest[...] = now
@@ -746,7 +746,7 @@
 
         lax.fori_loop(0, blocks, one, 0)
         for image in range(images):
-            index = last[m * images + image]
+            index = last[m, image]
             present = index >= 0
             piece = pieces[jnp.maximum(index, 0)].astype(jnp.float32)
             sums[m, image, : FROWS - 16] = jnp.where(present, piece[: FROWS - 16], 0.0).astype(
@@ -1564,7 +1564,7 @@
             def piece(k, carry, b=b, weights=weights):
                 rows = pl.ds(pl.multiple_of(k * PIECE, PIECE), PIECE)
                 number = b * pieces + k
-                seg = segs[m * blocks * pieces + number]
+                seg = segs[m, number]
                 image = jnp.minimum(seg, images - 1)
                 upper = all_grads[m][image // 2, image % 2]
                 unused, top = read_rows(upper[FROWS - 16 :].astype(jnp.float32))
@@ -1843,11 +1843,10 @@
     ends = jnp.cumsum(lengths, 1)
     firsts = position * capacity + PIECE * jnp.arange(capacity // PIECE, dtype=jnp.int32)
     segs = jnp.sum((firsts[None, :, None] >= ends[:, None, :]).astype(jnp.int32), 2)
-    same = jnp.pad((segs[:, 1:] == segs[:, :-1]).astype(jnp.int32), ((0, 0), (1, 0))).reshape(-1)
+    same = jnp.pad((segs[:, 1:] == segs[:, :-1]).astype(jnp.int32), ((0, 0), (1, 0)))
     here = segs[:, :, None] == jnp.arange(images, dtype=jnp.int32)[None, None, :]
     order = jnp.arange(capacity // PIECE, dtype=jnp.int32)[None, :, None]
-    last = jnp.max(jnp.where(here, order, -1), 1).reshape(-1)
-    segs = segs.reshape(-1)
+    last = jnp.max(jnp.where(here, order, -1), 1)
     gain_pix = jnp.pad(pixel_gain.astype(f32), (0, FROWS - features))[:, None]
     pixel_rows = jnp.pad(
         pixels[0].transpose(0, 2, 1), ((0, 0), (0, FROWS - features), (0, 0))

time: 502 us -> 500 us (level)
  no operation moved by 1% of the time
where the time goes in v6:
time: 500 us; the launch traced here: 496 us
  Pallas kernels  444 us (89%)
  local copies, waits for them, and re-layouts  28.5 us (6%)
  other arithmetic  14.1 us (3%)
  matrix products  8.4 us (2%)
    pallas_call x1, Pallas kernels, closing(): pl.pallas_call(functools.partial(closing_kernel, scale, images, features)...  241 us
    pallas_call x1, Pallas kernels, opening(): pl.pallas_call(functools.partial(opening_kernel, splits, scale, features)...  203 us
    unnamed x48, local copies, waits for them, and re-layouts  17.2 us

profile of v6, /device:TPU:0, one launch (start us, length us, event | category | flops | bytes accessed | tf_op | source)
XLA Modules:
  0.0 496.0 jit_solution(6287067537791145663)
XLA Ops:
  0.7 0.7 multiply_bitcast_fusion
  1.4 0.2 reduce_window_sum.11
  1.5 0.1 convert_reduce_fusion.1.refs_0_
  1.6 0.1 slice_compare_fusion
  1.7 0.6 pad_convert_fusion.refs_0_
  2.3 0.7 select_reduce_fusion.refs_1_
  3.0 5.2 %copy.67 = bf16[1,2,4096,261]{2,3,1,0:T(8,128)(2,1)S(1)} copy(bf16[1,2,4096,261]{2,1,3,0:T(2,128)(2,1)} %param.20) | data formatting | bytes 8552448 | tf_op args[1]
  8.2 0.0 copy-start.14
  8.2 0.0 copy-start.8
  8.3 0.0 copy-start.15
  8.3 0.0 copy-start.16
  8.3 0.0 copy-start.17
  8.3 0.0 copy-start.18
  8.3 0.0 copy-start.9
  8.3 2.6 pad.26.refs_13_.refs_1_
  10.9 0.8 reshape.264.refs_15_.refs_29_
  11.7 0.8 copy.51
  12.5 0.1 copy.59
  12.6 0.7 pad.31.clone
  13.3 202.7 %opening.1 = (bf16[4,2,2,2,16,1024]{5,4,3,2,1,0:T(8,128)(2,1)}, bf16[4,2,2,2,32,1024]{5,4,3,2,1,0:T(8,128)(2,1)}, bf16[4,2,2,2,32,384]{5,4,3,2,1,0:T(8,128)(2,1)...) custom-call(s32[2,16]{1,0:T(2,128)} %pad_convert_fusion.refs_0_, ...), custom_call_target="tpu_custom_call" | custom-call | tf_op jit(solution)/shard_map/opening/pallas_call | solution.py:1026
  216.0 2.2 copy.58
  218.2 241.2 %closing.1 = (bf16[2,2,32,1024]{3,2,1,0:T(8,128)(2,1)}, bf16[2,2,32,1024]{3,2,1,0:T(8,128)(2,1)}, bf16[2,2,32,1024]{3,2,1,0:T(8,128)(2,1)}, bf16[2,2,32,768]{3,2...) custom-call(s32[2,16]{1,0:T(2,128)} %copy-done.11, ...), custom_call_target="tpu_custom_call" | custom-call | tf_op jit(solution)/shard_map/closing/pallas_call | solution.py:1709
  459.4 2.2 bitcast_convert_fusion
  461.6 2.6 maximum_convert_fusion
  464.2 1.1 bitcast_convert_fusion.2
  465.3 1.1 bitcast_convert_fusion.4
  466.4 0.1 copy.69
  466.5 0.1 slice.55
  466.6 0.1 pad.45
  466.8 1.8 convolution_multiply_fusion
  468.6 0.8 multiply_convert_fusion
  469.4 2.0 fusion.4
  471.4 0.2 convert_reduce_fusion
  471.6 0.4 multiply_reduce_fusion.2
  472.1 0.1 add.55
  472.2 0.1 div.22
  472.3 0.8 slice.44
  473.0 3.8 multiply_reduce_fusion
  476.9 1.5 fusion.16
  478.4 0.1 dynamic-slice.2
  478.4 0.8 fusion.1
  479.2 1.3 dynamic_slice.13
  480.5 4.0 slice_bitcast_fusion
  484.6 8.1 %copy.57 = f32[1,2,4096,261]{2,1,3,0:T(2,128)} copy(f32[1,2,4096,261]{2,3,1,0:T(8,128)S(1)} %slice_bitcast_fusion) | data formatting | bytes 17104896
  492.7 0.6 fusion.10
  493.3 0.7 slice_convert_fusion
  493.9 0.5 fusion.13
  494.5 1.3 copy.71
  (43 shorter events, 0.2 us)
Async XLA Ops:
  1.6 0.7 copy-start.11
  8.2 2.7 copy-start.14
  8.2 3.4 copy-start.8
  8.3 3.4 copy-start.15
  8.3 3.4 copy-start.16
  8.3 3.4 copy-start.17
  8.3 3.4 copy-start.18
  8.3 4.2 copy-start.9
  459.4 4.8 copy-start.5
  459.4 4.8 copy-start.6
  461.6 3.7 copy-start.3
  461.6 3.7 copy-start.4
  464.1 2.2 copy-start.2
  465.3 3.3 copy-start.19
  468.6 2.8 copy-start
  472.2 4.7 copy-start.13
  472.3 4.6 copy-start.12
  476.8 1.6 copy-start.7
  484.5 8.7 %copy-start.10 = (bf16[2,2,80,128]{3,2,1,0:T(8,128)(2,1)S(1)}, bf16[2,2,80,128]{3,2,1,0:T(8,128)(2,1)}, u32[]{:S(2)}) copy-start(bf16[2,2,80,128]{3,2,1,0:T(8,128)(2,1)} %get-tuple-element.101) | copy-start | bytes 245764
  484.5 9.9 %copy-start.1 = (bf16[2,8,64,1024]{3,2,1,0:T(8,128)(2,1)S(1)}, bf16[2,8,64,1024]{3,2,1,0:T(8,128)(2,1)}, u32[]{:S(2)}) copy-start(bf16[2,8,64,1024]{3,2,1,0:T(8,128)(2,1)} %get-tuple-element.92) | copy-start | bytes 6291460
